TPU v7x, 128 devices: a whole 4x4x4 slice. The times are simulated.
128 devices in a mesh: gx: 8 (over y, x_lo), gy: 16 (over x_hi, z, core).
Axes of the slice: x: 4 (x_hi: 2, x_lo: 2; x = x_hi * 2 + x_lo), y: 4, z: 4, core: 2. Of those that a mesh axis runs over, the one named last changes fastest.
Arguments:
- pressure: float32 [5120, 128, 128], P(('gx', 'gy')), may hold values from -6 to 6
- couplings: bfloat16 [5120, 12, 128, 128], P(('gx', 'gy')), may hold values from -0.15625 to 0.15625
- nbr_dir: int32 [5120, 12], P(('gx', 'gy')), may hold values from 0 to 4, as said below
- nbr_idx: int32 [5120, 12], P(('gx', 'gy')), may hold values from 0 to 39, as said below
- export_ids: int32 [2048], P(('gx', 'gy')), may hold values from 0 to 39, as said below
- bnd_blk: int32 [8, 16, 8, 2], P('gx', 'gy'), may hold values from -1 to 39, as said below
- area: float32 [8, 16, 8, 2, 128], P('gx', 'gy'), may hold values from 0.1 to 1
- bnd_mat: int32 [8, 16, 8, 2], P('gx', 'gy'), may hold values from 0 to 15
- states: float32 [8, 16, 8, 2, 2, 128, 128], P('gx', 'gy'), may hold values from -4 to 4
- mat_pole: float32 [16, 2], replicated, may hold values from 0.2 to 0.95
- mat_res: float32 [16, 2], replicated, may hold values from 0.2 to 1
- mat_y0: float32 [16], replicated, may hold values from 0.1 to 1
Outputs:
- pressure_out: float32 [5120, 128, 128], P(('gx', 'gy'))
- states_out: float32 [8, 16, 8, 2, 2, 128, 128], P('gx', 'gy')
Inputs may be any that keep to these rules, and one draw needn't show every extreme that they name: Slot 0 of every block is the block itself with nbr_dir 0; slots may point outside the grid. `nbr_idx`: below 16 where nbr_dir is not 0. `export_ids`: the 16 entries of one device are distinct local blocks. `bnd_blk`: -1 marks an empty slot; several slots may name one block; some device fills all its slots.
All inputs are finite; a program needn't handle non-finite values.
Results may differ from a plain program's by a relative error of at most 0.028.
Values may be sent and summed in bfloat16 or wider, within the bound.
No kernel may reach another device: no remote copies, remote signals or barrier semaphores. Data moves between devices by JAX's collectives and lax.ppermute only.
A program may use at most 128 MiB of HBM per device.

v0:
```python
import jax
import jax.numpy as jnp
from jax import lax
from jax.sharding import PartitionSpec as P

STEPS = 3


leap_scale = 0.5
wall_scale = 0.5


def from_behind(value, axis, steps):
    count = lax.axis_size(axis)
    first, last = (max(0, -steps), min(count, count - steps))
    return lax.ppermute(value, axis, [(source, source + steps) for source in range(first, last)])


def filter_update(wall_press, held_states, filter_coef, held_area):
    orders = held_states.shape[-3]
    pole_rate = filter_coef[..., :orders][..., None, None]
    residue_rate = filter_coef[..., orders : 2 * orders][..., None, None]
    direct_admit = filter_coef[..., 2 * orders][..., None, None]
    wall_value = wall_press.astype(jnp.float32)
    updated = pole_rate * held_states + residue_rate * wall_value[..., None, :, :]
    wall_flux = direct_admit * wall_value + jnp.sum(updated, axis=-3)
    return (updated, (held_area[..., None, :] * wall_flux).astype(jnp.bfloat16))


def per_device(
    pressure,
    couplings,
    nbr_dir,
    nbr_idx,
    export_ids,
    bnd_blk,
    area,
    bnd_mat,
    states,
    mat_pole,
    mat_res,
    mat_y0,
):
    blocks = pressure.shape[0]
    exports = export_ids.shape[0]
    material_count = mat_y0.shape[0]
    material_ids = jnp.arange(material_count, dtype=jnp.int32)
    onehot_mat = (bnd_mat[..., None] == material_ids).astype(jnp.float32)
    coef_table = jnp.concatenate([mat_pole, mat_res, mat_y0[:, None]], axis=1)
    filter_coef = jnp.einsum(
        "xyocm,mk->xyock", onehot_mat, coef_table, precision=lax.Precision.HIGHEST
    )
    slot_blk = bnd_blk[0, 0]
    slot_live = slot_blk >= 0
    slot_safe = jnp.where(slot_live, slot_blk, 0)
    scatter_table = (
        slot_blk.reshape(-1)[None, :] == jnp.arange(blocks, dtype=jnp.int32)[:, None]
    ).astype(jnp.bfloat16)
    pool_index = jnp.where(nbr_dir == 0, nbr_idx, blocks + (nbr_dir - 1) * exports + nbr_idx)
    previous = pressure
    current = pressure
    held_states = states
    for iteration in range(STEPS):
        rounded = current.astype(jnp.bfloat16)
        outgoing = rounded[export_ids]
        from_west = from_behind(outgoing, "gx", 1)
        from_east = from_behind(outgoing, "gx", -1)
        from_south = from_behind(outgoing, "gy", 1)
        from_north = from_behind(outgoing, "gy", -1)
        wall_press = jnp.where(
            slot_live[..., None, None], rounded[slot_safe], jnp.zeros((), jnp.bfloat16)
        )[None, None]
        arrived = lax.all_to_all(wall_press, "gx", split_axis=2, concat_axis=2, tiled=True)
        held_states, answer = filter_update(arrived, held_states, filter_coef, area)
        returned = lax.all_to_all(answer, "gx", split_axis=2, concat_axis=2, tiled=True)
        source_pool = jnp.concatenate(
            [rounded, from_west, from_east, from_south, from_north], axis=0
        )
        gathered = source_pool[pool_index]
        interior = jnp.einsum(
            "bksc,bkcd->bsd", gathered, couplings, preferred_element_type=jnp.float32
        )
        boundary = jnp.einsum(
            "be,esc->bsc",
            scatter_table,
            returned.reshape((-1,) + rounded.shape[1:]),
            preferred_element_type=jnp.float32,
        )
        following = 2.0 * current - previous - leap_scale * interior - wall_scale * boundary
        previous = current
        current = following
    return (current, held_states)


def solution(mesh):
    return jax.shard_map(
        per_device,
        mesh=mesh,
        in_specs=(
            P(("gx", "gy"), None, None),
            P(("gx", "gy"), None, None, None),
            P(("gx", "gy"), None),
            P(("gx", "gy"), None),
            P(("gx", "gy")),
            P("gx", "gy", None, None),
            P("gx", "gy", None, None, None),
            P("gx", "gy", None, None),
            P("gx", "gy", None, None, None, None, None),
            P(),
            P(),
            P(),
        ),
        out_specs=(P(("gx", "gy"), None, None), P("gx", "gy", None, None, None, None, None)),
        check_vma=False,
    )
```

profile of v0, /device:TPU:105, one launch (start us, length us, event | category | flops | bytes accessed | tf_op | source)
XLA Modules:
  0.0 267.1 jit_solution(5527587465127314252)
XLA Ops:
  1.3 0.7 compare_select_fusion.1
  2.1 3.5 %constant_dynamic-update-slice_fusion.4 = (bf16[104,128,128]{2,1,0:T(8,128)(2,1)S(1)}, bf16[40,128,128]{2,1,0:T(8,128)(2,1)}) fusion(f32[40,128,128]{2,1,0:T(8,128)} %param.12), kind=kLoop, calls=%fused_computation.49 | loop fusion | flops 655359 | bytes 5242880
  5.6 2.8 %gather_fusion = bf16[16,128,128]{2,1,0:T(8,128)(2,1)} fusion(bf16[40,128,128]{2,1,0:T(8,128)(2,1)} %get-tuple-element.9, s32[1024]{0:T(1024)S(1)} %get-tuple-element.15), kind=kCustom, calls=%fused_computation | custom fusion | bytes 1048640 | tf_op jit(solution)/shard_map/gather | solution.py:65
  8.4 3.8 %collective-permute-start.2 = (bf16[16,128,128]{2,1,0:T(8,128)(2,1)}, bf16[16,128,128]{2,1,0:T(8,128)(2,1)}, u32[]{:S(2)}, u32[]{:S(2)}) collective-permute-start(bf16[16,128,128]{2,1,0:T(8,128)(2,1)} %gather_fusion), channel_id=1, source_target_pairs={{0,1},{1,2},{2,3},{3,4},{4,5},{5,6},{6,7},{7,8},{8,9},{9,10},{10,1... | collective-permute-start | bytes 1572872 | tf_op jit(solution)/shard_map/ppermute | solution.py:16
  12.3 2.1 collective-permute-start.1
  14.4 3.2 %collective-permute-start = (bf16[16,128,128]{2,1,0:T(8,128)(2,1)}, bf16[16,128,128]{2,1,0:T(8,128)(2,1)}, u32[]{:S(2)}, u32[]{:S(2)}) collective-permute-start(bf16[16,128,128]{2,1,0:T(8,128)(2,1)} %gather_fusion), channel_id=1, source_target_pairs={{0,16},{16,32},{32,48},{48,64},{64,80},{80,96},{96,112},{1,17},{17... | collective-permute-start | bytes 1572872 | tf_op jit(solution)/shard_map/ppermute | solution.py:16
  17.6 1.9 collective-permute-start.3
  19.6 2.7 %gather_fusion.2 = bf16[16,128,128]{2,1,0:T(8,128)(2,1)} fusion(bf16[40,128,128]{2,1,0:T(8,128)(2,1)} %get-tuple-element.9, s32[1024]{0:T(1024)S(1)} %get-tuple-element.14), kind=kCustom, calls=%fused_computation.2 | custom fusion | bytes 1048640 | tf_op jit(solution)/shard_map/gather | solution.py:71
  22.3 1.9 broadcast_select_fusion.2
  24.3 5.5 %all-to-all-start = ((bf16[1,1,8,2,128,128]{5,4,3,1,0,2:T(8,128)(2,1)}), bf16[1,1,8,2,128,128]{5,4,3,1,0,2:T(8,128)(2,1)}, u32[]{:S(2)}, u32[]{:S(2)}) async-start(bf16[1,1,8,2,128,128]{5,4,3,1,0,2:T(8,128)(2,1)} %broadcast_select_fusion.2), calls=%async_computation | async-start | bytes 1048576 | tf_op jit(solution)/shard_map/all_to_all | solution.py:73
  30.7 17.2 %all-to-all-done = bf16[1,1,8,2,128,128]{5,4,3,1,0,2:T(8,128)(2,1)} async-done(((bf16[1,1,8,2,128,128]{5,4,3,1,0,2:T(8,128)(2,1)}), bf16[1,1,8,2,128,128]{5,4,3,1,0,2:T(8,128)(2,1)}, u32[]{:S(2)}, u32[]{:S(2)}) %all-to-all-start) | async-done | bytes 524320 | tf_op jit(solution)/shard_map/all_to_all | solution.py:73
  47.9 1.1 convert_bitcast_fusion.2
  49.0 1.0 copy-done.3
  50.1 2.1 fusion.6
  52.1 2.1 fusion.10
  54.2 5.1 %all-to-all-start.1 = ((bf16[1,1,8,2,128,128]{5,4,3,1,0,2:T(8,128)(2,1)}), bf16[1,1,8,2,128,128]{5,4,3,1,0,2:T(8,128)(2,1)}, u32[]{:S(2)}, u32[]{:S(2)}) async-start(bf16[1,1,8,2,128,128]{5,4,3,1,0,2:T(8,128)(2,1)} %fusion.10), calls=%async_computation.1 | async-start | bytes 1048576 | tf_op jit(solution)/shard_map/all_to_all | solution.py:75
  59.3 1.1 constant_dynamic-update-slice_fusion.3
  60.5 1.1 constant_dynamic-update-slice_fusion.2
  61.6 1.1 constant_dynamic-update-slice_fusion.1
  62.8 1.1 constant_dynamic-update-slice_fusion
  63.9 13.6 %gather_fusion.1 = bf16[480,128,128]{2,1,0:T(8,128)(2,1)} fusion(bf16[104,128,128]{2,1,0:T(8,128)(2,1)S(1)} %constant_dynamic-update-slice_fusion, s32[1024]{0:T(1024)S(1)} %pad_clamp_fusion.1), kind=kCustom, calls=%fused_computation.1 | custom fusion | bytes 31459200 | tf_op jit(solution)/shard_map/gather | solution.py:79
  77.5 1.7 copy.56
  79.9 14.3 %constant_dynamic-update-slice_fusion.9 = (bf16[104,128,128]{2,1,0:T(8,128)(2,1)S(1)}, bf16[40,128,128]{2,1,0:T(8,128)(2,1)}, f32[40,128,128]{2,1,0:T(8,128)}) fusion(f32[40,128,128]{2,0,1:T(8,128)S(1)} %fusion.22, bf16[40,12,128,128]{3,2,1,0:T(8,128)(2,1)} %bitcast.84, bf16[40,12,128,128]{3,2,1,0:T(8,128)(2,1)} %param.13, f32[40,128,128]{2,1,0:T(8,128)S(1)} %copy-done.2), kind=kOutput, calls=%fused_computation.54 | convolution fusion | flops 2017853440 | bytes 41943040 | tf_op jit(solution)/shard_map/bksc,bkcd->bsd/dot_general | solution.py:80
  94.2 2.7 %gather_fusion.5 = bf16[16,128,128]{2,1,0:T(8,128)(2,1)} fusion(bf16[40,128,128]{2,1,0:T(8,128)(2,1)} %get-tuple-element.7, s32[1024]{0:T(1024)S(1)} %get-tuple-element.14), kind=kCustom, calls=%fused_computation.5 | custom fusion | bytes 1048640 | tf_op jit(solution)/shard_map/gather | solution.py:71
  96.9 1.9 broadcast_select_fusion.1
  98.9 5.2 %all-to-all-start.2 = ((bf16[1,1,8,2,128,128]{5,4,3,1,0,2:T(8,128)(2,1)}), bf16[1,1,8,2,128,128]{5,4,3,1,0,2:T(8,128)(2,1)}, u32[]{:S(2)}, u32[]{:S(2)}) async-start(bf16[1,1,8,2,128,128]{5,4,3,1,0,2:T(8,128)(2,1)} %broadcast_select_fusion.1), calls=%async_computation.2 | async-start | bytes 1048576 | tf_op jit(solution)/shard_map/all_to_all | solution.py:73
  104.0 2.7 %gather_fusion.3 = bf16[16,128,128]{2,1,0:T(8,128)(2,1)} fusion(bf16[40,128,128]{2,1,0:T(8,128)(2,1)} %get-tuple-element.7, s32[1024]{0:T(1024)S(1)} %get-tuple-element.15), kind=kCustom, calls=%fused_computation.3 | custom fusion | bytes 1048640 | tf_op jit(solution)/shard_map/gather | solution.py:65
  106.8 7.0 %collective-permute-start.6 = (bf16[16,128,128]{2,1,0:T(8,128)(2,1)}, bf16[16,128,128]{2,1,0:T(8,128)(2,1)}, u32[]{:S(2)}, u32[]{:S(2)}) collective-permute-start(bf16[16,128,128]{2,1,0:T(8,128)(2,1)} %gather_fusion.3), channel_id=1, source_target_pairs={{0,1},{1,2},{2,3},{3,4},{4,5},{5,6},{6,7},{7,8},{8,9},{9,10},{10,1... | collective-permute-start | bytes 1572872 | tf_op jit(solution)/shard_map/ppermute | solution.py:16
  113.7 2.5 collective-permute-start.5
  116.2 2.8 %collective-permute-start.4 = (bf16[16,128,128]{2,1,0:T(8,128)(2,1)}, bf16[16,128,128]{2,1,0:T(8,128)(2,1)}, u32[]{:S(2)}, u32[]{:S(2)}) collective-permute-start(bf16[16,128,128]{2,1,0:T(8,128)(2,1)} %gather_fusion.3), channel_id=1, source_target_pairs={{0,16},{16,32},{32,48},{48,64},{64,80},{80,96},{96,112},{1,17},{17... | collective-permute-start | bytes 1572872 | tf_op jit(solution)/shard_map/ppermute | solution.py:16
  119.0 1.9 collective-permute-start.7
  121.0 1.1 convert_bitcast_fusion.1
  122.1 3.1 %fusion.7 = f32[8,2,128,128]{3,2,1,0:T(8,128)S(1)} fusion(f32[1,1,8,2,2,128,128]{6,5,4,3,2,1,0:T(8,128)} %param.20, f32[8,2,128,128]{3,2,1,0:T(8,128)S(1)} %convert_bitcast_fusion.1, f32[8,2,128,128]{3,2,1,0:T(8,128)} %copy-done.3, f32[8,2,2]{2,1,0:T(2,128)S(1)} %copy.55, f32[8,2,2]{2,1,0:T(2,128)S(1)} %copy.53), kind=kLoop, calls=%fused_computation.26 | loop fusion | flops 3407872 | bytes 5243136 | tf_op jit(solution)/shard_map/reduce_sum | solution.py:26
  125.2 2.1 fusion.13
  127.3 5.4 %all-to-all-start.3 = ((bf16[1,1,8,2,128,128]{5,4,3,1,0,2:T(8,128)(2,1)}), bf16[1,1,8,2,128,128]{5,4,3,1,0,2:T(8,128)(2,1)}, u32[]{:S(2)}, u32[]{:S(2)}) async-start(bf16[1,1,8,2,128,128]{5,4,3,1,0,2:T(8,128)(2,1)} %fusion.13), calls=%async_computation.3 | async-start | bytes 1048576 | tf_op jit(solution)/shard_map/all_to_all | solution.py:75
  132.7 12.1 %collective-permute-done.4 = bf16[16,128,128]{2,1,0:T(8,128)(2,1)} collective-permute-done((bf16[16,128,128]{2,1,0:T(8,128)(2,1)}, bf16[16,128,128]{2,1,0:T(8,128)(2,1)}, u32[]{:S(2)}, u32[]{:S(2)}) %collective-permute-start.4) | collective-permute-done | bytes 524320 | tf_op jit(solution)/shard_map/ppermute | solution.py:16
  144.9 1.1 constant_dynamic-update-slice_fusion.8
  146.0 1.1 constant_dynamic-update-slice_fusion.7
  147.2 1.1 constant_dynamic-update-slice_fusion.6
  148.3 1.1 constant_dynamic-update-slice_fusion.5
  149.4 13.6 %gather_fusion.4 = bf16[480,128,128]{2,1,0:T(8,128)(2,1)} fusion(bf16[104,128,128]{2,1,0:T(8,128)(2,1)S(1)} %constant_dynamic-update-slice_fusion.5, s32[1024]{0:T(1024)S(1)} %pad_clamp_fusion.1), kind=kCustom, calls=%fused_computation.4 | custom fusion | bytes 31459200 | tf_op jit(solution)/shard_map/gather | solution.py:79
  163.1 1.7 copy.59
  164.8 2.1 fusion.20
  166.9 16.8 %constant_dynamic-update-slice_fusion.14 = (bf16[104,128,128]{2,1,0:T(8,128)(2,1)S(1)}, bf16[40,128,128]{2,1,0:T(8,128)(2,1)}, f32[40,128,128]{2,1,0:T(8,128)}) fusion(f32[40,128,128]{2,0,1:T(8,128)} %fusion.20, bf16[40,12,128,128]{3,2,1,0:T(8,128)(2,1)} %bitcast.83, bf16[40,12,128,128]{3,2,1,0:T(8,128)(2,1)} %param.13, f32[40,128,128]{2,1,0:T(8,128)} %param.12, ...), kind=kOutput, calls=%fused_computation.59 | convolution fusion | flops 2017853440 | bytes 44564480 | tf_op jit(solution)/shard_map/bksc,bkcd->bsd/dot_general | solution.py:80
  183.7 2.7 %gather_fusion.8 = bf16[16,128,128]{2,1,0:T(8,128)(2,1)} fusion(bf16[40,128,128]{2,1,0:T(8,128)(2,1)} %get-tuple-element.3, s32[1024]{0:T(1024)S(1)} %get-tuple-element.14), kind=kCustom, calls=%fused_computation.8 | custom fusion | bytes 1048640 | tf_op jit(solution)/shard_map/gather | solution.py:71
  186.4 1.9 broadcast_select_fusion
  188.4 5.5 %all-to-all-start.4 = ((bf16[1,1,8,2,128,128]{5,4,3,1,0,2:T(8,128)(2,1)}), bf16[1,1,8,2,128,128]{5,4,3,1,0,2:T(8,128)(2,1)}, u32[]{:S(2)}, u32[]{:S(2)}) async-start(bf16[1,1,8,2,128,128]{5,4,3,1,0,2:T(8,128)(2,1)} %broadcast_select_fusion), calls=%async_computation.4 | async-start | bytes 1048576 | tf_op jit(solution)/shard_map/all_to_all | solution.py:73
  193.9 2.7 %gather_fusion.6 = bf16[16,128,128]{2,1,0:T(8,128)(2,1)} fusion(bf16[40,128,128]{2,1,0:T(8,128)(2,1)} %get-tuple-element.3, s32[1024]{0:T(1024)S(1)} %get-tuple-element.15), kind=kCustom, calls=%fused_computation.6 | custom fusion | bytes 1048640 | tf_op jit(solution)/shard_map/gather | solution.py:65
  196.6 1.9 collective-permute-start.10
  198.5 3.1 %collective-permute-start.9 = (bf16[16,128,128]{2,1,0:T(8,128)(2,1)}, bf16[16,128,128]{2,1,0:T(8,128)(2,1)}, u32[]{:S(2)}, u32[]{:S(2)}) collective-permute-start(bf16[16,128,128]{2,1,0:T(8,128)(2,1)} %gather_fusion.6), channel_id=1, source_target_pairs={{16,0},{32,16},{48,32},{64,48},{80,64},{96,80},{112,96},{17,1},{33... | collective-permute-start | bytes 1572872 | tf_op jit(solution)/shard_map/ppermute | solution.py:16
  201.6 2.2 collective-permute-start.8
  203.8 3.0 %collective-permute-start.11 = (bf16[16,128,128]{2,1,0:T(8,128)(2,1)}, bf16[16,128,128]{2,1,0:T(8,128)(2,1)}, u32[]{:S(2)}, u32[]{:S(2)}) collective-permute-start(bf16[16,128,128]{2,1,0:T(8,128)(2,1)} %gather_fusion.6), channel_id=1, source_target_pairs={{1,0},{2,1},{3,2},{4,3},{5,4},{6,5},{7,6},{8,7},{9,8},{10,9},{11,1... | collective-permute-start | bytes 1572872 | tf_op jit(solution)/shard_map/ppermute | solution.py:16
  206.8 1.1 convert_bitcast_fusion
  207.9 4.6 %fusion.34 = (f32[8,2,128,128]{3,2,1,0:T(8,128)S(1)}, f32[1,1,8,2,2,128,128]{6,5,4,3,2,1,0:T(8,128)}) fusion(f32[8,2,128,128]{3,2,1,0:T(8,128)S(1)} %convert_bitcast_fusion, f32[8,2,128,128]{3,2,1,0:T(8,128)} %copy-done.4, f32[8,2,128,128]{3,2,1,0:T(8,128)} %copy-done.3, f32[8,2,2]{2,1,0:T(2,128)S(1)} %copy.55, f32[1,1,8,2,2,128,128]{6,5,4,3,2,1,0:T(8,128)} %param.20, ...), kind=kLoop, calls=%fused_computation.90 | loop fusion | flops 4980736 | bytes 8388864 | tf_op jit(solution)/shard_map/reduce_sum | solution.py:26
  212.5 2.1 fusion.16
  214.6 6.0 %all-to-all-start.5 = ((bf16[1,1,8,2,128,128]{5,4,3,1,0,2:T(8,128)(2,1)}), bf16[1,1,8,2,128,128]{5,4,3,1,0,2:T(8,128)(2,1)}, u32[]{:S(2)}, u32[]{:S(2)}) async-start(bf16[1,1,8,2,128,128]{5,4,3,1,0,2:T(8,128)(2,1)} %fusion.16), calls=%async_computation.5 | async-start | bytes 1048576 | tf_op jit(solution)/shard_map/all_to_all | solution.py:75
  220.6 11.4 %collective-permute-done.8 = bf16[16,128,128]{2,1,0:T(8,128)(2,1)} collective-permute-done((bf16[16,128,128]{2,1,0:T(8,128)(2,1)}, bf16[16,128,128]{2,1,0:T(8,128)(2,1)}, u32[]{:S(2)}, u32[]{:S(2)}) %collective-permute-start.8) | collective-permute-done | bytes 524320 | tf_op jit(solution)/shard_map/ppermute | solution.py:16
  232.0 1.1 constant_dynamic-update-slice_fusion.13
  233.2 1.1 constant_dynamic-update-slice_fusion.12
  234.3 1.1 constant_dynamic-update-slice_fusion.11
  235.4 1.1 constant_dynamic-update-slice_fusion.10
  236.6 13.6 %gather_fusion.7 = bf16[480,128,128]{2,1,0:T(8,128)(2,1)} fusion(bf16[104,128,128]{2,1,0:T(8,128)(2,1)S(1)} %constant_dynamic-update-slice_fusion.10, s32[1024]{0:T(1024)S(1)} %pad_clamp_fusion.1), kind=kCustom, calls=%fused_computation.7 | custom fusion | bytes 31459200 | tf_op jit(solution)/shard_map/gather | solution.py:79
  250.2 1.7 copy.62
  252.5 14.5 %fusion.3 = f32[40,128,128]{2,1,0:T(8,128)} fusion(f32[40,128,128]{2,0,1:T(8,128)S(1)} %fusion.18, f32[40,128,128]{2,1,0:T(8,128)S(1)} %copy-done.1, f32[40,128,128]{2,1,0:T(8,128)} %get-tuple-element.13, bf16[40,12,128,128]{3,2,1,0:T(8,128)(2,1)} %bitcast.85, bf16[40,12,128,128]{3,2,1,0:T(8,128)(2,1)} %param.13), kind=kOutput, calls=%fused_computation.14 | convolution fusion | flops 2017198080 | bytes 41943040 | tf_op jit(solution)/shard_map/bksc,bkcd->bsd/dot_general | solution.py:80
  (61 shorter events, 3.1 us)
Async XLA Ops:
  2.1 17.4 %copy-start.8 = (s32[1,1,8,2]{2,3,1,0:T(2,128)S(1)}, s32[1,1,8,2]{2,3,1,0:T(2,128)}, u32[]{:S(2)}) copy-start(s32[1,1,8,2]{2,3,1,0:T(2,128)} %param.17) | copy-start | bytes 196
  5.6 24.3 %copy-start.9 = (f32[16,2]{0,1:T(2,128)S(1)}, f32[16,2]{0,1:T(2,128)}, u32[]{:S(2)}) copy-start(f32[16,2]{0,1:T(2,128)} %param.22) | copy-start | bytes 388
  5.6 24.3 %copy-start.10 = (f32[16,2]{0,1:T(2,128)S(1)}, f32[16,2]{0,1:T(2,128)}, u32[]{:S(2)}) copy-start(f32[16,2]{0,1:T(2,128)} %param.21) | copy-start | bytes 388
  5.6 24.3 %copy-start.11 = (s32[1,1,8,2]{2,3,1,0:T(2,128)S(1)}, s32[1,1,8,2]{2,3,1,0:T(2,128)}, u32[]{:S(2)}) copy-start(s32[1,1,8,2]{2,3,1,0:T(2,128)} %param.19) | copy-start | bytes 196
  5.6 24.3 %copy-start.12 = (f32[16]{0:T(128)S(1)}, f32[16]{0:T(128)}, u32[]{:S(2)}) copy-start(f32[16]{0:T(128)} %param.23) | copy-start | bytes 196
  5.6 24.9 %copy-start.6 = (s32[40,12]{0,1:T(8,128)S(1)}, s32[40,12]{0,1:T(8,128)}, u32[]{:S(2)}) copy-start(s32[40,12]{0,1:T(8,128)} %param.15) | copy-start | bytes 5764
  5.6 24.9 %copy-start.7 = (s32[40,12]{0,1:T(8,128)S(1)}, s32[40,12]{0,1:T(8,128)}, u32[]{:S(2)}) copy-start(s32[40,12]{0,1:T(8,128)} %param.14) | copy-start | bytes 5764
  8.4 53.2 %collective-permute-start.2 = (bf16[16,128,128]{2,1,0:T(8,128)(2,1)}, bf16[16,128,128]{2,1,0:T(8,128)(2,1)}, u32[]{:S(2)}, u32[]{:S(2)}) collective-permute-start(bf16[16,128,128]{2,1,0:T(8,128)(2,1)} %gather_fusion), channel_id=1, source_target_pairs={{0,1},{1,2},{2,3},{3,4},{4,5},{5,6},{6,7},{7,8},{8,9},{9,10},{10,1... | collective-permute-start | bytes 1572872 | tf_op jit(solution)/shard_map/ppermute | solution.py:16
  12.3 48.2 %collective-permute-start.1 = (bf16[16,128,128]{2,1,0:T(8,128)(2,1)}, bf16[16,128,128]{2,1,0:T(8,128)(2,1)}, u32[]{:S(2)}, u32[]{:S(2)}) collective-permute-start(bf16[16,128,128]{2,1,0:T(8,128)(2,1)} %gather_fusion), channel_id=1, source_target_pairs={{16,0},{32,16},{48,32},{64,48},{80,64},{96,80},{112,96},{17,1},{33... | collective-permute-start | bytes 1572872 | tf_op jit(solution)/shard_map/ppermute | solution.py:16
  14.4 45.0 %collective-permute-start = (bf16[16,128,128]{2,1,0:T(8,128)(2,1)}, bf16[16,128,128]{2,1,0:T(8,128)(2,1)}, u32[]{:S(2)}, u32[]{:S(2)}) collective-permute-start(bf16[16,128,128]{2,1,0:T(8,128)(2,1)} %gather_fusion), channel_id=1, source_target_pairs={{0,16},{16,32},{32,48},{48,64},{64,80},{80,96},{96,112},{1,17},{17... | collective-permute-start | bytes 1572872 | tf_op jit(solution)/shard_map/ppermute | solution.py:16
  17.6 45.2 %collective-permute-start.3 = (bf16[16,128,128]{2,1,0:T(8,128)(2,1)}, bf16[16,128,128]{2,1,0:T(8,128)(2,1)}, u32[]{:S(2)}, u32[]{:S(2)}) collective-permute-start(bf16[16,128,128]{2,1,0:T(8,128)(2,1)} %gather_fusion), channel_id=1, source_target_pairs={{1,0},{2,1},{3,2},{4,3},{5,4},{6,5},{7,6},{8,7},{9,8},{10,9},{11,1... | collective-permute-start | bytes 1572872 | tf_op jit(solution)/shard_map/ppermute | solution.py:16
  24.3 23.6 %all-to-all-start = ((bf16[1,1,8,2,128,128]{5,4,3,1,0,2:T(8,128)(2,1)}), bf16[1,1,8,2,128,128]{5,4,3,1,0,2:T(8,128)(2,1)}, u32[]{:S(2)}, u32[]{:S(2)}) async-start(bf16[1,1,8,2,128,128]{5,4,3,1,0,2:T(8,128)(2,1)} %broadcast_select_fusion.2), calls=%async_computation | async-start | bytes 1048576 | tf_op jit(solution)/shard_map/all_to_all | solution.py:73
  30.7 21.4 %copy-start.5 = (f32[1,1,8,2,128]{4,3,2,1,0:T(2,128)S(1)}, f32[1,1,8,2,128]{4,3,2,1,0:T(2,128)}, u32[]{:S(2)}) copy-start(f32[1,1,8,2,128]{4,3,2,1,0:T(2,128)} %param.18) | copy-start | bytes 24580
  49.0 1.0 copy-start.3
  54.2 23.3 %all-to-all-start.1 = ((bf16[1,1,8,2,128,128]{5,4,3,1,0,2:T(8,128)(2,1)}), bf16[1,1,8,2,128,128]{5,4,3,1,0,2:T(8,128)(2,1)}, u32[]{:S(2)}, u32[]{:S(2)}) async-start(bf16[1,1,8,2,128,128]{5,4,3,1,0,2:T(8,128)(2,1)} %fusion.10), calls=%async_computation.1 | async-start | bytes 1048576 | tf_op jit(solution)/shard_map/all_to_all | solution.py:75
  77.5 2.4 copy-start.2
  98.9 22.1 %all-to-all-start.2 = ((bf16[1,1,8,2,128,128]{5,4,3,1,0,2:T(8,128)(2,1)}), bf16[1,1,8,2,128,128]{5,4,3,1,0,2:T(8,128)(2,1)}, u32[]{:S(2)}, u32[]{:S(2)}) async-start(bf16[1,1,8,2,128,128]{5,4,3,1,0,2:T(8,128)(2,1)} %broadcast_select_fusion.1), calls=%async_computation.2 | async-start | bytes 1048576 | tf_op jit(solution)/shard_map/all_to_all | solution.py:73
  106.8 40.4 %collective-permute-start.6 = (bf16[16,128,128]{2,1,0:T(8,128)(2,1)}, bf16[16,128,128]{2,1,0:T(8,128)(2,1)}, u32[]{:S(2)}, u32[]{:S(2)}) collective-permute-start(bf16[16,128,128]{2,1,0:T(8,128)(2,1)} %gather_fusion.3), channel_id=1, source_target_pairs={{0,1},{1,2},{2,3},{3,4},{4,5},{5,6},{6,7},{7,8},{8,9},{9,10},{10,1... | collective-permute-start | bytes 1572872 | tf_op jit(solution)/shard_map/ppermute | solution.py:16
  113.7 32.3 %collective-permute-start.5 = (bf16[16,128,128]{2,1,0:T(8,128)(2,1)}, bf16[16,128,128]{2,1,0:T(8,128)(2,1)}, u32[]{:S(2)}, u32[]{:S(2)}) collective-permute-start(bf16[16,128,128]{2,1,0:T(8,128)(2,1)} %gather_fusion.3), channel_id=1, source_target_pairs={{16,0},{32,16},{48,32},{64,48},{80,64},{96,80},{112,96},{17,1},{33... | collective-permute-start | bytes 1572872 | tf_op jit(solution)/shard_map/ppermute | solution.py:16
  116.2 28.7 %collective-permute-start.4 = (bf16[16,128,128]{2,1,0:T(8,128)(2,1)}, bf16[16,128,128]{2,1,0:T(8,128)(2,1)}, u32[]{:S(2)}, u32[]{:S(2)}) collective-permute-start(bf16[16,128,128]{2,1,0:T(8,128)(2,1)} %gather_fusion.3), channel_id=1, source_target_pairs={{0,16},{16,32},{32,48},{48,64},{64,80},{80,96},{96,112},{1,17},{17... | collective-permute-start | bytes 1572872 | tf_op jit(solution)/shard_map/ppermute | solution.py:16
  119.0 29.3 %collective-permute-start.7 = (bf16[16,128,128]{2,1,0:T(8,128)(2,1)}, bf16[16,128,128]{2,1,0:T(8,128)(2,1)}, u32[]{:S(2)}, u32[]{:S(2)}) collective-permute-start(bf16[16,128,128]{2,1,0:T(8,128)(2,1)} %gather_fusion.3), channel_id=1, source_target_pairs={{1,0},{2,1},{3,2},{4,3},{5,4},{6,5},{7,6},{8,7},{9,8},{10,9},{11,1... | collective-permute-start | bytes 1572872 | tf_op jit(solution)/shard_map/ppermute | solution.py:16
  122.1 3.1 %copy-start.4 = (f32[8,2,128,128]{3,2,1,0:T(8,128)}, f32[8,2,128,128]{3,2,1,0:T(8,128)S(1)}, u32[]{:S(2)}) copy-start(f32[8,2,128,128]{3,2,1,0:T(8,128)S(1)} %convert_bitcast_fusion.1) | copy-start | bytes 3145732
  127.3 35.8 %all-to-all-start.3 = ((bf16[1,1,8,2,128,128]{5,4,3,1,0,2:T(8,128)(2,1)}), bf16[1,1,8,2,128,128]{5,4,3,1,0,2:T(8,128)(2,1)}, u32[]{:S(2)}, u32[]{:S(2)}) async-start(bf16[1,1,8,2,128,128]{5,4,3,1,0,2:T(8,128)(2,1)} %fusion.13), calls=%async_computation.3 | async-start | bytes 1048576 | tf_op jit(solution)/shard_map/all_to_all | solution.py:75
  163.1 3.8 %copy-start = (f32[40,128,128]{2,1,0:T(8,128)S(1)}, f32[40,128,128]{2,1,0:T(8,128)}, u32[]{:S(2)}) copy-start(f32[40,128,128]{2,1,0:T(8,128)} %get-tuple-element.12) | copy-start | bytes 7864324
  188.4 18.4 %all-to-all-start.4 = ((bf16[1,1,8,2,128,128]{5,4,3,1,0,2:T(8,128)(2,1)}), bf16[1,1,8,2,128,128]{5,4,3,1,0,2:T(8,128)(2,1)}, u32[]{:S(2)}, u32[]{:S(2)}) async-start(bf16[1,1,8,2,128,128]{5,4,3,1,0,2:T(8,128)(2,1)} %broadcast_select_fusion), calls=%async_computation.4 | async-start | bytes 1048576 | tf_op jit(solution)/shard_map/all_to_all | solution.py:73
  196.6 37.7 %collective-permute-start.10 = (bf16[16,128,128]{2,1,0:T(8,128)(2,1)}, bf16[16,128,128]{2,1,0:T(8,128)(2,1)}, u32[]{:S(2)}, u32[]{:S(2)}) collective-permute-start(bf16[16,128,128]{2,1,0:T(8,128)(2,1)} %gather_fusion.6), channel_id=1, source_target_pairs={{0,1},{1,2},{2,3},{3,4},{4,5},{5,6},{6,7},{7,8},{8,9},{9,10},{10,1... | collective-permute-start | bytes 1572872 | tf_op jit(solution)/shard_map/ppermute | solution.py:16
  198.5 34.7 %collective-permute-start.9 = (bf16[16,128,128]{2,1,0:T(8,128)(2,1)}, bf16[16,128,128]{2,1,0:T(8,128)(2,1)}, u32[]{:S(2)}, u32[]{:S(2)}) collective-permute-start(bf16[16,128,128]{2,1,0:T(8,128)(2,1)} %gather_fusion.6), channel_id=1, source_target_pairs={{16,0},{32,16},{48,32},{64,48},{80,64},{96,80},{112,96},{17,1},{33... | collective-permute-start | bytes 1572872 | tf_op jit(solution)/shard_map/ppermute | solution.py:16
  201.6 30.4 %collective-permute-start.8 = (bf16[16,128,128]{2,1,0:T(8,128)(2,1)}, bf16[16,128,128]{2,1,0:T(8,128)(2,1)}, u32[]{:S(2)}, u32[]{:S(2)}) collective-permute-start(bf16[16,128,128]{2,1,0:T(8,128)(2,1)} %gather_fusion.6), channel_id=1, source_target_pairs={{0,16},{16,32},{32,48},{48,64},{64,80},{80,96},{96,112},{1,17},{17... | collective-permute-start | bytes 1572872 | tf_op jit(solution)/shard_map/ppermute | solution.py:16
  203.8 31.6 %collective-permute-start.11 = (bf16[16,128,128]{2,1,0:T(8,128)(2,1)}, bf16[16,128,128]{2,1,0:T(8,128)(2,1)}, u32[]{:S(2)}, u32[]{:S(2)}) collective-permute-start(bf16[16,128,128]{2,1,0:T(8,128)(2,1)} %gather_fusion.6), channel_id=1, source_target_pairs={{1,0},{2,1},{3,2},{4,3},{5,4},{6,5},{7,6},{8,7},{9,8},{10,9},{11,1... | collective-permute-start | bytes 1572872 | tf_op jit(solution)/shard_map/ppermute | solution.py:16
  214.6 35.6 %all-to-all-start.5 = ((bf16[1,1,8,2,128,128]{5,4,3,1,0,2:T(8,128)(2,1)}), bf16[1,1,8,2,128,128]{5,4,3,1,0,2:T(8,128)(2,1)}, u32[]{:S(2)}, u32[]{:S(2)}) async-start(bf16[1,1,8,2,128,128]{5,4,3,1,0,2:T(8,128)(2,1)} %fusion.16), calls=%async_computation.5 | async-start | bytes 1048576 | tf_op jit(solution)/shard_map/all_to_all | solution.py:75
  250.2 2.3 copy-start.1
where the time goes:
time: 269 us; the launch traced here: 267 us
  local copies, waits for them, and re-layouts  77.9 us (29%)
  starting transfers between devices  68.1 us (25%)
  matrix products  49.2 us (18%)
  waiting for transfers between devices  40.7 us (15%)
  other arithmetic  30 us (11%)
    dot_general x3, matrix products, per_device(): jnp.einsum('bksc,bkcd->bsd', gathered, couplings, preferred_element_type=...  45.7 us
    gather x3, local copies, waits for them, and re-layouts, per_device(): gathered = source_pool[pool_index]  40.9 us
    ppermute x12, starting transfers between devices, from_behind(): lax.ppermute(value, axis, [(source, source + steps) for source in range(f...  35.4 us
    ppermute x12, waiting for transfers between devices, from_behind(): lax.ppermute(value, axis, [(source, source + steps) for source in range(f...  23.6 us
    all_to_all x3, waiting for transfers between devices, per_device(): lax.all_to_all(wall_press, 'gx', split_axis=2, concat_axis=2, tiled=True)  17.2 us
    all_to_all x3, starting transfers between devices, per_device(): lax.all_to_all(answer, 'gx', split_axis=2, concat_axis=2, tiled=True)  16.6 us
    all_to_all x3, starting transfers between devices, per_device(): lax.all_to_all(wall_press, 'gx', split_axis=2, concat_axis=2, tiled=True)  16.1 us
    unnamed x36, local copies, waits for them, and re-layouts  11.3 us
  transfers between devices with their start and end apart: 18, of which 3 were waited for; matrix products, arithmetic and copies ran while one was open for 32% of the time, Pallas kernels for 0%

commit v1 on v0

v1 whole, which is shorter than its diff:
```python
import functools

import jax
import jax.numpy as jnp
from jax import lax
from jax.experimental import pallas as pl
from jax.experimental.pallas import tpu as pltpu
from jax.sharding import PartitionSpec as P

VMEM = pltpu.VMEM
SMEM = pltpu.SMEM
DMA = pltpu.SemaphoreType.DMA
F32 = jnp.float32
BF16 = jnp.bfloat16

COEF_NAMES = ("now", "last", "older", "pole_sum", "pole_product", "second_pole")
COEF_ROWS = 16


def spec(space):
    return pl.BlockSpec(memory_space=space)


def params(megabytes):
    return pltpu.CompilerParams(vmem_limit_bytes=megabytes * 1024 * 1024)


def cost(flops, moved):
    return pl.CostEstimate(flops=0, bytes_accessed=0, transcendentals=0)


TURNS = (0, 1, -1, 2)
BACK = (0, 2, 1, 3)


def other_x(value):
    count = lax.axis_size("gx")
    return lax.ppermute(value, "gx", [(i, i ^ 1) for i in range(count)])


def along_y(value, steps):
    count = lax.axis_size("gx")
    return lax.ppermute(value, "gx", [(i, (i + 2 * steps) % count) for i in range(count)])


def along_gy(value, first, skip=()):
    pairs = [(i, i + 1) for i in range(first, lax.axis_size("gy") - 1, 2) if i not in skip]
    return lax.ppermute(value, "gy", pairs + [(j, i) for i, j in pairs])


def around_of(exports):
    gx, gy = lax.axis_size("gx"), lax.axis_size("gy")
    seam = gy // 2 - 1
    across = other_x(exports)
    core = along_gy(exports, 0)
    beside = along_gy(exports, 1, (seam,))
    on = [(i, i - 2) for i in range(3, gx, 2)] + [(i, i + 2) for i in range(0, gx - 2, 2)]
    passed = lax.ppermute(across, "gx", on)
    over = [(i * gy + seam, (i ^ 1) * gy + seam + 1) for i in range(gx)]
    seamed = lax.ppermute(across, ("gx", "gy"), over + [(j, i) for i, j in over])
    return across, passed, core, beside, seamed


def position():
    gx = lax.axis_index("gx")
    return gx // 2, gx % 2


def gx_of(y, x, turn, cross):
    return 2 * ((y + turn) & 3) + (x ^ cross)


def over_gx(parts, after):
    cap = parts[0].shape[0] // 2
    arrived = [parts[0]] + [along_y(parts[t], TURNS[t]) for t in range(1, len(TURNS))]
    return (*arrived, other_x(turned(arrived, cap, after)))


def turn_kernel(cap, *refs):
    parts, (out, sems) = refs[: len(TURNS)], refs[-2:]
    copies = [
        pltpu.make_async_copy(part.at[pl.ds(cap, cap)], out.at[pl.ds(t * cap, cap)], sems.at[t])
        for t, part in enumerate(parts)
    ]
    for copy in copies:
        copy.start()
    for copy in copies:
        copy.wait()


def turned(parts, cap, after):
    shape = (len(parts) * cap,) + parts[0].shape[1:]
    return pl.pallas_call(
        functools.partial(turn_kernel, cap),
        out_shape=jax.ShapeDtypeStruct(shape, parts[0].dtype),
        in_specs=[spec(pl.ANY)] * (len(parts) + len(after)),
        out_specs=spec(pl.ANY),
        scratch_shapes=[DMA((len(parts),))],
        compiler_params=params(8),
        cost_estimate=cost(0, 1000000),
        name="turned",
    )(*parts, *after)


def arrivals(arrived, cap):
    y, x = position()
    for cross in range(2):
        for t, turn in enumerate(TURNS):
            device = gx_of(y, x, -turn, cross)
            for c in range(cap):
                ref = arrived[-1].at[t * cap + c] if cross else arrived[t].at[c]
                yield cross, t, c, device, ref


def export_kernel(ids, pressure, out, held, sems):
    count = out.shape[0]

    def copy(i):
        return pltpu.make_async_copy(pressure.at[ids[i]], held.at[i], sems.at[i])

    for i in range(count):
        copy(i).start()
    for i in range(count):
        copy(i).wait()
        out[i] = held[i].astype(BF16)


def exports_of(ids, pressure):
    count, shape = ids.shape[0], pressure.shape[1:]
    return pl.pallas_call(
        export_kernel,
        out_shape=jax.ShapeDtypeStruct((count,) + shape, BF16),
        in_specs=[spec(SMEM), spec(pltpu.HBM)],
        out_specs=spec(VMEM),
        scratch_shapes=[VMEM((count,) + shape, F32), DMA((count,))],
        compiler_params=params(56),
        cost_estimate=cost(0, count * 98304),
        name="exports",
    )(ids, pressure)


def prepare_kernel(ids, turn, offset, walls, pressure, tiles, after, order, index, wall_at, others, taken, place):
    del tiles, after
    blocks, exports = order.shape[0], ids.shape[0]

    @pl.loop(0, blocks)
    def _(b):
        taken[b] = 0

    for j in range(exports):
        taken[ids[j]] = 1
        place[ids[j]] = j
        order[j] = ids[j]

    def one(b, count):
        free = taken[b] == 0

        @pl.when(free)
        def _():
            place[b] = count
            order[count] = b
            others[count - exports] = pressure[b].astype(BF16)

        return count + jnp.where(free, 1, 0)

    lax.fori_loop(0, blocks, one, exports)
    own = jnp.zeros_like(offset[...])
    for b in range(blocks):
        own = jnp.where(offset[...] == b, place[b], own)
    x, odd = lax.axis_index("gx") % 2, lax.axis_index("gy") % 2
    toward = turn[...]
    part = jnp.where(toward == 1, 1 - x, jnp.where(toward == 2, x, jnp.where(toward == 3, 3 - odd, 2 + odd)))
    index[...] = jnp.where(toward == 0, own, blocks + exports * part + offset[...])
    cap, owners = walls.shape
    for o in range(owners):
        for c in range(cap):
            at = walls[c, o]
            wall_at[c, o] = jnp.where(at < 0, -1, place[jnp.maximum(at, 0)])


def prepare(ids, turn, offset, walls, pressure, tiles, after):
    blocks, rows, cells = pressure.shape
    exports = ids.shape[0]
    return pl.pallas_call(
        prepare_kernel,
        out_shape=(
            jax.ShapeDtypeStruct((blocks,), jnp.int32),
            jax.ShapeDtypeStruct(turn.shape, jnp.int32),
            jax.ShapeDtypeStruct(walls.shape, jnp.int32),
            jax.ShapeDtypeStruct((blocks - exports, rows, cells), BF16),
        ),
        in_specs=[spec(SMEM), spec(VMEM), spec(VMEM), spec(SMEM), spec(VMEM), spec(VMEM), spec(pl.ANY)],
        out_specs=(spec(SMEM), spec(VMEM), spec(SMEM), spec(VMEM)),
        scratch_shapes=[SMEM((blocks,), jnp.int32), SMEM((blocks,), jnp.int32)],
        compiler_params=params(8),
        cost_estimate=cost(0, 5000000),
        name="prepare",
    )(ids, turn, offset, walls, pressure, tiles, after)


def respond_kernel(mats, pole, res, direct, states, area, after, *outs):
    del after
    rows = states.shape[2]
    cap = mats.shape[0]
    y, x = position()
    for t, turn in enumerate(TURNS):
        for cross in range(2):
            for c in range(cap):
                device = gx_of(y, x, turn, cross)
                slot, to, out = device * cap + c, cross * cap + c, outs[t]
                m = mats[c, device]
                p1, p2 = pole[0, m], pole[1, m]
                r1, r2, y0 = res[0, m], res[1, m], direct[m]
                wall = area[slot]
                first, second = p1 * states[slot, 0], p2 * states[slot, 1]
                out[to, 0:rows, :] = (wall * (first + second)).astype(BF16)
                out[to, rows : 2 * rows, :] = (wall * (p1 * first + p2 * second)).astype(BF16)
                ones = jnp.ones_like(wall)
                coefs = (
                    wall * (y0 + (r1 + r2)),
                    wall * (r1 * p1 + r2 * p2),
                    wall * (r1 * (p1 * p1) + r2 * (p2 * p2)),
                    ones * (p1 + p2),
                    ones * (p1 * p2),
                    ones * p2,
                )
                high = [v.astype(BF16).astype(F32) for v in coefs]
                low = [v - h for v, h in zip(coefs, high)]
                pad = [jnp.zeros_like(wall)] * (COEF_ROWS - 2 * len(coefs))
                out[to, 2 * rows :, :] = jnp.concatenate(high + low + pad, axis=0).astype(BF16)


def responses(mats, pole, res, direct, states, area, after):
    _, _, rows, cells = states.shape
    cap = mats.shape[0]
    return pl.pallas_call(
        respond_kernel,
        out_shape=[jax.ShapeDtypeStruct((2 * cap, 2 * rows + COEF_ROWS, cells), BF16)] * len(TURNS),
        in_specs=[spec(SMEM)] * 4 + [spec(VMEM)] * 2 + [spec(pl.ANY)],
        out_specs=[spec(VMEM)] * len(TURNS),
        compiler_params=params(8),
        cost_estimate=cost(0, 3000000),
        name="responses",
    )(mats, pole, res, direct, states, area, after)


def coef_row(message, name):
    at = COEF_NAMES.index(name)
    rows = message[message.shape[0] - COEF_ROWS :, :].astype(F32)
    return rows[at : at + 1] + rows[at + len(COEF_NAMES) : at + len(COEF_NAMES) + 1]


def block_of(parts, at):
    exports, others = parts
    count = exports.shape[0]
    return jnp.where(at < count, exports[jnp.minimum(at, count - 1)], others[jnp.maximum(at - count, 0)])


def base_kernel(step, wall_at, order, pressure, *refs):
    message, refs = refs[: len(TURNS) + 1], refs[len(TURNS) + 1 :]
    pairs = [refs[2 * i : 2 * i + 2] for i in range(len(refs) // 2)]
    base = refs[-1]
    fields, rounded = pairs[: step - 1], pairs[step - 1 : 2 * step - 1]
    rows = base.shape[1]
    exports, others = rounded[0][0].shape[0], rounded[0][1].shape[0]

    def start(part, count, offset):
        @pl.loop(0, count)
        def _(i):
            if step == 1:
                base[i + offset] = pressure[order[i + offset]]
            elif step == 2:
                base[i + offset] = 2.0 * fields[0][part][i] - pressure[order[i + offset]]
            else:
                base[i + offset] = 2.0 * fields[0][part][i] - fields[1][part][i]

    start(0, exports, 0)
    start(1, others, exports)

    for _, _, c, device, slot in arrivals(message, wall_at.shape[0]):
        at = wall_at[c, device]

        @pl.when(at >= 0)
        def _():
            row = functools.partial(coef_row, slot)
            values = [block_of(r, at).astype(F32) for r in rounded]
            flux = row("now") * values[0]
            if step >= 2:
                flux = flux + row("last") * values[1]
            first = slot[0:rows, :].astype(F32)
            if step == 1:
                flux = flux + first
            else:
                second = slot[rows : 2 * rows, :].astype(F32)
                if step == 2:
                    flux = flux + second
                else:
                    flux = flux + row("older") * values[2]
                    flux = flux + (row("pole_sum") * second - row("pole_product") * first)
            base[at] = base[at] - 0.5 * flux


def base_of(step, wall_at, order, message, pressure, fields, rounded):
    arrays = list(message) + [a for pair in list(fields) + list(rounded) for a in pair]
    return pl.pallas_call(
        functools.partial(base_kernel, step),
        out_shape=jax.ShapeDtypeStruct(pressure.shape, F32),
        in_specs=[spec(SMEM)] * 2 + [spec(pl.ANY if step == 3 else VMEM)] + [spec(VMEM)] * len(arrays),
        out_specs=spec(VMEM),
        compiler_params=params(8),
        cost_estimate=cost(0, 9000000),
        name=f"base_{step}",
    )(wall_at, order, pressure, *arrays)


def wall_kernel(wall_at, after, *refs):
    del after
    message, refs = refs[: len(TURNS) + 1], refs[len(TURNS) + 1 :]
    rounded, outs = [refs[2 * i : 2 * i + 2] for i in range(3)], refs[6:]
    rows = rounded[0][0].shape[1]
    cap = wall_at.shape[0]

    for cross, t, c, device, slot in arrivals(message, cap):
        at = wall_at[c, device]
        out = outs[BACK[t]].at[cross * cap + c]

        @pl.when(at < 0)
        def _():
            out[...] = jnp.zeros_like(out[...])

        @pl.when(at >= 0)
        def _():
            r3, r2, r1 = [block_of(r, at).astype(F32) for r in rounded]
            pole = coef_row(slot, "second_pole")
            out[0:rows, :] = (r2 + coef_row(slot, "pole_sum") * r1).astype(BF16)
            out[rows:, :] = (r3 + pole * (r2 + pole * r1)).astype(BF16)


def walls_of(wall_at, message, rounded, after):
    rows, cells = rounded[0][0].shape[1:]
    cap = wall_at.shape[0]
    arrays = list(message) + [a for pair in rounded for a in pair]
    return pl.pallas_call(
        wall_kernel,
        out_shape=[jax.ShapeDtypeStruct((2 * cap, 2 * rows, cells), BF16)] * len(TURNS),
        in_specs=[spec(SMEM), spec(pl.ANY)] + [spec(VMEM)] * len(arrays),
        out_specs=[spec(VMEM)] * len(TURNS),
        compiler_params=params(8),
        cost_estimate=cost(0, 4000000),
        name="walls",
    )(wall_at, after, *arrays)


def states_kernel(mats, pole, res, states, *refs):
    walls, out = refs[:-1], refs[-1]
    rows = states.shape[2]
    cap = mats.shape[0]
    for _, _, c, device, slot in arrivals(walls, cap):
        m, e = mats[c, device], device * cap + c
        p1, p2 = pole[0, m], pole[1, m]
        second = slot[rows:, :].astype(F32)
        first = second + (p1 - p2) * slot[0:rows, :].astype(F32)
        out[e, 0] = (p1 * p1 * p1) * states[e, 0] + res[0, m] * first
        out[e, 1] = (p2 * p2 * p2) * states[e, 1] + res[1, m] * second


def states_after(mats, pole, res, states, walls):
    return pl.pallas_call(
        states_kernel,
        out_shape=jax.ShapeDtypeStruct(states.shape, F32),
        in_specs=[spec(SMEM)] * 3 + [spec(VMEM)] * (1 + len(walls)),
        out_specs=spec(VMEM),
        compiler_params=params(8),
        cost_estimate=cost(0, 5000000),
        name="states_after",
    )(mats, pole, res, states, *walls)


def interior(pool, index, order, tiles, i):
    block = order[i]
    neigh = index.shape[0]
    sources = jnp.concatenate([pool[index[k, block]] for k in range(neigh)], axis=1)
    return jnp.dot(sources, tiles[block], preferred_element_type=F32)


def fill_pool(parts, pool, sems):
    *parts, beside, seamed = parts
    copies, at = [], 0
    for i, part in enumerate(parts):
        copies.append(pltpu.make_async_copy(part, pool.at[pl.ds(at, part.shape[0])], sems.at[i]))
        at += part.shape[0]
    for copy in copies:
        copy.start()
    seam = lax.axis_size("gy") // 2
    place = lax.axis_index("gy")
    at_seam = (place == seam - 1) | (place == seam)
    target = pool.at[pl.ds(at, beside.shape[0])]

    @pl.when(at_seam)
    def _():
        pltpu.make_async_copy(seamed, target, sems.at[len(parts)]).start()

    @pl.when(jnp.logical_not(at_seam))
    def _():
        pltpu.make_async_copy(beside, target, sems.at[len(parts)]).start()

    for copy in copies:
        copy.wait()
    pltpu.make_async_copy(beside, target, sems.at[len(parts)]).wait()


def first_kernel(order, index, tiles, base, *refs):
    parts, (field, exports, pool, sems) = refs[:-4], refs[-4:]
    fill_pool(parts, pool, sems)

    @pl.loop(0, exports.shape[0], unroll=8)
    def _(i):
        value = base[i] - 0.5 * interior(pool, index, order, tiles, i)
        field[i] = value
        exports[i] = value.astype(BF16)


def first_blocks(order, index, tiles, base, pool, name):
    rows, cells = base.shape[1:]
    exports = pool[0].shape[0]
    return pl.pallas_call(
        first_kernel,
        out_shape=(
            jax.ShapeDtypeStruct((exports, rows, cells), F32),
            jax.ShapeDtypeStruct((exports, rows, cells), BF16),
            jax.ShapeDtypeStruct((sum(p.shape[0] for p in pool[:-1]), rows, cells), BF16),
        ),
        in_specs=[spec(SMEM)] * 2 + [spec(VMEM)] * 2 + [spec(pl.ANY)] * len(pool),
        out_specs=(spec(VMEM),) * 3,
        scratch_shapes=[DMA((len(pool) - 1,))],
        compiler_params=params(8),
        cost_estimate=cost(exports * 50331648, 10000000),
        name=name,
    )(order, index, tiles, base, *pool)


def other_kernel(order, index, tiles, base, pool, field, others):
    count = others.shape[0]
    exports = order.shape[0] - count

    @pl.loop(0, count, unroll=8)
    def _(i):
        value = base[i + exports] - 0.5 * interior(pool, index, order, tiles, i + exports)
        field[i] = value
        others[i] = value.astype(BF16)


def other_blocks(order, index, tiles, base, pool, count, name):
    rows, cells = base.shape[1:]
    return pl.pallas_call(
        other_kernel,
        out_shape=(
            jax.ShapeDtypeStruct((count, rows, cells), F32),
            jax.ShapeDtypeStruct((count, rows, cells), BF16),
        ),
        in_specs=[spec(SMEM)] * 2 + [spec(VMEM)] * 3,
        out_specs=(spec(VMEM),) * 2,
        compiler_params=params(8),
        cost_estimate=cost(count * 50331648, 15000000),
        name=name,
    )(order, index, tiles, base, pool)


def last_kernel(order, index, tiles, base, *refs):
    parts, (out, pool, fresh, pool_sems, out_sems) = refs[:-5], refs[-5:]
    fill_pool(parts, pool, pool_sems)
    count = out.shape[0]

    def copy(i):
        return pltpu.make_async_copy(fresh.at[i], out.at[order[i]], out_sems.at[i])

    @pl.loop(0, count, unroll=8)
    def _(i):
        fresh[i] = base[i] - 0.5 * interior(pool, index, order, tiles, i)
        copy(i).start()

    @pl.loop(0, count)
    def _(i):
        copy(i).wait()


def last_blocks(order, index, tiles, base, pool):
    blocks, rows, cells = base.shape
    return pl.pallas_call(
        last_kernel,
        out_shape=jax.ShapeDtypeStruct((blocks, rows, cells), F32),
        in_specs=[spec(SMEM)] * 2 + [spec(VMEM)] * 2 + [spec(pl.ANY)] * len(pool),
        out_specs=spec(pltpu.HBM),
        scratch_shapes=[
            VMEM((sum(p.shape[0] for p in pool[:-1]), rows, cells), BF16),
            VMEM((blocks, rows, cells), F32),
            DMA((len(pool) - 1,)),
            DMA((blocks,)),
        ],
        compiler_params=params(10),
        cost_estimate=cost(blocks * 50331648, 25000000),
        name="last",
    )(order, index, tiles, base, *pool)


def per_device(
    pressure, couplings, nbr_dir, nbr_idx, export_ids, bnd_blk, area, bnd_mat, states, mat_pole, mat_res, mat_y0
):
    blocks, rows, cells = pressure.shape
    neigh = couplings.shape[1]
    exports = export_ids.shape[0]
    owners, cap = bnd_blk.shape[2:]
    slots = owners * cap

    e1 = exports_of(export_ids, pressure)
    around = around_of(e1)

    tiles = couplings.reshape(blocks, neigh * cells, cells)
    mats = bnd_mat.reshape(owners, cap).T
    pole, res = mat_pole.T, mat_res.T
    held = states.reshape((slots,) + states.shape[4:])
    message = responses(mats, pole, res, mat_y0, held, area.reshape(slots, 1, cells), around[2])
    message = over_gx(message, (around[0], around[3]))
    order, index, wall_at, o1 = prepare(
        export_ids, nbr_dir.T, nbr_idx.T, bnd_blk.reshape(owners, cap).T, pressure, tiles, around[3]
    )

    base = base_of(1, wall_at, order, message, pressure, (), ((e1, o1),))
    p1_first, e2, pool = first_blocks(order, index, tiles, base, (e1, o1) + around, "exports_1")
    around = around_of(e2)
    p1_other, o2 = other_blocks(order, index, tiles, base, pool, blocks - exports, "others_1")
    p1 = (p1_first, p1_other)

    base = base_of(2, wall_at, order, message, pressure, (p1,), ((e2, o2), (e1, o1)))
    p2_first, e3, pool = first_blocks(order, index, tiles, base, (e2, o2) + around, "exports_2")
    around = around_of(e3)
    p2_other, o3 = other_blocks(order, index, tiles, base, pool, blocks - exports, "others_2")
    p2 = (p2_first, p2_other)

    rounded = ((e3, o3), (e2, o2), (e1, o1))
    walls = over_gx(walls_of(wall_at, message, rounded, around[2]), (around[0],))
    base = base_of(3, wall_at, order, message, pressure, (p2, p1), rounded)
    p3 = last_blocks(order, index, tiles, base, (e3, o3) + around)
    held = states_after(mats, pole, res, held, walls)
    return p3, held.reshape(states.shape)


def solution(mesh):
    return jax.shard_map(
        per_device,
        mesh=mesh,
        in_specs=(
            P(("gx", "gy"), None, None),
            P(("gx", "gy"), None, None, None),
            P(("gx", "gy"), None),
            P(("gx", "gy"), None),
            P(("gx", "gy")),
            P("gx", "gy", None, None),
            P("gx", "gy", None, None, None),
            P("gx", "gy", None, None),
            P("gx", "gy", None, None, None, None, None),
            P(),
            P(),
            P(),
        ),
        out_specs=(P(("gx", "gy"), None, None), P("gx", "gy", None, None, None, None, None)),
        check_vma=False,
    )
```

time: 269 us -> 125 us (0.46)
  the two profiles are of different devices: /device:TPU:105 before, /device:TPU:40 now
where the time goes in v1:
time: 125 us; the launch traced here: 124 us
  waiting for transfers between devices  49.8 us (40%)
  Pallas kernels  35.7 us (29%)
  starting transfers between devices  32 us (26%)
  local copies, waits for them, and re-layouts  5.55 us (4%)
    ppermute x5, waiting for transfers between devices, other_x(): return lax.ppermute(value, 'gx', [(i, i ^ 1) for i in range(count)])  19.9 us
    ppermute x3, waiting for transfers between devices, around_of(): passed = lax.ppermute(across, 'gx', on)  17.9 us
    ppermute x6, waiting for transfers between devices, along_y(): lax.ppermute(value, 'gx', [(i, (i + 2 * steps) % count) for i in range(co...  12 us
    ppermute x6, starting transfers between devices, along_y(): lax.ppermute(value, 'gx', [(i, (i + 2 * steps) % count) for i in range(co...  8.1 us
    ppermute x6, starting transfers between devices, along_gy(): return lax.ppermute(value, 'gy', pairs + [(j, i) for i, j in pairs])  8 us
    pallas_call x2, Pallas kernels, other_blocks(): pl.pallas_call(other_kernel, out_shape=(jax.ShapeDtypeStruct((count, rows...  7.64 us
    ppermute x5, starting transfers between devices, other_x(): return lax.ppermute(value, 'gx', [(i, i ^ 1) for i in range(count)])  7.02 us
    pallas_call x1, Pallas kernels, last_blocks(): pl.pallas_call(last_kernel, out_shape=jax.ShapeDtypeStruct((blocks, rows,...  6.86 us
  transfers between devices with their start and end apart: 23, of which 11 were waited for; matrix products, arithmetic and copies ran while one was open for 0% of the time, Pallas kernels for 19%

profile of v1, /device:TPU:40, one launch (start us, length us, event | category | flops | bytes accessed | tf_op | source)
XLA Modules:
  0.0 124.2 jit_solution(7949529866760879121)
XLA Ops:
  0.7 0.0 slice-start
  0.7 3.4 %exports.1.refs_5_.refs_0_.refs_9_.refs_13_ = bf16[16,128,128]{2,1,0:T(8,128)(2,1)} custom-call(s32[16]{0:T(128)} %ids.3, f32[40,128,128]{2,1,0:T(8,128)} %pressure.9), custom_call_target="tpu_custom_call" | custom-call | tf_op jit(solution)/shard_map/exports/pallas_call | solution.py:130
  4.1 0.1 collective-permute-start.1
  4.2 1.6 %collective-permute-start.5 = (bf16[16,128,128]{2,1,0:T(8,128)(2,1)}, bf16[16,128,128]{2,1,0:T(8,128)(2,1)S(1)}, u32[]{:S(2)}, u32[]{:S(2)}) collective-permute-start(bf16[16,128,128]{2,1,0:T(8,128)(2,1)} %exports.1.refs_5_.refs_0_.refs_9_.refs_13_), channel_id=1, source_target_pairs={{0,16},{16,0},{32,48},{48,32},{64,80},{80,64},{96,112},{112,96},{1... | collective-permute-start | bytes 1572872 | tf_op jit(solution)/shard_map/ppermute | solution.py:38
  5.8 1.9 %collective-permute-start = (bf16[16,128,128]{2,1,0:T(8,128)(2,1)}, bf16[16,128,128]{2,1,0:T(8,128)(2,1)S(1)}, u32[]{:S(2)}, u32[]{:S(2)}) collective-permute-start(bf16[16,128,128]{2,1,0:T(8,128)(2,1)} %exports.1.refs_5_.refs_0_.refs_9_.refs_13_), channel_id=1, source_target_pairs={{1,2},{3,4},{5,6},{9,10},{11,12},{13,14},{2,1},{4,3},{6,5},{10,9},... | collective-permute-start | bytes 1572872 | tf_op jit(solution)/shard_map/ppermute | solution.py:48
  7.8 0.0 copy-start.1
  7.8 0.0 copy-start.4
  7.8 0.0 copy-start.5
  7.8 0.0 copy-start.10
  7.8 0.0 copy-start.11
  7.8 1.0 responses.1
  8.9 1.6 %collective-permute-start.2 = (bf16[4,272,128]{2,1,0:T(8,128)(2,1)S(1)}, bf16[4,272,128]{2,1,0:T(8,128)(2,1)S(1)}, u32[]{:S(2)}, u32[]{:S(2)}) collective-permute-start(bf16[4,272,128]{2,1,0:T(8,128)(2,1)S(1)} %get-tuple-element.28), channel_id=1, source_target_pairs={{0,32},{16,48},{32,64},{48,80},{64,96},{80,112},{96,0},{112,16},{1... | collective-permute-start | bytes 835592 | tf_op jit(solution)/shard_map/ppermute | solution.py:43
  10.5 0.5 collective-permute-start.3
  11.0 2.3 %collective-permute-start.4 = (bf16[4,272,128]{2,1,0:T(8,128)(2,1)S(1)}, bf16[4,272,128]{2,1,0:T(8,128)(2,1)S(1)}, u32[]{:S(2)}, u32[]{:S(2)}) collective-permute-start(bf16[4,272,128]{2,1,0:T(8,128)(2,1)S(1)} %get-tuple-element.30), channel_id=1, source_target_pairs={{0,64},{16,80},{32,96},{48,112},{64,0},{80,16},{96,32},{112,48},{1... | collective-permute-start | bytes 835592 | tf_op jit(solution)/shard_map/ppermute | solution.py:43
  13.3 5.5 %collective-permute-done.5.refs_4_.refs_2_ = bf16[16,128,128]{2,1,0:T(8,128)(2,1)S(1)} collective-permute-done((bf16[16,128,128]{2,1,0:T(8,128)(2,1)}, bf16[16,128,128]{2,1,0:T(8,128)(2,1)S(1)}, u32[]{:S(2)}, u32[]{:S(2)}) %collective-permute-start.5) | collective-permute-done | bytes 524320 | tf_op jit(solution)/shard_map/ppermute | solution.py:38
  18.8 0.0 collective-permute-done.2.refs_1_
  18.8 0.5 collective-permute-done.3.refs_2_
  19.3 6.7 %collective-permute-done.4.refs_3_ = bf16[4,272,128]{2,1,0:T(8,128)(2,1)S(1)} collective-permute-done((bf16[4,272,128]{2,1,0:T(8,128)(2,1)S(1)}, bf16[4,272,128]{2,1,0:T(8,128)(2,1)S(1)}, u32[]{:S(2)}, u32[]{:S(2)}) %collective-permute-start.4) | collective-permute-done | bytes 278560 | tf_op jit(solution)/shard_map/ppermute | solution.py:43
  26.0 0.7 turned.2
  26.7 0.6 collective-permute-start.6
  27.3 0.7 collective-permute-start.8
  28.0 1.9 %collective-permute-start.7 = (bf16[16,128,128]{2,1,0:T(8,128)(2,1)S(1)}, bf16[16,128,128]{2,1,0:T(8,128)(2,1)S(1)}, u32[]{:S(2)}, u32[]{:S(2)}) collective-permute-start(bf16[16,128,128]{2,1,0:T(8,128)(2,1)S(1)} %collective-permute-done.5.refs_4_.refs_2_), channel_id=1, source_target_pairs={{48,16},{80,48},{112,80},{0,32},{32,64},{64,96},{49,17},{81,49},{1... | collective-permute-start | bytes 1572872 | tf_op jit(solution)/shard_map/ppermute | solution.py:58
  30.0 0.0 copy-start
  30.0 5.5 %copy-done = bf16[40,12,128,128]{3,2,1,0:T(8,128)(2,1)S(1)} copy-done((bf16[40,12,128,128]{3,2,1,0:T(8,128)(2,1)S(1)}, bf16[40,12,128,128]{3,2,1,0:T(8,128)(2,1)}, u32[]{:S(2)}) %copy-start) | copy-done | bytes 15728664
  35.5 2.1 %prepare.1 = (s32[40]{0:T(128)S(1)}, s32[12,40]{1,0:T(8,128)S(1)}, s32[2,8]{1,0:T(2,128)S(1)}, bf16[24,128,128]{2,1,0:T(8,128)(2,1)S(1)}) custom-call(s32[16]{0:T(128)S(1)} %copy-done.10, s32[12,40]{1,0:T(8,128)S(1)} %bitcast.24, s32[12,40]{1,0:T(8,128)S(1)} %bitcast.25, s32[2,8]{1,0:T(2,128)S(1)} %bitcast.33, f32[40,128,128]{2,1,0:T(8,128)S(1)} %copy-done.1, ...), custom_call_target="tpu_custom_call" | custom-call | tf_op jit(solution)/shard_map/prepare/pallas_call | solution.py:184
  37.6 4.3 %collective-permute-done.6.refs_4_ = bf16[8,272,128]{2,1,0:T(8,128)(2,1)S(1)} collective-permute-done((bf16[8,272,128]{2,1,0:T(8,128)(2,1)S(1)}, bf16[8,272,128]{2,1,0:T(8,128)(2,1)S(1)}, u32[]{:S(2)}, u32[]{:S(2)}) %collective-permute-start.6) | collective-permute-done | bytes 557088 | tf_op jit(solution)/shard_map/ppermute | solution.py:38
  41.9 1.2 base_1.1.base
  43.1 0.0 collective-permute-done.8.refs_6_
  43.1 1.0 collective-permute-done.7.refs_3_
  44.1 3.1 %exports_1.1 = (f32[16,128,128]{2,1,0:T(8,128)S(1)}, bf16[16,128,128]{2,1,0:T(8,128)(2,1)S(1)}, bf16[104,128,128]{2,1,0:T(8,128)(2,1)S(1)}) custom-call(s32[40]{0:T(128)S(1)} %get-tuple-element.24.order, s32[12,40]{1,0:T(8,128)S(1)} %get-tuple-element.25.index, bf16[40,1536,128]{2,1,0:T(8,128)(2,1)S(1)} %bitcast.17, f32[40,128,128]{2,1,0:T(8,128)S(1)} %base_1.1.base, ...), custom_call_target="tpu_custom_call" | custom-call | tf_op jit(solution)/shard_map/exports_1/pallas_call | solution.py:426
  47.2 1.6 %collective-permute-start.9 = (bf16[16,128,128]{2,1,0:T(8,128)(2,1)S(1)}, bf16[16,128,128]{2,1,0:T(8,128)(2,1)S(1)}, u32[]{:S(2)}, u32[]{:S(2)}) collective-permute-start(bf16[16,128,128]{2,1,0:T(8,128)(2,1)S(1)} %get-tuple-element.35.refs_7_.refs_0_.refs_11_), channel_id=1, source_target_pairs={{0,16},{16,0},{32,48},{48,32},{64,80},{80,64},{96,112},{112,96},{1... | collective-permute-start | bytes 1572872 | tf_op jit(solution)/shard_map/ppermute | solution.py:38
  48.7 1.9 %collective-permute-start.12 = (bf16[16,128,128]{2,1,0:T(8,128)(2,1)S(1)}, bf16[16,128,128]{2,1,0:T(8,128)(2,1)S(1)}, u32[]{:S(2)}, u32[]{:S(2)}) collective-permute-start(bf16[16,128,128]{2,1,0:T(8,128)(2,1)S(1)} %get-tuple-element.35.refs_7_.refs_0_.refs_11_), channel_id=1, source_target_pairs={{1,2},{3,4},{5,6},{9,10},{11,12},{13,14},{2,1},{4,3},{6,5},{10,9},... | collective-permute-start | bytes 1572872 | tf_op jit(solution)/shard_map/ppermute | solution.py:48
  50.6 2.1 %collective-permute-start.11 = (bf16[16,128,128]{2,1,0:T(8,128)(2,1)S(1)}, bf16[16,128,128]{2,1,0:T(8,128)(2,1)S(1)}, u32[]{:S(2)}, u32[]{:S(2)}) collective-permute-start(bf16[16,128,128]{2,1,0:T(8,128)(2,1)S(1)} %get-tuple-element.35.refs_7_.refs_0_.refs_11_), channel_id=1, source_target_pairs={{0,1},{2,3},{4,5},{6,7},{8,9},{10,11},{12,13},{14,15},{1,0},{3,2},... | collective-permute-start | bytes 1572872 | tf_op jit(solution)/shard_map/ppermute | solution.py:48
  52.7 7.8 %collective-permute-done.9.refs_2_ = bf16[16,128,128]{2,1,0:T(8,128)(2,1)S(1)} collective-permute-done((bf16[16,128,128]{2,1,0:T(8,128)(2,1)S(1)}, bf16[16,128,128]{2,1,0:T(8,128)(2,1)S(1)}, u32[]{:S(2)}, u32[]{:S(2)}) %collective-permute-start.9) | collective-permute-done | bytes 524320 | tf_op jit(solution)/shard_map/ppermute | solution.py:38
  60.5 0.7 collective-permute-start.13
  61.2 2.5 %collective-permute-start.10 = (bf16[16,128,128]{2,1,0:T(8,128)(2,1)S(1)}, bf16[16,128,128]{2,1,0:T(8,128)(2,1)S(1)}, u32[]{:S(2)}, u32[]{:S(2)}) collective-permute-start(bf16[16,128,128]{2,1,0:T(8,128)(2,1)S(1)} %collective-permute-done.9.refs_2_), channel_id=1, source_target_pairs={{48,16},{80,48},{112,80},{0,32},{32,64},{64,96},{49,17},{81,49},{1... | collective-permute-start | bytes 1572872 | tf_op jit(solution)/shard_map/ppermute | solution.py:58
  63.8 3.8 %others_1.1 = (f32[24,128,128]{2,1,0:T(8,128)S(1)}, bf16[24,128,128]{2,1,0:T(8,128)(2,1)S(1)}) custom-call(s32[40]{0:T(128)S(1)} %get-tuple-element.24.order, s32[12,40]{1,0:T(8,128)S(1)} %get-tuple-element.25.index, bf16[40,1536,128]{2,1,0:T(8,128)(2,1)S(1)} %bitcast.18, f32[40,128,128]{2,1,0:T(8,128)S(1)} %base_1.1.base, ...), custom_call_target="tpu_custom_call" | custom-call | tf_op jit(solution)/shard_map/others_1/pallas_call | solution.py:455
  67.6 1.3 %base_2.1.base = f32[40,128,128]{2,1,0:T(8,128)S(1)} custom-call(s32[2,8]{1,0:T(2,128)S(1)} %get-tuple-element.26.wall_at, s32[40]{0:T(128)S(1)} %get-tuple-element.24.order, f32[40,128,128]{2,1,0:T(8,128)S(1)} %copy-done.1, bf16[4,272,128]{2,1,0:T(8,128)(2,1)S(1)} %get-tuple-element.27.refs_0_, bf16[4,272,128]{2,1,0:T(8,128)(2,1)S(1)} %collective-permute-done.2.refs_1_, ...), custom_call_target="tpu_custom_call" | custom-call | tf_op jit(solution)/shard_map/base_2/pallas_call | solution.py:305
  68.8 0.0 collective-permute-done.12.refs_5_
  68.9 0.0 collective-permute-done.13.refs_6_
  68.9 6.6 %collective-permute-done.10.refs_3_ = bf16[16,128,128]{2,1,0:T(8,128)(2,1)S(1)} collective-permute-done((bf16[16,128,128]{2,1,0:T(8,128)(2,1)S(1)}, bf16[16,128,128]{2,1,0:T(8,128)(2,1)S(1)}, u32[]{:S(2)}, u32[]{:S(2)}) %collective-permute-start.10) | collective-permute-done | bytes 524320 | tf_op jit(solution)/shard_map/ppermute | solution.py:58
  75.5 3.1 %exports_2.1 = (f32[16,128,128]{2,1,0:T(8,128)S(1)}, bf16[16,128,128]{2,1,0:T(8,128)(2,1)S(1)}, bf16[104,128,128]{2,1,0:T(8,128)(2,1)S(1)}) custom-call(s32[40]{0:T(128)S(1)} %get-tuple-element.24.order, s32[12,40]{1,0:T(8,128)S(1)} %get-tuple-element.25.index, bf16[40,1536,128]{2,1,0:T(8,128)(2,1)S(1)} %bitcast.19, f32[40,128,128]{2,1,0:T(8,128)S(1)} %base_2.1.base, ...), custom_call_target="tpu_custom_call" | custom-call | tf_op jit(solution)/shard_map/exports_2/pallas_call | solution.py:426
  78.6 0.1 collective-permute-start.16
  78.7 1.6 %collective-permute-start.14 = (bf16[16,128,128]{2,1,0:T(8,128)(2,1)S(1)}, bf16[16,128,128]{2,1,0:T(8,128)(2,1)S(1)}, u32[]{:S(2)}, u32[]{:S(2)}) collective-permute-start(bf16[16,128,128]{2,1,0:T(8,128)(2,1)S(1)} %get-tuple-element.40.refs_9_.refs_0_.refs_5_), channel_id=1, source_target_pairs={{0,16},{16,0},{32,48},{48,32},{64,80},{80,64},{96,112},{112,96},{1... | collective-permute-start | bytes 1572872 | tf_op jit(solution)/shard_map/ppermute | solution.py:38
  80.2 3.8 %others_2.1 = (f32[24,128,128]{2,1,0:T(8,128)S(1)}, bf16[24,128,128]{2,1,0:T(8,128)(2,1)S(1)}) custom-call(s32[40]{0:T(128)S(1)} %get-tuple-element.24.order, s32[12,40]{1,0:T(8,128)S(1)} %get-tuple-element.25.index, bf16[40,1536,128]{2,1,0:T(8,128)(2,1)S(1)} %bitcast.20, f32[40,128,128]{2,1,0:T(8,128)S(1)} %base_2.1.base, ...), custom_call_target="tpu_custom_call" | custom-call | tf_op jit(solution)/shard_map/others_2/pallas_call | solution.py:455
  84.1 0.0 collective-permute-done.16.refs_4_.after
  84.1 1.0 walls.1
  85.1 0.9 collective-permute-start.19
  86.0 1.2 collective-permute-start.20
  87.2 1.6 %collective-permute-start.21 = (bf16[4,256,128]{2,1,0:T(8,128)(2,1)S(1)}, bf16[4,256,128]{2,1,0:T(8,128)(2,1)S(1)}, u32[]{:S(2)}, u32[]{:S(2)}) collective-permute-start(bf16[4,256,128]{2,1,0:T(8,128)(2,1)S(1)} %get-tuple-element.45), channel_id=1, source_target_pairs={{0,64},{16,80},{32,96},{48,112},{64,0},{80,16},{96,32},{112,48},{1... | collective-permute-start | bytes 786440 | tf_op jit(solution)/shard_map/ppermute | solution.py:43
  88.8 1.9 %collective-permute-start.17 = (bf16[16,128,128]{2,1,0:T(8,128)(2,1)S(1)}, bf16[16,128,128]{2,1,0:T(8,128)(2,1)S(1)}, u32[]{:S(2)}, u32[]{:S(2)}) collective-permute-start(bf16[16,128,128]{2,1,0:T(8,128)(2,1)S(1)} %get-tuple-element.40.refs_9_.refs_0_.refs_5_), channel_id=1, source_target_pairs={{1,2},{3,4},{5,6},{9,10},{11,12},{13,14},{2,1},{4,3},{6,5},{10,9},... | collective-permute-start | bytes 1572872 | tf_op jit(solution)/shard_map/ppermute | solution.py:48
  90.7 2.3 %collective-permute-done.14.refs_2_.refs_4_ = bf16[16,128,128]{2,1,0:T(8,128)(2,1)S(1)} collective-permute-done((bf16[16,128,128]{2,1,0:T(8,128)(2,1)S(1)}, bf16[16,128,128]{2,1,0:T(8,128)(2,1)S(1)}, u32[]{:S(2)}, u32[]{:S(2)}) %collective-permute-start.14) | collective-permute-done | bytes 524320 | tf_op jit(solution)/shard_map/ppermute | solution.py:38
  93.0 0.7 collective-permute-start.18
  93.7 0.5 collective-permute-done.19.refs_1_
  94.2 2.4 %collective-permute-start.15 = (bf16[16,128,128]{2,1,0:T(8,128)(2,1)S(1)}, bf16[16,128,128]{2,1,0:T(8,128)(2,1)S(1)}, u32[]{:S(2)}, u32[]{:S(2)}) collective-permute-start(bf16[16,128,128]{2,1,0:T(8,128)(2,1)S(1)} %collective-permute-done.14.refs_2_.refs_4_), channel_id=1, source_target_pairs={{48,16},{80,48},{112,80},{0,32},{32,64},{64,96},{49,17},{81,49},{1... | collective-permute-start | bytes 1572872 | tf_op jit(solution)/shard_map/ppermute | solution.py:58
  96.6 0.0 collective-permute-done.20.refs_2_
  96.6 4.3 %collective-permute-done.21.refs_3_ = bf16[4,256,128]{2,1,0:T(8,128)(2,1)S(1)} collective-permute-done((bf16[4,256,128]{2,1,0:T(8,128)(2,1)S(1)}, bf16[4,256,128]{2,1,0:T(8,128)(2,1)S(1)}, u32[]{:S(2)}, u32[]{:S(2)}) %collective-permute-start.21) | collective-permute-done | bytes 262176 | tf_op jit(solution)/shard_map/ppermute | solution.py:43
  100.9 0.7 turned.3
  101.6 1.7 %collective-permute-start.22 = (bf16[8,256,128]{2,1,0:T(8,128)(2,1)S(1)}, bf16[8,256,128]{2,1,0:T(8,128)(2,1)S(1)}, u32[]{:S(2)}, u32[]{:S(2)}) collective-permute-start(bf16[8,256,128]{2,1,0:T(8,128)(2,1)S(1)} %turned.3), channel_id=1, source_target_pairs={{0,16},{16,0},{32,48},{48,32},{64,80},{80,64},{96,112},{112,96},{1... | collective-permute-start | bytes 1572872 | tf_op jit(solution)/shard_map/ppermute | solution.py:38
  103.3 1.3 %base_3.1.base = f32[40,128,128]{2,1,0:T(8,128)S(1)} custom-call(s32[2,8]{1,0:T(2,128)S(1)} %get-tuple-element.26.wall_at, s32[40]{0:T(128)S(1)} %get-tuple-element.24.order, f32[40,128,128]{2,1,0:T(8,128)S(1)} %copy-done.1, bf16[4,272,128]{2,1,0:T(8,128)(2,1)S(1)} %get-tuple-element.27.refs_0_, bf16[4,272,128]{2,1,0:T(8,128)(2,1)S(1)} %collective-permute-done.2.refs_1_, ...), custom_call_target="tpu_custom_call" | custom-call | tf_op jit(solution)/shard_map/base_3/pallas_call | solution.py:305
  104.6 0.0 collective-permute-done.18.refs_6_
  104.6 10.3 %collective-permute-done.15.refs_3_ = bf16[16,128,128]{2,1,0:T(8,128)(2,1)S(1)} collective-permute-done((bf16[16,128,128]{2,1,0:T(8,128)(2,1)S(1)}, bf16[16,128,128]{2,1,0:T(8,128)(2,1)S(1)}, u32[]{:S(2)}, u32[]{:S(2)}) %collective-permute-start.15) | collective-permute-done | bytes 524320 | tf_op jit(solution)/shard_map/ppermute | solution.py:58
  114.9 6.9 %last.1 = f32[40,128,128]{2,1,0:T(8,128)} custom-call(s32[40]{0:T(128)S(1)} %get-tuple-element.24.order, s32[12,40]{1,0:T(8,128)S(1)} %get-tuple-element.25.index, bf16[40,1536,128]{2,1,0:T(8,128)(2,1)S(1)} %bitcast.21, f32[40,128,128]{2,1,0:T(8,128)S(1)} %base_3.1.base, bf16[16,128,128]{2,1,0:T(8,128)(2,1)S(1)} %get-tuple-element.40.refs_9_.refs_0_.refs_5_, ...), custom_call_target="tpu_custom_call" | custom-call | tf_op jit(solution)/shard_map/last/pallas_call | solution.py:489
  121.8 2.4 %states_after.1 = f32[16,2,128,128]{3,2,1,0:T(8,128)} custom-call(s32[2,8]{1,0:T(2,128)S(1)} %bitcast.28, f32[2,16]{1,0:T(2,128)S(1)} %bitcast.30, f32[2,16]{1,0:T(2,128)S(1)} %bitcast.32, f32[16,2,128,128]{3,2,1,0:T(8,128)S(1)} %bitcast.23, bf16[4,256,128]{2,1,0:T(8,128)(2,1)S(1)} %get-tuple-element.42.refs_0_, ...), custom_call_target="tpu_custom_call" | custom-call | tf_op jit(solution)/shard_map/states_after/pallas_call | solution.py:368
  (32 shorter events, 0.1 us)
Async XLA Ops:
  0.6 7.1 %copy-start.12 = (f32[16]{0:T(128)S(1)}, f32[16]{0:T(128)}, u32[]{:S(2)}) copy-start(f32[16]{0:T(128)} %direct.1) | copy-start | bytes 196
  0.6 7.1 %copy-start.9 = (f32[16,2]{0,1:T(2,128)S(1)}, f32[16,2]{0,1:T(2,128)}, u32[]{:S(2)}) copy-start(f32[16,2]{0,1:T(2,128)} %param.22) | copy-start | bytes 388
  0.7 7.1 %copy-start.8 = (f32[16,2]{0,1:T(2,128)S(1)}, f32[16,2]{0,1:T(2,128)}, u32[]{:S(2)}) copy-start(f32[16,2]{0,1:T(2,128)} %param.21) | copy-start | bytes 388
  0.7 7.1 %copy-start.3 = (f32[1,1,8,2,2,128,128]{6,5,4,3,2,1,0:T(8,128)S(1)}, f32[1,1,8,2,2,128,128]{6,5,4,3,2,1,0:T(8,128)}, u32[]{:S(2)}) copy-start(f32[1,1,8,2,2,128,128]{6,5,4,3,2,1,0:T(8,128)} %param.20) | copy-start | bytes 6291460
  0.7 7.1 %copy-start.7 = (s32[1,1,8,2]{2,3,1,0:T(2,128)S(1)}, s32[1,1,8,2]{2,3,1,0:T(2,128)}, u32[]{:S(2)}) copy-start(s32[1,1,8,2]{2,3,1,0:T(2,128)} %param.19) | copy-start | bytes 196
  0.7 7.1 %copy-start.6 = (f32[1,1,8,2,128]{4,3,2,1,0:T(2,128)S(1)}, f32[1,1,8,2,128]{4,3,2,1,0:T(2,128)}, u32[]{:S(2)}) copy-start(f32[1,1,8,2,128]{4,3,2,1,0:T(2,128)} %param.18) | copy-start | bytes 24580
  0.7 43.4 %slice-start = ((s8[15728640]{0:T(1024)(128)(4,1)}), s8[3145728]{0:T(1024)(128)(4,1)S(1)}, s32[]{:S(2)}) async-start(s8[15728640]{0:T(1024)(128)(4,1)} %bitcast.15), calls=%async_computation | async-start | bytes 6291456
  4.1 3.6 %collective-permute-start.1 = (bf16[16,128,128]{2,1,0:T(8,128)(2,1)}, bf16[16,128,128]{2,1,0:T(8,128)(2,1)S(1)}, u32[]{:S(2)}, u32[]{:S(2)}) collective-permute-start(bf16[16,128,128]{2,1,0:T(8,128)(2,1)} %exports.1.refs_5_.refs_0_.refs_9_.refs_13_), channel_id=1, source_target_pairs={{0,1},{2,3},{4,5},{6,7},{8,9},{10,11},{12,13},{14,15},{1,0},{3,2},... | collective-permute-start | bytes 1572872 | tf_op jit(solution)/shard_map/ppermute | solution.py:48
  4.2 14.6 %collective-permute-start.5 = (bf16[16,128,128]{2,1,0:T(8,128)(2,1)}, bf16[16,128,128]{2,1,0:T(8,128)(2,1)S(1)}, u32[]{:S(2)}, u32[]{:S(2)}) collective-permute-start(bf16[16,128,128]{2,1,0:T(8,128)(2,1)} %exports.1.refs_5_.refs_0_.refs_9_.refs_13_), channel_id=1, source_target_pairs={{0,16},{16,0},{32,48},{48,32},{64,80},{80,64},{96,112},{112,96},{1... | collective-permute-start | bytes 1572872 | tf_op jit(solution)/shard_map/ppermute | solution.py:38
  5.8 13.0 %collective-permute-start = (bf16[16,128,128]{2,1,0:T(8,128)(2,1)}, bf16[16,128,128]{2,1,0:T(8,128)(2,1)S(1)}, u32[]{:S(2)}, u32[]{:S(2)}) collective-permute-start(bf16[16,128,128]{2,1,0:T(8,128)(2,1)} %exports.1.refs_5_.refs_0_.refs_9_.refs_13_), channel_id=1, source_target_pairs={{1,2},{3,4},{5,6},{9,10},{11,12},{13,14},{2,1},{4,3},{6,5},{10,9},... | collective-permute-start | bytes 1572872 | tf_op jit(solution)/shard_map/ppermute | solution.py:48
  7.8 22.2 %copy-start.1 = (f32[40,128,128]{2,1,0:T(8,128)S(1)}, f32[40,128,128]{2,1,0:T(8,128)}, u32[]{:S(2)}) copy-start(f32[40,128,128]{2,1,0:T(8,128)} %pressure.9) | copy-start | bytes 7864324
  7.8 22.2 %copy-start.4 = (s32[40,12]{0,1:T(8,128)S(1)}, s32[40,12]{0,1:T(8,128)}, u32[]{:S(2)}) copy-start(s32[40,12]{0,1:T(8,128)} %param.14) | copy-start | bytes 5764
  7.8 22.2 %copy-start.5 = (s32[40,12]{0,1:T(8,128)S(1)}, s32[40,12]{0,1:T(8,128)}, u32[]{:S(2)}) copy-start(s32[40,12]{0,1:T(8,128)} %param.15) | copy-start | bytes 5764
  7.8 22.2 %copy-start.10 = (s32[16]{0:T(128)S(1)}, s32[16]{0:T(128)}, u32[]{:S(2)}) copy-start(s32[16]{0:T(128)} %ids.3) | copy-start | bytes 196
  7.8 22.2 %copy-start.11 = (s32[1,1,8,2]{2,3,1,0:T(2,128)S(1)}, s32[1,1,8,2]{2,3,1,0:T(2,128)}, u32[]{:S(2)}) copy-start(s32[1,1,8,2]{2,3,1,0:T(2,128)} %param.17) | copy-start | bytes 196
  8.9 9.9 %collective-permute-start.2 = (bf16[4,272,128]{2,1,0:T(8,128)(2,1)S(1)}, bf16[4,272,128]{2,1,0:T(8,128)(2,1)S(1)}, u32[]{:S(2)}, u32[]{:S(2)}) collective-permute-start(bf16[4,272,128]{2,1,0:T(8,128)(2,1)S(1)} %get-tuple-element.28), channel_id=1, source_target_pairs={{0,32},{16,48},{32,64},{48,80},{64,96},{80,112},{96,0},{112,16},{1... | collective-permute-start | bytes 835592 | tf_op jit(solution)/shard_map/ppermute | solution.py:43
  10.5 8.8 %collective-permute-start.3 = (bf16[4,272,128]{2,1,0:T(8,128)(2,1)S(1)}, bf16[4,272,128]{2,1,0:T(8,128)(2,1)S(1)}, u32[]{:S(2)}, u32[]{:S(2)}) collective-permute-start(bf16[4,272,128]{2,1,0:T(8,128)(2,1)S(1)} %get-tuple-element.29), channel_id=1, source_target_pairs={{0,96},{16,112},{32,0},{48,16},{64,32},{80,48},{96,64},{112,80},{1... | collective-permute-start | bytes 835592 | tf_op jit(solution)/shard_map/ppermute | solution.py:43
  11.0 15.0 %collective-permute-start.4 = (bf16[4,272,128]{2,1,0:T(8,128)(2,1)S(1)}, bf16[4,272,128]{2,1,0:T(8,128)(2,1)S(1)}, u32[]{:S(2)}, u32[]{:S(2)}) collective-permute-start(bf16[4,272,128]{2,1,0:T(8,128)(2,1)S(1)} %get-tuple-element.30), channel_id=1, source_target_pairs={{0,64},{16,80},{32,96},{48,112},{64,0},{80,16},{96,32},{112,48},{1... | collective-permute-start | bytes 835592 | tf_op jit(solution)/shard_map/ppermute | solution.py:43
  26.7 15.2 %collective-permute-start.6 = (bf16[8,272,128]{2,1,0:T(8,128)(2,1)S(1)}, bf16[8,272,128]{2,1,0:T(8,128)(2,1)S(1)}, u32[]{:S(2)}, u32[]{:S(2)}) collective-permute-start(bf16[8,272,128]{2,1,0:T(8,128)(2,1)S(1)} %turned.2), channel_id=1, source_target_pairs={{0,16},{16,0},{32,48},{48,32},{64,80},{80,64},{96,112},{112,96},{1... | collective-permute-start | bytes 1671176 | tf_op jit(solution)/shard_map/ppermute | solution.py:38
  27.3 15.7 %collective-permute-start.8 = (bf16[16,128,128]{2,1,0:T(8,128)(2,1)S(1)}, bf16[16,128,128]{2,1,0:T(8,128)(2,1)S(1)}, u32[]{:S(2)}, u32[]{:S(2)}) collective-permute-start(bf16[16,128,128]{2,1,0:T(8,128)(2,1)S(1)} %collective-permute-done.5.refs_4_.refs_2_), channel_id=1, source_target_pairs={{7,24},{23,8},{39,56},{55,40},{71,88},{87,72},{103,120},{119,104},... | collective-permute-start | bytes 1572872 | tf_op jit(solution)/shard_map/ppermute | solution.py:60
  28.0 16.0 %collective-permute-start.7 = (bf16[16,128,128]{2,1,0:T(8,128)(2,1)S(1)}, bf16[16,128,128]{2,1,0:T(8,128)(2,1)S(1)}, u32[]{:S(2)}, u32[]{:S(2)}) collective-permute-start(bf16[16,128,128]{2,1,0:T(8,128)(2,1)S(1)} %collective-permute-done.5.refs_4_.refs_2_), channel_id=1, source_target_pairs={{48,16},{80,48},{112,80},{0,32},{32,64},{64,96},{49,17},{81,49},{1... | collective-permute-start | bytes 1572872 | tf_op jit(solution)/shard_map/ppermute | solution.py:58
  30.0 5.5 %copy-start = (bf16[40,12,128,128]{3,2,1,0:T(8,128)(2,1)S(1)}, bf16[40,12,128,128]{3,2,1,0:T(8,128)(2,1)}, u32[]{:S(2)}) copy-start(bf16[40,12,128,128]{3,2,1,0:T(8,128)(2,1)} %param.13) | copy-start | bytes 47185924
  35.5 6.4 %copy-start.2 = (bf16[16,128,128]{2,1,0:T(8,128)(2,1)S(1)}, bf16[16,128,128]{2,1,0:T(8,128)(2,1)}, u32[]{:S(2)}) copy-start(bf16[16,128,128]{2,1,0:T(8,128)(2,1)} %exports.1.refs_5_.refs_0_.refs_9_.refs_13_) | copy-start | bytes 1572868
  35.5 8.6 %slice-start.1 = ((s8[15728640]{0:T(1024)(128)(4,1)}), s8[4194304]{0:T(1024)(128)(4,1)S(1)}, s32[]{:S(2)}) async-start(s8[15728640]{0:T(1024)(128)(4,1)} %bitcast.15), calls=%async_computation.1 | async-start | bytes 8388608
  35.5 8.6 %slice-start.2 = ((s8[15728640]{0:T(1024)(128)(4,1)}), s8[4194304]{0:T(1024)(128)(4,1)S(1)}, s32[]{:S(2)}) async-start(s8[15728640]{0:T(1024)(128)(4,1)} %bitcast.15), calls=%async_computation.2 | async-start | bytes 8388608
  35.5 8.6 %slice-start.3 = ((s8[15728640]{0:T(1024)(128)(4,1)}), s8[4194304]{0:T(1024)(128)(4,1)S(1)}, s32[]{:S(2)}) async-start(s8[15728640]{0:T(1024)(128)(4,1)} %bitcast.15), calls=%async_computation.3 | async-start | bytes 8388608
  47.2 13.4 %collective-permute-start.9 = (bf16[16,128,128]{2,1,0:T(8,128)(2,1)S(1)}, bf16[16,128,128]{2,1,0:T(8,128)(2,1)S(1)}, u32[]{:S(2)}, u32[]{:S(2)}) collective-permute-start(bf16[16,128,128]{2,1,0:T(8,128)(2,1)S(1)} %get-tuple-element.35.refs_7_.refs_0_.refs_11_), channel_id=1, source_target_pairs={{0,16},{16,0},{32,48},{48,32},{64,80},{80,64},{96,112},{112,96},{1... | collective-permute-start | bytes 1572872 | tf_op jit(solution)/shard_map/ppermute | solution.py:38
  48.7 20.1 %collective-permute-start.12 = (bf16[16,128,128]{2,1,0:T(8,128)(2,1)S(1)}, bf16[16,128,128]{2,1,0:T(8,128)(2,1)S(1)}, u32[]{:S(2)}, u32[]{:S(2)}) collective-permute-start(bf16[16,128,128]{2,1,0:T(8,128)(2,1)S(1)} %get-tuple-element.35.refs_7_.refs_0_.refs_11_), channel_id=1, source_target_pairs={{1,2},{3,4},{5,6},{9,10},{11,12},{13,14},{2,1},{4,3},{6,5},{10,9},... | collective-permute-start | bytes 1572872 | tf_op jit(solution)/shard_map/ppermute | solution.py:48
  50.6 18.2 %collective-permute-start.11 = (bf16[16,128,128]{2,1,0:T(8,128)(2,1)S(1)}, bf16[16,128,128]{2,1,0:T(8,128)(2,1)S(1)}, u32[]{:S(2)}, u32[]{:S(2)}) collective-permute-start(bf16[16,128,128]{2,1,0:T(8,128)(2,1)S(1)} %get-tuple-element.35.refs_7_.refs_0_.refs_11_), channel_id=1, source_target_pairs={{0,1},{2,3},{4,5},{6,7},{8,9},{10,11},{12,13},{14,15},{1,0},{3,2},... | collective-permute-start | bytes 1572872 | tf_op jit(solution)/shard_map/ppermute | solution.py:48
  60.5 8.3 %collective-permute-start.13 = (bf16[16,128,128]{2,1,0:T(8,128)(2,1)S(1)}, bf16[16,128,128]{2,1,0:T(8,128)(2,1)S(1)}, u32[]{:S(2)}, u32[]{:S(2)}) collective-permute-start(bf16[16,128,128]{2,1,0:T(8,128)(2,1)S(1)} %collective-permute-done.9.refs_2_), channel_id=1, source_target_pairs={{7,24},{23,8},{39,56},{55,40},{71,88},{87,72},{103,120},{119,104},... | collective-permute-start | bytes 1572872 | tf_op jit(solution)/shard_map/ppermute | solution.py:60
  61.2 14.3 %collective-permute-start.10 = (bf16[16,128,128]{2,1,0:T(8,128)(2,1)S(1)}, bf16[16,128,128]{2,1,0:T(8,128)(2,1)S(1)}, u32[]{:S(2)}, u32[]{:S(2)}) collective-permute-start(bf16[16,128,128]{2,1,0:T(8,128)(2,1)S(1)} %collective-permute-done.9.refs_2_), channel_id=1, source_target_pairs={{48,16},{80,48},{112,80},{0,32},{32,64},{64,96},{49,17},{81,49},{1... | collective-permute-start | bytes 1572872 | tf_op jit(solution)/shard_map/ppermute | solution.py:58
  78.6 5.5 %collective-permute-start.16 = (bf16[16,128,128]{2,1,0:T(8,128)(2,1)S(1)}, bf16[16,128,128]{2,1,0:T(8,128)(2,1)S(1)}, u32[]{:S(2)}, u32[]{:S(2)}) collective-permute-start(bf16[16,128,128]{2,1,0:T(8,128)(2,1)S(1)} %get-tuple-element.40.refs_9_.refs_0_.refs_5_), channel_id=1, source_target_pairs={{0,1},{2,3},{4,5},{6,7},{8,9},{10,11},{12,13},{14,15},{1,0},{3,2},... | collective-permute-start | bytes 1572872 | tf_op jit(solution)/shard_map/ppermute | solution.py:48
  78.7 14.3 %collective-permute-start.14 = (bf16[16,128,128]{2,1,0:T(8,128)(2,1)S(1)}, bf16[16,128,128]{2,1,0:T(8,128)(2,1)S(1)}, u32[]{:S(2)}, u32[]{:S(2)}) collective-permute-start(bf16[16,128,128]{2,1,0:T(8,128)(2,1)S(1)} %get-tuple-element.40.refs_9_.refs_0_.refs_5_), channel_id=1, source_target_pairs={{0,16},{16,0},{32,48},{48,32},{64,80},{80,64},{96,112},{112,96},{1... | collective-permute-start | bytes 1572872 | tf_op jit(solution)/shard_map/ppermute | solution.py:38
  85.1 9.2 %collective-permute-start.19 = (bf16[4,256,128]{2,1,0:T(8,128)(2,1)S(1)}, bf16[4,256,128]{2,1,0:T(8,128)(2,1)S(1)}, u32[]{:S(2)}, u32[]{:S(2)}) collective-permute-start(bf16[4,256,128]{2,1,0:T(8,128)(2,1)S(1)} %get-tuple-element.43), channel_id=1, source_target_pairs={{0,32},{16,48},{32,64},{48,80},{64,96},{80,112},{96,0},{112,16},{1... | collective-permute-start | bytes 786440 | tf_op jit(solution)/shard_map/ppermute | solution.py:43
  86.0 10.7 %collective-permute-start.20 = (bf16[4,256,128]{2,1,0:T(8,128)(2,1)S(1)}, bf16[4,256,128]{2,1,0:T(8,128)(2,1)S(1)}, u32[]{:S(2)}, u32[]{:S(2)}) collective-permute-start(bf16[4,256,128]{2,1,0:T(8,128)(2,1)S(1)} %get-tuple-element.44), channel_id=1, source_target_pairs={{0,96},{16,112},{32,0},{48,16},{64,32},{80,48},{96,64},{112,80},{1... | collective-permute-start | bytes 786440 | tf_op jit(solution)/shard_map/ppermute | solution.py:43
  87.2 13.7 %collective-permute-start.21 = (bf16[4,256,128]{2,1,0:T(8,128)(2,1)S(1)}, bf16[4,256,128]{2,1,0:T(8,128)(2,1)S(1)}, u32[]{:S(2)}, u32[]{:S(2)}) collective-permute-start(bf16[4,256,128]{2,1,0:T(8,128)(2,1)S(1)} %get-tuple-element.45), channel_id=1, source_target_pairs={{0,64},{16,80},{32,96},{48,112},{64,0},{80,16},{96,32},{112,48},{1... | collective-permute-start | bytes 786440 | tf_op jit(solution)/shard_map/ppermute | solution.py:43
  88.8 15.8 %collective-permute-start.17 = (bf16[16,128,128]{2,1,0:T(8,128)(2,1)S(1)}, bf16[16,128,128]{2,1,0:T(8,128)(2,1)S(1)}, u32[]{:S(2)}, u32[]{:S(2)}) collective-permute-start(bf16[16,128,128]{2,1,0:T(8,128)(2,1)S(1)} %get-tuple-element.40.refs_9_.refs_0_.refs_5_), channel_id=1, source_target_pairs={{1,2},{3,4},{5,6},{9,10},{11,12},{13,14},{2,1},{4,3},{6,5},{10,9},... | collective-permute-start | bytes 1572872 | tf_op jit(solution)/shard_map/ppermute | solution.py:48
  93.0 11.6 %collective-permute-start.18 = (bf16[16,128,128]{2,1,0:T(8,128)(2,1)S(1)}, bf16[16,128,128]{2,1,0:T(8,128)(2,1)S(1)}, u32[]{:S(2)}, u32[]{:S(2)}) collective-permute-start(bf16[16,128,128]{2,1,0:T(8,128)(2,1)S(1)} %collective-permute-done.14.refs_2_.refs_4_), channel_id=1, source_target_pairs={{7,24},{23,8},{39,56},{55,40},{71,88},{87,72},{103,120},{119,104},... | collective-permute-start | bytes 1572872 | tf_op jit(solution)/shard_map/ppermute | solution.py:60
  94.2 20.7 %collective-permute-start.15 = (bf16[16,128,128]{2,1,0:T(8,128)(2,1)S(1)}, bf16[16,128,128]{2,1,0:T(8,128)(2,1)S(1)}, u32[]{:S(2)}, u32[]{:S(2)}) collective-permute-start(bf16[16,128,128]{2,1,0:T(8,128)(2,1)S(1)} %collective-permute-done.14.refs_2_.refs_4_), channel_id=1, source_target_pairs={{48,16},{80,48},{112,80},{0,32},{32,64},{64,96},{49,17},{81,49},{1... | collective-permute-start | bytes 1572872 | tf_op jit(solution)/shard_map/ppermute | solution.py:58
  101.6 20.2 %collective-permute-start.22 = (bf16[8,256,128]{2,1,0:T(8,128)(2,1)S(1)}, bf16[8,256,128]{2,1,0:T(8,128)(2,1)S(1)}, u32[]{:S(2)}, u32[]{:S(2)}) collective-permute-start(bf16[8,256,128]{2,1,0:T(8,128)(2,1)S(1)} %turned.3), channel_id=1, source_target_pairs={{0,16},{16,0},{32,48},{48,32},{64,80},{80,64},{96,112},{112,96},{1... | collective-permute-start | bytes 1572872 | tf_op jit(solution)/shard_map/ppermute | solution.py:38

commit v2 on v1

--- a/solution.py
+++ b/solution.py
@@ -25,8 +25,8 @@
     return pltpu.CompilerParams(vmem_limit_bytes=megabytes * 1024 * 1024)
 
 
-def cost(flops, moved):
-    return pl.CostEstimate(flops=0, bytes_accessed=0, transcendentals=0)
+def cost(microseconds):
+    return pl.CostEstimate(flops=int(1e9 * microseconds), bytes_accessed=0, transcendentals=0)
 
 
 TURNS = (0, 1, -1, 2)
@@ -43,22 +43,19 @@
     return lax.ppermute(value, "gx", [(i, (i + 2 * steps) % count) for i in range(count)])
 
 
-def along_gy(value, first, skip=()):
-    pairs = [(i, i + 1) for i in range(first, lax.axis_size("gy") - 1, 2) if i not in skip]
+def along_gy(value, first):
+    pairs = [(i, i + 1) for i in range(first, lax.axis_size("gy") - 1, 2)]
     return lax.ppermute(value, "gy", pairs + [(j, i) for i, j in pairs])
 
 
-def around_of(exports):
-    gx, gy = lax.axis_size("gx"), lax.axis_size("gy")
-    seam = gy // 2 - 1
-    across = other_x(exports)
-    core = along_gy(exports, 0)
-    beside = along_gy(exports, 1, (seam,))
+def passed_on(across):
+    gx = lax.axis_size("gx")
     on = [(i, i - 2) for i in range(3, gx, 2)] + [(i, i + 2) for i in range(0, gx - 2, 2)]
-    passed = lax.ppermute(across, "gx", on)
-    over = [(i * gy + seam, (i ^ 1) * gy + seam + 1) for i in range(gx)]
-    seamed = lax.ppermute(across, ("gx", "gy"), over + [(j, i) for i, j in over])
-    return across, passed, core, beside, seamed
+    return lax.ppermute(across, "gx", on)
+
+
+def beside_of(exports):
+    return other_x(exports), along_gy(exports, 0), along_gy(exports, 1)
 
 
 def position():
@@ -70,14 +67,18 @@
     return 2 * ((y + turn) & 3) + (x ^ cross)
 
 
-def over_gx(parts, after):
-    cap = parts[0].shape[0] // 2
-    arrived = [parts[0]] + [along_y(parts[t], TURNS[t]) for t in range(1, len(TURNS))]
-    return (*arrived, other_x(turned(arrived, cap, after)))
-
-
-def turn_kernel(cap, *refs):
-    parts, (out, sems) = refs[: len(TURNS)], refs[-2:]
+def over_y(parts):
+    return (parts[0], *(along_y(parts[t], TURNS[t]) for t in range(1, len(TURNS))))
+
+
+def over_x(arrived, through=(), after=()):
+    cap = arrived[0].shape[0] // 2
+    slots, *through = turned(arrived, cap, through, after)
+    return (*arrived, other_x(slots)), *through
+
+
+def turn_kernel(cap, outs, *refs):
+    parts, out, sems = refs[: len(TURNS)], refs[-1 - outs], refs[-1]
     copies = [
         pltpu.make_async_copy(part.at[pl.ds(cap, cap)], out.at[pl.ds(t * cap, cap)], sems.at[t])
         for t, part in enumerate(parts)
@@ -88,18 +89,20 @@
         copy.wait()
 
 
-def turned(parts, cap, after):
+def turned(parts, cap, through, after):
     shape = (len(parts) * cap,) + parts[0].shape[1:]
-    return pl.pallas_call(
-        functools.partial(turn_kernel, cap),
-        out_shape=jax.ShapeDtypeStruct(shape, parts[0].dtype),
-        in_specs=[spec(pl.ANY)] * (len(parts) + len(after)),
-        out_specs=spec(pl.ANY),
+    kept = [jax.ShapeDtypeStruct(array.shape, array.dtype) for array in through]
+    return pl.pallas_call(
+        functools.partial(turn_kernel, cap, 1 + len(kept)),
+        out_shape=[jax.ShapeDtypeStruct(shape, parts[0].dtype)] + kept,
+        in_specs=[spec(pl.ANY)] * (len(parts) + len(through) + len(after)),
+        out_specs=[spec(pl.ANY)] * (1 + len(kept)),
         scratch_shapes=[DMA((len(parts),))],
-        compiler_params=params(8),
-        cost_estimate=cost(0, 1000000),
+        input_output_aliases={len(parts) + i: 1 + i for i in range(len(kept))},
+        compiler_params=params(8),
+        cost_estimate=cost(0),
         name="turned",
-    )(*parts, *after)
+    )(*parts, *through, *after)
 
 
 def arrivals(arrived, cap):
@@ -134,13 +137,13 @@
         out_specs=spec(VMEM),
         scratch_shapes=[VMEM((count,) + shape, F32), DMA((count,))],
         compiler_params=params(56),
-        cost_estimate=cost(0, count * 98304),
+        cost_estimate=cost(3),
         name="exports",
     )(ids, pressure)
 
 
-def prepare_kernel(ids, turn, offset, walls, pressure, tiles, after, order, index, wall_at, others, taken, place):
-    del tiles, after
+def prepare_kernel(ids, turn, offset, walls, pressure, after, order, index, wall_at, others, taken, place):
+    del after
     blocks, exports = order.shape[0], ids.shape[0]
 
     @pl.loop(0, blocks)
@@ -178,7 +181,7 @@
             wall_at[c, o] = jnp.where(at < 0, -1, place[jnp.maximum(at, 0)])
 
 
-def prepare(ids, turn, offset, walls, pressure, tiles, after):
+def prepare(ids, turn, offset, walls, pressure, after):
     blocks, rows, cells = pressure.shape
     exports = ids.shape[0]
     return pl.pallas_call(
@@ -189,32 +192,34 @@
             jax.ShapeDtypeStruct(walls.shape, jnp.int32),
             jax.ShapeDtypeStruct((blocks - exports, rows, cells), BF16),
         ),
-        in_specs=[spec(SMEM), spec(VMEM), spec(VMEM), spec(SMEM), spec(VMEM), spec(VMEM), spec(pl.ANY)],
+        in_specs=[spec(SMEM), spec(VMEM), spec(VMEM), spec(SMEM), spec(VMEM), spec(pl.ANY)],
         out_specs=(spec(SMEM), spec(VMEM), spec(SMEM), spec(VMEM)),
         scratch_shapes=[SMEM((blocks,), jnp.int32), SMEM((blocks,), jnp.int32)],
         compiler_params=params(8),
-        cost_estimate=cost(0, 5000000),
+        cost_estimate=cost(2.1),
         name="prepare",
-    )(ids, turn, offset, walls, pressure, tiles, after)
-
-
-def respond_kernel(mats, pole, res, direct, states, area, after, *outs):
+    )(ids, turn, offset, walls, pressure, after)
+
+
+def respond_kernel(power, table, states, area, after, *outs):
     del after
-    rows = states.shape[2]
-    cap = mats.shape[0]
+    slots, orders, rows, _ = states.shape
+    cap = outs[0].shape[0] // 2
+    materials = (table.shape[0] - slots) // (2 * orders + 1)
     y, x = position()
     for t, turn in enumerate(TURNS):
         for cross in range(2):
             for c in range(cap):
                 device = gx_of(y, x, turn, cross)
                 slot, to, out = device * cap + c, cross * cap + c, outs[t]
-                m = mats[c, device]
-                p1, p2 = pole[0, m], pole[1, m]
-                r1, r2, y0 = res[0, m], res[1, m], direct[m]
+                m = table[(2 * orders + 1) * materials + c * (slots // cap) + device].astype(jnp.int32)
+                p1, p2, r1, r2, y0 = [table[n * materials + m] for n in range(2 * orders + 1)]
                 wall = area[slot]
                 first, second = p1 * states[slot, 0], p2 * states[slot, 1]
+                if power == 2:
+                    out[to] = (wall * (p1 * first + p2 * second)).astype(BF16)
+                    continue
                 out[to, 0:rows, :] = (wall * (first + second)).astype(BF16)
-                out[to, rows : 2 * rows, :] = (wall * (p1 * first + p2 * second)).astype(BF16)
                 ones = jnp.ones_like(wall)
                 coefs = (
                     wall * (y0 + (r1 + r2)),
@@ -227,21 +232,21 @@
                 high = [v.astype(BF16).astype(F32) for v in coefs]
                 low = [v - h for v, h in zip(coefs, high)]
                 pad = [jnp.zeros_like(wall)] * (COEF_ROWS - 2 * len(coefs))
-                out[to, 2 * rows :, :] = jnp.concatenate(high + low + pad, axis=0).astype(BF16)
-
-
-def responses(mats, pole, res, direct, states, area, after):
+                out[to, rows:, :] = jnp.concatenate(high + low + pad, axis=0).astype(BF16)
+
+
+def responses(power, table, states, area, cap, after):
     _, _, rows, cells = states.shape
-    cap = mats.shape[0]
-    return pl.pallas_call(
-        respond_kernel,
-        out_shape=[jax.ShapeDtypeStruct((2 * cap, 2 * rows + COEF_ROWS, cells), BF16)] * len(TURNS),
-        in_specs=[spec(SMEM)] * 4 + [spec(VMEM)] * 2 + [spec(pl.ANY)],
+    height = rows + (COEF_ROWS if power == 1 else 0)
+    return pl.pallas_call(
+        functools.partial(respond_kernel, power),
+        out_shape=[jax.ShapeDtypeStruct((2 * cap, height, cells), BF16)] * len(TURNS),
+        in_specs=[spec(SMEM), spec(VMEM), spec(VMEM), spec(pl.ANY)],
         out_specs=[spec(VMEM)] * len(TURNS),
         compiler_params=params(8),
-        cost_estimate=cost(0, 3000000),
-        name="responses",
-    )(mats, pole, res, direct, states, area, after)
+        cost_estimate=cost(1),
+        name=f"responses_{power}",
+    )(table, states, area, after)
 
 
 def coef_row(message, name):
@@ -258,6 +263,7 @@
 
 def base_kernel(step, wall_at, order, pressure, *refs):
     message, refs = refs[: len(TURNS) + 1], refs[len(TURNS) + 1 :]
+    later, refs = (message, refs) if step == 1 else (refs[: len(TURNS) + 1], refs[len(TURNS) + 1 :])
     pairs = [refs[2 * i : 2 * i + 2] for i in range(len(refs) // 2)]
     base = refs[-1]
     fields, rounded = pairs[: step - 1], pairs[step - 1 : 2 * step - 1]
@@ -277,7 +283,8 @@
     start(0, exports, 0)
     start(1, others, exports)
 
-    for _, _, c, device, slot in arrivals(message, wall_at.shape[0]):
+    cap = wall_at.shape[0]
+    for (_, _, c, device, slot), (*_, next_slot) in zip(arrivals(message, cap), arrivals(later, cap)):
         at = wall_at[c, device]
 
         @pl.when(at >= 0)
@@ -291,7 +298,7 @@
             if step == 1:
                 flux = flux + first
             else:
-                second = slot[rows : 2 * rows, :].astype(F32)
+                second = next_slot[...].astype(F32)
                 if step == 2:
                     flux = flux + second
                 else:
@@ -300,23 +307,22 @@
             base[at] = base[at] - 0.5 * flux
 
 
-def base_of(step, wall_at, order, message, pressure, fields, rounded):
-    arrays = list(message) + [a for pair in list(fields) + list(rounded) for a in pair]
+def base_of(step, wall_at, order, messages, pressure, fields, rounded):
+    arrays = [a for arrived in messages for a in arrived] + [a for pair in list(fields) + list(rounded) for a in pair]
     return pl.pallas_call(
         functools.partial(base_kernel, step),
         out_shape=jax.ShapeDtypeStruct(pressure.shape, F32),
         in_specs=[spec(SMEM)] * 2 + [spec(pl.ANY if step == 3 else VMEM)] + [spec(VMEM)] * len(arrays),
         out_specs=spec(VMEM),
         compiler_params=params(8),
-        cost_estimate=cost(0, 9000000),
+        cost_estimate=cost(1.6 if step == 1 else 0),
         name=f"base_{step}",
     )(wall_at, order, pressure, *arrays)
 
 
-def wall_kernel(wall_at, after, *refs):
-    del after
+def wall_kernel(wall_at, *refs):
     message, refs = refs[: len(TURNS) + 1], refs[len(TURNS) + 1 :]
-    rounded, outs = [refs[2 * i : 2 * i + 2] for i in range(3)], refs[6:]
+    rounded, outs = [refs[2 * i : 2 * i + 2] for i in range(3)], refs[-len(TURNS) :]
     rows = rounded[0][0].shape[1]
     cap = wall_at.shape[0]
 
@@ -343,25 +349,31 @@
     return pl.pallas_call(
         wall_kernel,
         out_shape=[jax.ShapeDtypeStruct((2 * cap, 2 * rows, cells), BF16)] * len(TURNS),
-        in_specs=[spec(SMEM), spec(pl.ANY)] + [spec(VMEM)] * len(arrays),
+        in_specs=[spec(SMEM)] + [spec(VMEM)] * len(arrays) + [spec(pl.ANY)] * len(after),
         out_specs=[spec(VMEM)] * len(TURNS),
         compiler_params=params(8),
-        cost_estimate=cost(0, 4000000),
+        cost_estimate=cost(0),
         name="walls",
-    )(wall_at, after, *arrays)
+    )(wall_at, *arrays, *after)
 
 
 def states_kernel(mats, pole, res, states, *refs):
-    walls, out = refs[:-1], refs[-1]
+    walls, (out, fresh, sems) = refs[:-3], refs[-3:]
     rows = states.shape[2]
     cap = mats.shape[0]
+    copies = []
     for _, _, c, device, slot in arrivals(walls, cap):
         m, e = mats[c, device], device * cap + c
         p1, p2 = pole[0, m], pole[1, m]
         second = slot[rows:, :].astype(F32)
         first = second + (p1 - p2) * slot[0:rows, :].astype(F32)
-        out[e, 0] = (p1 * p1 * p1) * states[e, 0] + res[0, m] * first
-        out[e, 1] = (p2 * p2 * p2) * states[e, 1] + res[1, m] * second
+        n = len(copies)
+        fresh[n, 0] = (p1 * p1 * p1) * states[e, 0] + res[0, m] * first
+        fresh[n, 1] = (p2 * p2 * p2) * states[e, 1] + res[1, m] * second
+        copies.append(pltpu.make_async_copy(fresh.at[n], out.at[e], sems.at[n]))
+        copies[-1].start()
+    for copy in copies:
+        copy.wait()
 
 
 def states_after(mats, pole, res, states, walls):
@@ -369,9 +381,10 @@
         states_kernel,
         out_shape=jax.ShapeDtypeStruct(states.shape, F32),
         in_specs=[spec(SMEM)] * 3 + [spec(VMEM)] * (1 + len(walls)),
-        out_specs=spec(VMEM),
-        compiler_params=params(8),
-        cost_estimate=cost(0, 5000000),
+        out_specs=spec(pltpu.HBM),
+        scratch_shapes=[VMEM(states.shape, F32), DMA(states.shape[:1])],
+        compiler_params=params(8),
+        cost_estimate=cost(0),
         name="states_after",
     )(mats, pole, res, states, *walls)
 
@@ -384,29 +397,14 @@
 
 
 def fill_pool(parts, pool, sems):
-    *parts, beside, seamed = parts
     copies, at = [], 0
     for i, part in enumerate(parts):
         copies.append(pltpu.make_async_copy(part, pool.at[pl.ds(at, part.shape[0])], sems.at[i]))
         at += part.shape[0]
     for copy in copies:
         copy.start()
-    seam = lax.axis_size("gy") // 2
-    place = lax.axis_index("gy")
-    at_seam = (place == seam - 1) | (place == seam)
-    target = pool.at[pl.ds(at, beside.shape[0])]
-
-    @pl.when(at_seam)
-    def _():
-        pltpu.make_async_copy(seamed, target, sems.at[len(parts)]).start()
-
-    @pl.when(jnp.logical_not(at_seam))
-    def _():
-        pltpu.make_async_copy(beside, target, sems.at[len(parts)]).start()
-
     for copy in copies:
         copy.wait()
-    pltpu.make_async_copy(beside, target, sems.at[len(parts)]).wait()
 
 
 def first_kernel(order, index, tiles, base, *refs):
@@ -428,18 +426,19 @@
         out_shape=(
             jax.ShapeDtypeStruct((exports, rows, cells), F32),
             jax.ShapeDtypeStruct((exports, rows, cells), BF16),
-            jax.ShapeDtypeStruct((sum(p.shape[0] for p in pool[:-1]), rows, cells), BF16),
+            jax.ShapeDtypeStruct((sum(p.shape[0] for p in pool), rows, cells), BF16),
         ),
         in_specs=[spec(SMEM)] * 2 + [spec(VMEM)] * 2 + [spec(pl.ANY)] * len(pool),
         out_specs=(spec(VMEM),) * 3,
-        scratch_shapes=[DMA((len(pool) - 1,))],
-        compiler_params=params(8),
-        cost_estimate=cost(exports * 50331648, 10000000),
+        scratch_shapes=[DMA((len(pool),))],
+        compiler_params=params(8),
+        cost_estimate=cost(3.1),
         name=name,
     )(order, index, tiles, base, *pool)
 
 
-def other_kernel(order, index, tiles, base, pool, field, others):
+def other_kernel(order, index, tiles, base, pool, after, field, others):
+    del after
     count = others.shape[0]
     exports = order.shape[0] - count
 
@@ -450,7 +449,7 @@
         others[i] = value.astype(BF16)
 
 
-def other_blocks(order, index, tiles, base, pool, count, name):
+def other_blocks(order, index, tiles, base, pool, count, after, name):
     rows, cells = base.shape[1:]
     return pl.pallas_call(
         other_kernel,
@@ -458,12 +457,12 @@
             jax.ShapeDtypeStruct((count, rows, cells), F32),
             jax.ShapeDtypeStruct((count, rows, cells), BF16),
         ),
-        in_specs=[spec(SMEM)] * 2 + [spec(VMEM)] * 3,
+        in_specs=[spec(SMEM)] * 2 + [spec(VMEM)] * 3 + [spec(pl.ANY)],
         out_specs=(spec(VMEM),) * 2,
         compiler_params=params(8),
-        cost_estimate=cost(count * 50331648, 15000000),
+        cost_estimate=cost(0),
         name=name,
-    )(order, index, tiles, base, pool)
+    )(order, index, tiles, base, pool, after)
 
 
 def last_kernel(order, index, tiles, base, *refs):
@@ -492,13 +491,13 @@
         in_specs=[spec(SMEM)] * 2 + [spec(VMEM)] * 2 + [spec(pl.ANY)] * len(pool),
         out_specs=spec(pltpu.HBM),
         scratch_shapes=[
-            VMEM((sum(p.shape[0] for p in pool[:-1]), rows, cells), BF16),
+            VMEM((sum(p.shape[0] for p in pool), rows, cells), BF16),
             VMEM((blocks, rows, cells), F32),
-            DMA((len(pool) - 1,)),
+            DMA((len(pool),)),
             DMA((blocks,)),
         ],
         compiler_params=params(10),
-        cost_estimate=cost(blocks * 50331648, 25000000),
+        cost_estimate=cost(0),
         name="last",
     )(order, index, tiles, base, *pool)
 
@@ -513,35 +512,41 @@
     slots = owners * cap
 
     e1 = exports_of(export_ids, pressure)
-    around = around_of(e1)
 
     tiles = couplings.reshape(blocks, neigh * cells, cells)
     mats = bnd_mat.reshape(owners, cap).T
-    pole, res = mat_pole.T, mat_res.T
+    owned = (mats, mat_pole.T, mat_res.T)
     held = states.reshape((slots,) + states.shape[4:])
-    message = responses(mats, pole, res, mat_y0, held, area.reshape(slots, 1, cells), around[2])
-    message = over_gx(message, (around[0], around[3]))
+    table = [t.reshape(-1) for t in (mat_pole.T, mat_res.T, mat_y0, mats.astype(F32))]
+    walled = (jnp.concatenate(table), held, area.reshape(slots, 1, cells), cap)
+
+    across, core, beside = beside_of(e1)
+    message, across = over_x(over_y(responses(1, *walled, core)), (across,))
+    around = (across, passed_on(across), core, beside)
     order, index, wall_at, o1 = prepare(
-        export_ids, nbr_dir.T, nbr_idx.T, bnd_blk.reshape(owners, cap).T, pressure, tiles, around[3]
+        export_ids, nbr_dir.T, nbr_idx.T, bnd_blk.reshape(owners, cap).T, pressure, across
     )
-
-    base = base_of(1, wall_at, order, message, pressure, (), ((e1, o1),))
+    base = base_of(1, wall_at, order, (message,), pressure, (), ((e1, o1),))
     p1_first, e2, pool = first_blocks(order, index, tiles, base, (e1, o1) + around, "exports_1")
-    around = around_of(e2)
-    p1_other, o2 = other_blocks(order, index, tiles, base, pool, blocks - exports, "others_1")
+
+    across, core, beside = beside_of(e2)
+    later, across = over_x(over_y(responses(2, *walled, core)), (across,))
+    around = (across, passed_on(across), core, beside)
+    p1_other, o2 = other_blocks(order, index, tiles, base, pool, blocks - exports, across, "others_1")
     p1 = (p1_first, p1_other)
-
-    base = base_of(2, wall_at, order, message, pressure, (p1,), ((e2, o2), (e1, o1)))
+    base = base_of(2, wall_at, order, (message, later), pressure, (p1,), ((e2, o2), (e1, o1)))
     p2_first, e3, pool = first_blocks(order, index, tiles, base, (e2, o2) + around, "exports_2")
-    around = around_of(e3)
-    p2_other, o3 = other_blocks(order, index, tiles, base, pool, blocks - exports, "others_2")
+
+    across, core, beside = beside_of(e3)
+    around = (across, passed_on(across), core, beside)
+    p2_other, o3 = other_blocks(order, index, tiles, base, pool, blocks - exports, core, "others_2")
     p2 = (p2_first, p2_other)
-
     rounded = ((e3, o3), (e2, o2), (e1, o1))
-    walls = over_gx(walls_of(wall_at, message, rounded, around[2]), (around[0],))
-    base = base_of(3, wall_at, order, message, pressure, (p2, p1), rounded)
+    walls = over_y(walls_of(wall_at, message, rounded, (core,)))
+    (walls,) = over_x(walls, (), (across,))
+    base = base_of(3, wall_at, order, (message, later), pressure, (p2, p1), rounded)
     p3 = last_blocks(order, index, tiles, base, (e3, o3) + around)
-    held = states_after(mats, pole, res, held, walls)
+    held = states_after(*owned, held, walls)
     return p3, held.reshape(states.shape)
 
 

time: 125 us -> 116 us (0.928); the launches traced: 124 us -> 114 us
  waiting for transfers between devices: 49.8 us -> 35.6 us
  starting transfers between devices: 32 us -> 37.4 us
  local copies, waits for them, and re-layouts: 5.55 us -> 1.9 us
  Pallas kernels: 35.7 us -> 37.8 us
    ppermute x6 -> x3, waiting for transfers between devices: 17.9 us -> 10.8 us  [passed_on(): return lax.ppermute(across, 'gx', on)]
    ppermute x6 -> x9, waiting for transfers between devices: 12 us -> 6.08 us  [along_y(): lax.ppermute(value, 'gx', [(i, (i + 2 * steps) % count) for i in range(co...]
    unnamed x34 -> x28, local copies, waits for them, and re-layouts: 5.55 us -> 1.65 us
    ppermute x6 -> x9, starting transfers between devices: 8.1 us -> 12 us  [along_y(): lax.ppermute(value, 'gx', [(i, (i + 2 * steps) % count) for i in range(co...]
    ppermute x5 -> x6, starting transfers between devices: 7.02 us -> 10.6 us  [other_x(): return lax.ppermute(value, 'gx', [(i, i ^ 1) for i in range(count)])]
    ppermute x5 -> x6, waiting for transfers between devices: 19.9 us -> 17.8 us  [other_x(): return lax.ppermute(value, 'gx', [(i, i ^ 1) for i in range(count)])]
    ppermute x6, starting transfers between devices: 8 us -> 5.98 us  [along_gy(): return lax.ppermute(value, 'gy', pairs + [(j, i) for i, j in pairs])]
    pallas_call x3 -> x5, Pallas kernels: 2.44 us -> 3.09 us  [the longest x2 1.62 us: responses(): pl.pallas_call(functools.partial(respond_kernel, power), out_shape=[jax.S...]
  transfers between devices with their start and end apart: 23 -> 24, of which waited for: 11 -> 13; matrix products, arithmetic and copies ran while one was open for 0% -> 0% of each run, Pallas kernels for 19% -> 23%
where the time goes in v2:
time: 116 us; the launch traced here: 114 us
  Pallas kernels  37.8 us (33%)
  starting transfers between devices  37.4 us (32%)
  waiting for transfers between devices  35.6 us (31%)
  local copies, waits for them, and re-layouts  1.9 us (2%)
    ppermute x6, waiting for transfers between devices, other_x(): return lax.ppermute(value, 'gx', [(i, i ^ 1) for i in range(count)])  17.8 us
    ppermute x9, starting transfers between devices, along_y(): lax.ppermute(value, 'gx', [(i, (i + 2 * steps) % count) for i in range(co...  12 us
    ppermute x3, waiting for transfers between devices, passed_on(): return lax.ppermute(across, 'gx', on)  10.8 us
    ppermute x6, starting transfers between devices, other_x(): return lax.ppermute(value, 'gx', [(i, i ^ 1) for i in range(count)])  10.6 us
    ppermute x3, starting transfers between devices, passed_on(): return lax.ppermute(across, 'gx', on)  8.86 us
    pallas_call x2, Pallas kernels, other_blocks(): pl.pallas_call(other_kernel, out_shape=(jax.ShapeDtypeStruct((count, rows...  7.23 us
    pallas_call x1, Pallas kernels, last_blocks(): pl.pallas_call(last_kernel, out_shape=jax.ShapeDtypeStruct((blocks, rows,...  6.95 us
    pallas_call x2, Pallas kernels, first_blocks(): pl.pallas_call(first_kernel, out_shape=(jax.ShapeDtypeStruct((exports, ro...  6.92 us
  transfers between devices with their start and end apart: 24, of which 13 were waited for; matrix products, arithmetic and copies ran while one was open for 0% of the time, Pallas kernels for 23%

profile of v2, /device:TPU:40, one launch (start us, length us, event | category | flops | bytes accessed | tf_op | source)
XLA Modules:
  0.0 113.9 jit_solution(10163619034410653572)
XLA Ops:
  0.7 3.0 %exports.1.refs_5_.refs_0_.refs_14_.refs_18_.refs_9_ = bf16[16,128,128]{2,1,0:T(8,128)(2,1)} custom-call(s32[16]{0:T(128)} %ids.3, f32[40,128,128]{2,1,0:T(8,128)} %pressure.9), custom_call_target="tpu_custom_call" | custom-call | flops 3000000000 | tf_op jit(solution)/shard_map/exports/pallas_call | solution.py:133
  3.7 0.0 copy-start.2
  3.7 0.0 copy-start.1
  3.7 0.1 collective-permute-start
  3.8 1.6 %collective-permute-start.4 = (bf16[16,128,128]{2,1,0:T(8,128)(2,1)}, bf16[16,128,128]{2,1,0:T(8,128)(2,1)}, u32[]{:S(2)}, u32[]{:S(2)}) collective-permute-start(bf16[16,128,128]{2,1,0:T(8,128)(2,1)} %exports.1.refs_5_.refs_0_.refs_14_.refs_18_.refs_9_), channel_id=1, source_target_pairs={{0,16},{16,0},{32,48},{48,32},{64,80},{80,64},{96,112},{112,96},{1... | collective-permute-start | bytes 1572872 | tf_op jit(solution)/shard_map/ppermute | solution.py:38
  5.4 0.1 reshape.35
  5.5 0.1 reshape.33
  5.6 0.1 reshape.32
  5.7 0.1 pad_maximum_fusion.table
  5.7 0.3 collective-permute-done.after.refs_4_
  6.1 1.6 %copy-done.3 = f32[1,1,8,2,2,128,128]{6,5,4,3,2,1,0:T(8,128)S(1)} copy-done((f32[1,1,8,2,2,128,128]{6,5,4,3,2,1,0:T(8,128)S(1)}, f32[1,1,8,2,2,128,128]{6,5,4,3,2,1,0:T(8,128)}, u32[]{:S(2)}) %copy-start.3) | copy-done | bytes 2097176
  7.7 0.8 responses_1.1
  8.5 1.6 %collective-permute-start.1 = (bf16[4,144,128]{2,1,0:T(8,128)(2,1)S(1)}, bf16[4,144,128]{2,1,0:T(8,128)(2,1)S(1)}, u32[]{:S(2)}, u32[]{:S(2)}) collective-permute-start(bf16[4,144,128]{2,1,0:T(8,128)(2,1)S(1)} %get-tuple-element.33), channel_id=1, source_target_pairs={{0,32},{16,48},{32,64},{48,80},{64,96},{80,112},{96,0},{112,16},{1... | collective-permute-start | bytes 442376 | tf_op jit(solution)/shard_map/ppermute | solution.py:43
  10.1 0.5 collective-permute-start.2
  10.6 2.3 %collective-permute-start.3 = (bf16[4,144,128]{2,1,0:T(8,128)(2,1)S(1)}, bf16[4,144,128]{2,1,0:T(8,128)(2,1)S(1)}, u32[]{:S(2)}, u32[]{:S(2)}) collective-permute-start(bf16[4,144,128]{2,1,0:T(8,128)(2,1)S(1)} %get-tuple-element.35), channel_id=1, source_target_pairs={{0,64},{16,80},{32,96},{48,112},{64,0},{80,16},{96,32},{112,48},{1... | collective-permute-start | bytes 442376 | tf_op jit(solution)/shard_map/ppermute | solution.py:43
  12.9 1.9 %collective-permute-start.7 = (bf16[16,128,128]{2,1,0:T(8,128)(2,1)S(1)}, bf16[16,128,128]{2,1,0:T(8,128)(2,1)S(1)}, u32[]{:S(2)}, u32[]{:S(2)}) collective-permute-start(bf16[16,128,128]{2,1,0:T(8,128)(2,1)S(1)} %copy-done.2), channel_id=1, source_target_pairs={{1,2},{3,4},{5,6},{7,8},{9,10},{11,12},{13,14},{2,1},{4,3},{6,5},{... | collective-permute-start | bytes 1572872 | tf_op jit(solution)/shard_map/ppermute | solution.py:48
  14.8 3.7 %collective-permute-done.4.refs_4_ = bf16[16,128,128]{2,1,0:T(8,128)(2,1)} collective-permute-done((bf16[16,128,128]{2,1,0:T(8,128)(2,1)}, bf16[16,128,128]{2,1,0:T(8,128)(2,1)}, u32[]{:S(2)}, u32[]{:S(2)}) %collective-permute-start.4) | collective-permute-done | bytes 524320 | tf_op jit(solution)/shard_map/ppermute | solution.py:38
  18.5 0.0 collective-permute-done.2.refs_2_
  18.5 1.1 collective-permute-done.3.refs_3_
  19.6 0.4 turned.3
  20.0 2.8 %collective-permute-start.6 = (bf16[16,128,128]{2,1,0:T(8,128)(2,1)}, bf16[16,128,128]{2,1,0:T(8,128)(2,1)S(1)}, u32[]{:S(2)}, u32[]{:S(2)}) collective-permute-start(bf16[16,128,128]{2,1,0:T(8,128)(2,1)} %get-tuple-element.36.after.refs_2_), channel_id=1, source_target_pairs={{48,16},{80,48},{112,80},{0,32},{32,64},{64,96},{49,17},{81,49},{1... | collective-permute-start | bytes 1572872 | tf_op jit(solution)/shard_map/ppermute | solution.py:54
  22.8 2.0 %collective-permute-start.5 = (bf16[8,144,128]{2,1,0:T(8,128)(2,1)S(1)}, bf16[8,144,128]{2,1,0:T(8,128)(2,1)S(1)}, u32[]{:S(2)}, u32[]{:S(2)}) collective-permute-start(bf16[8,144,128]{2,1,0:T(8,128)(2,1)S(1)} %get-tuple-element.40), channel_id=1, source_target_pairs={{0,16},{16,0},{32,48},{48,32},{64,80},{80,64},{96,112},{112,96},{1... | collective-permute-start | bytes 884744 | tf_op jit(solution)/shard_map/ppermute | solution.py:38
  24.8 2.1 %prepare.1 = (s32[40]{0:T(128)S(1)}, s32[12,40]{1,0:T(8,128)S(1)}, s32[2,8]{1,0:T(2,128)S(1)}, bf16[24,128,128]{2,1,0:T(8,128)(2,1)S(1)}) custom-call(s32[16]{0:T(128)S(1)} %copy-done.12, s32[12,40]{1,0:T(8,128)S(1)} %bitcast.28, s32[12,40]{1,0:T(8,128)S(1)} %bitcast.29, s32[2,8]{1,0:T(2,128)S(1)} %bitcast.32, f32[40,128,128]{2,1,0:T(8,128)S(1)} %copy-done.1, ...), custom_call_target="tpu_custom_call" | custom-call | flops 2100000000 | tf_op jit(solution)/shard_map/prepare/pallas_call | solution.py:187
  27.0 4.2 %collective-permute-done.5.refs_4_ = bf16[8,144,128]{2,1,0:T(8,128)(2,1)S(1)} collective-permute-done((bf16[8,144,128]{2,1,0:T(8,128)(2,1)S(1)}, bf16[8,144,128]{2,1,0:T(8,128)(2,1)S(1)}, u32[]{:S(2)}, u32[]{:S(2)}) %collective-permute-start.5) | collective-permute-done | bytes 294944 | tf_op jit(solution)/shard_map/ppermute | solution.py:38
  31.2 1.4 %base_1.1.base = f32[40,128,128]{2,1,0:T(8,128)S(1)} custom-call(s32[2,8]{1,0:T(2,128)S(1)} %get-tuple-element.39.wall_at, s32[40]{0:T(128)S(1)} %get-tuple-element.37.order, f32[40,128,128]{2,1,0:T(8,128)S(1)} %copy-done.1, bf16[4,144,128]{2,1,0:T(8,128)(2,1)S(1)} %get-tuple-element.32.refs_0_, bf16[4,144,128]{2,1,0:T(8,128)(2,1)S(1)} %collective-permute-done.1.refs_1_, ...), custom_call_target="tpu_custom_call" | custom-call | flops 1600000000 | tf_op jit(solution)/shard_map/base_1/pallas_call | solution.py:312
  32.6 2.8 %collective-permute-done.6.refs_3_ = bf16[16,128,128]{2,1,0:T(8,128)(2,1)S(1)} collective-permute-done((bf16[16,128,128]{2,1,0:T(8,128)(2,1)}, bf16[16,128,128]{2,1,0:T(8,128)(2,1)S(1)}, u32[]{:S(2)}, u32[]{:S(2)}) %collective-permute-start.6) | collective-permute-done | bytes 524320 | tf_op jit(solution)/shard_map/ppermute | solution.py:54
  35.3 4.0 %exports_1.1 = (f32[16,128,128]{2,1,0:T(8,128)S(1)}, bf16[16,128,128]{2,1,0:T(8,128)(2,1)S(1)}, bf16[104,128,128]{2,1,0:T(8,128)(2,1)S(1)}) custom-call(s32[40]{0:T(128)S(1)} %get-tuple-element.37.order, s32[12,40]{1,0:T(8,128)S(1)} %get-tuple-element.38.index, bf16[40,1536,128]{2,1,0:T(8,128)(2,1)S(1)} %bitcast.15, f32[40,128,128]{2,1,0:T(8,128)S(1)} %base_1.1.base, ...), custom_call_target="tpu_custom_call" | custom-call | flops 3100000000 | tf_op jit(solution)/shard_map/exports_1/pallas_call | solution.py:424
  39.3 0.1 collective-permute-start.8
  39.4 1.6 %collective-permute-start.12 = (bf16[16,128,128]{2,1,0:T(8,128)(2,1)S(1)}, bf16[16,128,128]{2,1,0:T(8,128)(2,1)S(1)}, u32[]{:S(2)}, u32[]{:S(2)}) collective-permute-start(bf16[16,128,128]{2,1,0:T(8,128)(2,1)S(1)} %get-tuple-element.42.refs_12_.refs_0_.refs_16_.refs_7_), channel_id=1, source_target_pairs={{0,16},{16,0},{32,48},{48,32},{64,80},{80,64},{96,112},{112,96},{1... | collective-permute-start | bytes 1572872 | tf_op jit(solution)/shard_map/ppermute | solution.py:38
  41.0 0.3 collective-permute-done.8.after.refs_4_
  41.3 0.8 responses_2.1
  42.1 1.2 %collective-permute-start.9 = (bf16[4,128,128]{2,1,0:T(8,128)(2,1)S(1)}, bf16[4,128,128]{2,1,0:T(8,128)(2,1)S(1)}, u32[]{:S(2)}, u32[]{:S(2)}) collective-permute-start(bf16[4,128,128]{2,1,0:T(8,128)(2,1)S(1)} %get-tuple-element.44), channel_id=1, source_target_pairs={{0,32},{16,48},{32,64},{48,80},{64,96},{80,112},{96,0},{112,16},{1... | collective-permute-start | bytes 393224 | tf_op jit(solution)/shard_map/ppermute | solution.py:43
  43.3 0.9 collective-permute-start.10
  44.2 1.9 %collective-permute-start.11 = (bf16[4,128,128]{2,1,0:T(8,128)(2,1)S(1)}, bf16[4,128,128]{2,1,0:T(8,128)(2,1)S(1)}, u32[]{:S(2)}, u32[]{:S(2)}) collective-permute-start(bf16[4,128,128]{2,1,0:T(8,128)(2,1)S(1)} %get-tuple-element.46), channel_id=1, source_target_pairs={{0,64},{16,80},{32,96},{48,112},{64,0},{80,16},{96,32},{112,48},{1... | collective-permute-start | bytes 393224 | tf_op jit(solution)/shard_map/ppermute | solution.py:43
  46.1 1.9 %collective-permute-start.15 = (bf16[16,128,128]{2,1,0:T(8,128)(2,1)S(1)}, bf16[16,128,128]{2,1,0:T(8,128)(2,1)S(1)}, u32[]{:S(2)}, u32[]{:S(2)}) collective-permute-start(bf16[16,128,128]{2,1,0:T(8,128)(2,1)S(1)} %get-tuple-element.42.refs_12_.refs_0_.refs_16_.refs_7_), channel_id=1, source_target_pairs={{1,2},{3,4},{5,6},{7,8},{9,10},{11,12},{13,14},{2,1},{4,3},{6,5},{... | collective-permute-start | bytes 1572872 | tf_op jit(solution)/shard_map/ppermute | solution.py:48
  48.0 5.8 %collective-permute-done.12.refs_4_ = bf16[16,128,128]{2,1,0:T(8,128)(2,1)S(1)} collective-permute-done((bf16[16,128,128]{2,1,0:T(8,128)(2,1)S(1)}, bf16[16,128,128]{2,1,0:T(8,128)(2,1)S(1)}, u32[]{:S(2)}, u32[]{:S(2)}) %collective-permute-start.12) | collective-permute-done | bytes 524320 | tf_op jit(solution)/shard_map/ppermute | solution.py:38
  53.8 0.4 turned.4
  54.2 3.0 %collective-permute-start.14 = (bf16[16,128,128]{2,1,0:T(8,128)(2,1)S(1)}, bf16[16,128,128]{2,1,0:T(8,128)(2,1)S(1)}, u32[]{:S(2)}, u32[]{:S(2)}) collective-permute-start(bf16[16,128,128]{2,1,0:T(8,128)(2,1)S(1)} %get-tuple-element.50.after.refs_2_), channel_id=1, source_target_pairs={{48,16},{80,48},{112,80},{0,32},{32,64},{64,96},{49,17},{81,49},{1... | collective-permute-start | bytes 1572872 | tf_op jit(solution)/shard_map/ppermute | solution.py:54
  57.2 1.6 %collective-permute-start.13 = (bf16[8,128,128]{2,1,0:T(8,128)(2,1)S(1)}, bf16[8,128,128]{2,1,0:T(8,128)(2,1)S(1)}, u32[]{:S(2)}, u32[]{:S(2)}) collective-permute-start(bf16[8,128,128]{2,1,0:T(8,128)(2,1)S(1)} %get-tuple-element.47), channel_id=1, source_target_pairs={{0,16},{16,0},{32,48},{48,32},{64,80},{80,64},{96,112},{112,96},{1... | collective-permute-start | bytes 786440 | tf_op jit(solution)/shard_map/ppermute | solution.py:38
  58.9 3.6 %others_1.1 = (f32[24,128,128]{2,1,0:T(8,128)S(1)}, bf16[24,128,128]{2,1,0:T(8,128)(2,1)S(1)}) custom-call(s32[40]{0:T(128)S(1)} %get-tuple-element.37.order, s32[12,40]{1,0:T(8,128)S(1)} %get-tuple-element.38.index, bf16[40,1536,128]{2,1,0:T(8,128)(2,1)S(1)} %bitcast.16, f32[40,128,128]{2,1,0:T(8,128)S(1)} %base_1.1.base, ...), custom_call_target="tpu_custom_call" | custom-call | tf_op jit(solution)/shard_map/others_1/pallas_call | solution.py:454
  62.5 2.4 %collective-permute-done.13.refs_9_ = bf16[8,128,128]{2,1,0:T(8,128)(2,1)S(1)} collective-permute-done((bf16[8,128,128]{2,1,0:T(8,128)(2,1)S(1)}, bf16[8,128,128]{2,1,0:T(8,128)(2,1)S(1)}, u32[]{:S(2)}, u32[]{:S(2)}) %collective-permute-start.13) | collective-permute-done | bytes 262176 | tf_op jit(solution)/shard_map/ppermute | solution.py:38
  64.9 1.6 %base_2.1.base = f32[40,128,128]{2,1,0:T(8,128)S(1)} custom-call(s32[2,8]{1,0:T(2,128)S(1)} %get-tuple-element.39.wall_at, s32[40]{0:T(128)S(1)} %get-tuple-element.37.order, f32[40,128,128]{2,1,0:T(8,128)S(1)} %copy-done.1, bf16[4,144,128]{2,1,0:T(8,128)(2,1)S(1)} %get-tuple-element.32.refs_0_, bf16[4,144,128]{2,1,0:T(8,128)(2,1)S(1)} %collective-permute-done.1.refs_1_, ...), custom_call_target="tpu_custom_call" | custom-call | tf_op jit(solution)/shard_map/base_2/pallas_call | solution.py:312
  66.5 3.0 %collective-permute-done.14.refs_3_ = bf16[16,128,128]{2,1,0:T(8,128)(2,1)S(1)} collective-permute-done((bf16[16,128,128]{2,1,0:T(8,128)(2,1)S(1)}, bf16[16,128,128]{2,1,0:T(8,128)(2,1)S(1)}, u32[]{:S(2)}, u32[]{:S(2)}) %collective-permute-start.14) | collective-permute-done | bytes 524320 | tf_op jit(solution)/shard_map/ppermute | solution.py:54
  69.5 2.9 %exports_2.1 = (f32[16,128,128]{2,1,0:T(8,128)S(1)}, bf16[16,128,128]{2,1,0:T(8,128)(2,1)S(1)}, bf16[104,128,128]{2,1,0:T(8,128)(2,1)S(1)}) custom-call(s32[40]{0:T(128)S(1)} %get-tuple-element.37.order, s32[12,40]{1,0:T(8,128)S(1)} %get-tuple-element.38.index, bf16[40,1536,128]{2,1,0:T(8,128)(2,1)S(1)} %bitcast.17, f32[40,128,128]{2,1,0:T(8,128)S(1)} %base_2.1.base, ...), custom_call_target="tpu_custom_call" | custom-call | flops 3100000000 | tf_op jit(solution)/shard_map/exports_2/pallas_call | solution.py:424
  72.5 0.1 collective-permute-start.16
  72.6 1.6 %collective-permute-start.17 = (bf16[16,128,128]{2,1,0:T(8,128)(2,1)S(1)}, bf16[16,128,128]{2,1,0:T(8,128)(2,1)S(1)}, u32[]{:S(2)}, u32[]{:S(2)}) collective-permute-start(bf16[16,128,128]{2,1,0:T(8,128)(2,1)S(1)} %get-tuple-element.55.refs_14_.refs_0_.refs_5_), channel_id=1, source_target_pairs={{0,16},{16,0},{32,48},{48,32},{64,80},{80,64},{96,112},{112,96},{1... | collective-permute-start | bytes 1572872 | tf_op jit(solution)/shard_map/ppermute | solution.py:38
  74.1 0.3 collective-permute-done.16.after.refs_4_.refs_11_
  74.5 3.6 %others_2.1 = (f32[24,128,128]{2,1,0:T(8,128)S(1)}, bf16[24,128,128]{2,1,0:T(8,128)(2,1)S(1)}) custom-call(s32[40]{0:T(128)S(1)} %get-tuple-element.37.order, s32[12,40]{1,0:T(8,128)S(1)} %get-tuple-element.38.index, bf16[40,1536,128]{2,1,0:T(8,128)(2,1)S(1)} %bitcast.18, f32[40,128,128]{2,1,0:T(8,128)S(1)} %base_2.1.base, ...), custom_call_target="tpu_custom_call" | custom-call | tf_op jit(solution)/shard_map/others_2/pallas_call | solution.py:454
  78.1 1.6 %walls.1 = (bf16[4,256,128]{2,1,0:T(8,128)(2,1)S(1)}, bf16[4,256,128]{2,1,0:T(8,128)(2,1)S(1)}, bf16[4,256,128]{2,1,0:T(8,128)(2,1)S(1)}, bf16[4,256,128]{2,1,0:T(8,128)(2,1)S(1)}) custom-call(s32[2,8]{1,0:T(2,128)S(1)} %get-tuple-element.39.wall_at, bf16[4,144,128]{2,1,0:T(8,128)(2,1)S(1)} %get-tuple-element.32.refs_0_, ...), custom_call_target="tpu_custom_call" | custom-call | tf_op jit(solution)/shard_map/walls/pallas_call | solution.py:349
  79.7 1.2 %collective-permute-start.20 = (bf16[4,256,128]{2,1,0:T(8,128)(2,1)S(1)}, bf16[4,256,128]{2,1,0:T(8,128)(2,1)S(1)}, u32[]{:S(2)}, u32[]{:S(2)}) collective-permute-start(bf16[4,256,128]{2,1,0:T(8,128)(2,1)S(1)} %get-tuple-element.59), channel_id=1, source_target_pairs={{0,32},{16,48},{32,64},{48,80},{64,96},{80,112},{96,0},{112,16},{1... | collective-permute-start | bytes 786440 | tf_op jit(solution)/shard_map/ppermute | solution.py:43
  80.9 0.9 collective-permute-start.21
  81.7 1.6 %collective-permute-start.22 = (bf16[4,256,128]{2,1,0:T(8,128)(2,1)S(1)}, bf16[4,256,128]{2,1,0:T(8,128)(2,1)S(1)}, u32[]{:S(2)}, u32[]{:S(2)}) collective-permute-start(bf16[4,256,128]{2,1,0:T(8,128)(2,1)S(1)} %get-tuple-element.61), channel_id=1, source_target_pairs={{0,64},{16,80},{32,96},{48,112},{64,0},{80,16},{96,32},{112,48},{1... | collective-permute-start | bytes 786440 | tf_op jit(solution)/shard_map/ppermute | solution.py:43
  83.3 1.9 %collective-permute-start.19 = (bf16[16,128,128]{2,1,0:T(8,128)(2,1)S(1)}, bf16[16,128,128]{2,1,0:T(8,128)(2,1)S(1)}, u32[]{:S(2)}, u32[]{:S(2)}) collective-permute-start(bf16[16,128,128]{2,1,0:T(8,128)(2,1)S(1)} %get-tuple-element.55.refs_14_.refs_0_.refs_5_), channel_id=1, source_target_pairs={{1,2},{3,4},{5,6},{7,8},{9,10},{11,12},{13,14},{2,1},{4,3},{6,5},{... | collective-permute-start | bytes 1572872 | tf_op jit(solution)/shard_map/ppermute | solution.py:48
  85.2 1.7 %collective-permute-done.17.refs_2_.refs_4_ = bf16[16,128,128]{2,1,0:T(8,128)(2,1)S(1)} collective-permute-done((bf16[16,128,128]{2,1,0:T(8,128)(2,1)S(1)}, bf16[16,128,128]{2,1,0:T(8,128)(2,1)S(1)}, u32[]{:S(2)}, u32[]{:S(2)}) %collective-permute-start.17) | collective-permute-done | bytes 524320 | tf_op jit(solution)/shard_map/ppermute | solution.py:38
  86.9 3.0 %collective-permute-start.18 = (bf16[16,128,128]{2,1,0:T(8,128)(2,1)S(1)}, bf16[16,128,128]{2,1,0:T(8,128)(2,1)S(1)}, u32[]{:S(2)}, u32[]{:S(2)}) collective-permute-start(bf16[16,128,128]{2,1,0:T(8,128)(2,1)S(1)} %collective-permute-done.17.refs_2_.refs_4_), channel_id=1, source_target_pairs={{48,16},{80,48},{112,80},{0,32},{32,64},{64,96},{49,17},{81,49},{1... | collective-permute-start | bytes 1572872 | tf_op jit(solution)/shard_map/ppermute | solution.py:54
  89.9 0.0 collective-permute-done.20.refs_1_
  90.0 0.0 collective-permute-done.21.refs_2_
  90.0 4.9 %collective-permute-done.22.refs_3_ = bf16[4,256,128]{2,1,0:T(8,128)(2,1)S(1)} collective-permute-done((bf16[4,256,128]{2,1,0:T(8,128)(2,1)S(1)}, bf16[4,256,128]{2,1,0:T(8,128)(2,1)S(1)}, u32[]{:S(2)}, u32[]{:S(2)}) %collective-permute-start.22) | collective-permute-done | bytes 262176 | tf_op jit(solution)/shard_map/ppermute | solution.py:43
  94.9 0.7 turned.5
  95.6 2.2 %collective-permute-start.23 = (bf16[8,256,128]{2,1,0:T(8,128)(2,1)S(1)}, bf16[8,256,128]{2,1,0:T(8,128)(2,1)S(1)}, u32[]{:S(2)}, u32[]{:S(2)}) collective-permute-start(bf16[8,256,128]{2,1,0:T(8,128)(2,1)S(1)} %turned.5), channel_id=1, source_target_pairs={{0,16},{16,0},{32,48},{48,32},{64,80},{80,64},{96,112},{112,96},{1... | collective-permute-start | bytes 1572872 | tf_op jit(solution)/shard_map/ppermute | solution.py:38
  97.8 1.8 %base_3.1.base = f32[40,128,128]{2,1,0:T(8,128)S(1)} custom-call(s32[2,8]{1,0:T(2,128)S(1)} %get-tuple-element.39.wall_at, s32[40]{0:T(128)S(1)} %get-tuple-element.37.order, f32[40,128,128]{2,1,0:T(8,128)S(1)} %copy-done.1, bf16[4,144,128]{2,1,0:T(8,128)(2,1)S(1)} %get-tuple-element.32.refs_0_, bf16[4,144,128]{2,1,0:T(8,128)(2,1)S(1)} %collective-permute-done.1.refs_1_, ...), custom_call_target="tpu_custom_call" | custom-call | tf_op jit(solution)/shard_map/base_3/pallas_call | solution.py:312
  99.7 5.0 %collective-permute-done.18.refs_3_ = bf16[16,128,128]{2,1,0:T(8,128)(2,1)S(1)} collective-permute-done((bf16[16,128,128]{2,1,0:T(8,128)(2,1)S(1)}, bf16[16,128,128]{2,1,0:T(8,128)(2,1)S(1)}, u32[]{:S(2)}, u32[]{:S(2)}) %collective-permute-start.18) | collective-permute-done | bytes 524320 | tf_op jit(solution)/shard_map/ppermute | solution.py:54
  104.7 6.9 %last.1 = f32[40,128,128]{2,1,0:T(8,128)} custom-call(s32[40]{0:T(128)S(1)} %get-tuple-element.37.order, s32[12,40]{1,0:T(8,128)S(1)} %get-tuple-element.38.index, bf16[40,1536,128]{2,1,0:T(8,128)(2,1)S(1)} %bitcast.19, f32[40,128,128]{2,1,0:T(8,128)S(1)} %base_3.1.base, bf16[16,128,128]{2,1,0:T(8,128)(2,1)S(1)} %get-tuple-element.55.refs_14_.refs_0_.refs_5_, ...), custom_call_target="tpu_custom_call" | custom-call | tf_op jit(solution)/shard_map/last/pallas_call | solution.py:488
  111.6 2.1 %states_after.1 = f32[16,2,128,128]{3,2,1,0:T(8,128)} custom-call(s32[2,8]{1,0:T(2,128)S(1)} %bitcast.23, f32[2,16]{1,0:T(2,128)S(1)} %bitcast.27, f32[2,16]{1,0:T(2,128)S(1)} %bitcast.25, f32[16,2,128,128]{3,2,1,0:T(8,128)S(1)} %bitcast.22, bf16[4,256,128]{2,1,0:T(8,128)(2,1)S(1)} %get-tuple-element.58.refs_0_, ...), custom_call_target="tpu_custom_call" | custom-call | tf_op jit(solution)/shard_map/states_after/pallas_call | solution.py:380
  (34 shorter events, 0.1 us)
Async XLA Ops:
  0.6 4.8 %copy-start.5 = (s32[1,1,8,2]{2,3,1,0:T(2,128)S(1)}, s32[1,1,8,2]{2,3,1,0:T(2,128)}, u32[]{:S(2)}) copy-start(s32[1,1,8,2]{2,3,1,0:T(2,128)} %param.19) | copy-start | bytes 196
  0.6 4.8 %copy-start.6 = (f32[16,2]{0,1:T(2,128)S(1)}, f32[16,2]{0,1:T(2,128)}, u32[]{:S(2)}) copy-start(f32[16,2]{0,1:T(2,128)} %param.22) | copy-start | bytes 388
  0.7 4.9 %copy-start.7 = (f32[16,2]{0,1:T(2,128)S(1)}, f32[16,2]{0,1:T(2,128)}, u32[]{:S(2)}) copy-start(f32[16,2]{0,1:T(2,128)} %param.21) | copy-start | bytes 388
  0.7 5.0 %copy-start.13 = (f32[16]{0:T(128)S(1)}, f32[16]{0:T(128)}, u32[]{:S(2)}) copy-start(f32[16]{0:T(128)} %param.23) | copy-start | bytes 196
  0.7 5.4 %copy-start.10 = (f32[1,1,8,2,128]{4,3,2,1,0:T(2,128)S(1)}, f32[1,1,8,2,128]{4,3,2,1,0:T(2,128)}, u32[]{:S(2)}) copy-start(f32[1,1,8,2,128]{4,3,2,1,0:T(2,128)} %param.18) | copy-start | bytes 24580
  0.7 24.1 %copy-start.8 = (s32[40,12]{0,1:T(8,128)S(1)}, s32[40,12]{0,1:T(8,128)}, u32[]{:S(2)}) copy-start(s32[40,12]{0,1:T(8,128)} %param.14) | copy-start | bytes 5764
  0.7 24.1 %copy-start.9 = (s32[40,12]{0,1:T(8,128)S(1)}, s32[40,12]{0,1:T(8,128)}, u32[]{:S(2)}) copy-start(s32[40,12]{0,1:T(8,128)} %param.15) | copy-start | bytes 5764
  0.7 24.1 %copy-start.11 = (s32[1,1,8,2]{2,3,1,0:T(2,128)S(1)}, s32[1,1,8,2]{2,3,1,0:T(2,128)}, u32[]{:S(2)}) copy-start(s32[1,1,8,2]{2,3,1,0:T(2,128)} %param.17) | copy-start | bytes 196
  0.7 24.1 %copy-start.12 = (s32[16]{0:T(128)S(1)}, s32[16]{0:T(128)}, u32[]{:S(2)}) copy-start(s32[16]{0:T(128)} %ids.3) | copy-start | bytes 196
  3.7 9.2 %copy-start.2 = (bf16[16,128,128]{2,1,0:T(8,128)(2,1)S(1)}, bf16[16,128,128]{2,1,0:T(8,128)(2,1)}, u32[]{:S(2)}) copy-start(bf16[16,128,128]{2,1,0:T(8,128)(2,1)} %exports.1.refs_5_.refs_0_.refs_14_.refs_18_.refs_9_) | copy-start | bytes 1572868
  3.7 21.1 %copy-start.1 = (f32[40,128,128]{2,1,0:T(8,128)S(1)}, f32[40,128,128]{2,1,0:T(8,128)}, u32[]{:S(2)}) copy-start(f32[40,128,128]{2,1,0:T(8,128)} %pressure.9) | copy-start | bytes 7864324
  3.7 2.3 %collective-permute-start = (bf16[16,128,128]{2,1,0:T(8,128)(2,1)}, bf16[16,128,128]{2,1,0:T(8,128)(2,1)}, u32[]{:S(2)}, u32[]{:S(2)}) collective-permute-start(bf16[16,128,128]{2,1,0:T(8,128)(2,1)} %exports.1.refs_5_.refs_0_.refs_14_.refs_18_.refs_9_), channel_id=1, source_target_pairs={{0,1},{2,3},{4,5},{6,7},{8,9},{10,11},{12,13},{14,15},{1,0},{3,2},... | collective-permute-start | bytes 1572872 | tf_op jit(solution)/shard_map/ppermute | solution.py:48
  3.8 14.7 %collective-permute-start.4 = (bf16[16,128,128]{2,1,0:T(8,128)(2,1)}, bf16[16,128,128]{2,1,0:T(8,128)(2,1)}, u32[]{:S(2)}, u32[]{:S(2)}) collective-permute-start(bf16[16,128,128]{2,1,0:T(8,128)(2,1)} %exports.1.refs_5_.refs_0_.refs_14_.refs_18_.refs_9_), channel_id=1, source_target_pairs={{0,16},{16,0},{32,48},{48,32},{64,80},{80,64},{96,112},{112,96},{1... | collective-permute-start | bytes 1572872 | tf_op jit(solution)/shard_map/ppermute | solution.py:38
  6.1 1.6 %copy-start.3 = (f32[1,1,8,2,2,128,128]{6,5,4,3,2,1,0:T(8,128)S(1)}, f32[1,1,8,2,2,128,128]{6,5,4,3,2,1,0:T(8,128)}, u32[]{:S(2)}) copy-start(f32[1,1,8,2,2,128,128]{6,5,4,3,2,1,0:T(8,128)} %param.20) | copy-start | bytes 6291460
  8.5 10.0 %collective-permute-start.1 = (bf16[4,144,128]{2,1,0:T(8,128)(2,1)S(1)}, bf16[4,144,128]{2,1,0:T(8,128)(2,1)S(1)}, u32[]{:S(2)}, u32[]{:S(2)}) collective-permute-start(bf16[4,144,128]{2,1,0:T(8,128)(2,1)S(1)} %get-tuple-element.33), channel_id=1, source_target_pairs={{0,32},{16,48},{32,64},{48,80},{64,96},{80,112},{96,0},{112,16},{1... | collective-permute-start | bytes 442376 | tf_op jit(solution)/shard_map/ppermute | solution.py:43
  10.1 8.4 %collective-permute-start.2 = (bf16[4,144,128]{2,1,0:T(8,128)(2,1)S(1)}, bf16[4,144,128]{2,1,0:T(8,128)(2,1)S(1)}, u32[]{:S(2)}, u32[]{:S(2)}) collective-permute-start(bf16[4,144,128]{2,1,0:T(8,128)(2,1)S(1)} %get-tuple-element.34), channel_id=1, source_target_pairs={{0,96},{16,112},{32,0},{48,16},{64,32},{80,48},{96,64},{112,80},{1... | collective-permute-start | bytes 442376 | tf_op jit(solution)/shard_map/ppermute | solution.py:43
  10.6 9.0 %collective-permute-start.3 = (bf16[4,144,128]{2,1,0:T(8,128)(2,1)S(1)}, bf16[4,144,128]{2,1,0:T(8,128)(2,1)S(1)}, u32[]{:S(2)}, u32[]{:S(2)}) collective-permute-start(bf16[4,144,128]{2,1,0:T(8,128)(2,1)S(1)} %get-tuple-element.35), channel_id=1, source_target_pairs={{0,64},{16,80},{32,96},{48,112},{64,0},{80,16},{96,32},{112,48},{1... | collective-permute-start | bytes 442376 | tf_op jit(solution)/shard_map/ppermute | solution.py:43
  12.9 19.7 %collective-permute-start.7 = (bf16[16,128,128]{2,1,0:T(8,128)(2,1)S(1)}, bf16[16,128,128]{2,1,0:T(8,128)(2,1)S(1)}, u32[]{:S(2)}, u32[]{:S(2)}) collective-permute-start(bf16[16,128,128]{2,1,0:T(8,128)(2,1)S(1)} %copy-done.2), channel_id=1, source_target_pairs={{1,2},{3,4},{5,6},{7,8},{9,10},{11,12},{13,14},{2,1},{4,3},{6,5},{... | collective-permute-start | bytes 1572872 | tf_op jit(solution)/shard_map/ppermute | solution.py:48
  19.6 15.7 %copy-start = (bf16[40,12,128,128]{3,2,1,0:T(8,128)(2,1)S(1)}, bf16[40,12,128,128]{3,2,1,0:T(8,128)(2,1)}, u32[]{:S(2)}) copy-start(bf16[40,12,128,128]{3,2,1,0:T(8,128)(2,1)} %param.13) | copy-start | bytes 47185924
  20.0 15.3 %collective-permute-start.6 = (bf16[16,128,128]{2,1,0:T(8,128)(2,1)}, bf16[16,128,128]{2,1,0:T(8,128)(2,1)S(1)}, u32[]{:S(2)}, u32[]{:S(2)}) collective-permute-start(bf16[16,128,128]{2,1,0:T(8,128)(2,1)} %get-tuple-element.36.after.refs_2_), channel_id=1, source_target_pairs={{48,16},{80,48},{112,80},{0,32},{32,64},{64,96},{49,17},{81,49},{1... | collective-permute-start | bytes 1572872 | tf_op jit(solution)/shard_map/ppermute | solution.py:54
  22.8 8.4 %collective-permute-start.5 = (bf16[8,144,128]{2,1,0:T(8,128)(2,1)S(1)}, bf16[8,144,128]{2,1,0:T(8,128)(2,1)S(1)}, u32[]{:S(2)}, u32[]{:S(2)}) collective-permute-start(bf16[8,144,128]{2,1,0:T(8,128)(2,1)S(1)} %get-tuple-element.40), channel_id=1, source_target_pairs={{0,16},{16,0},{32,48},{48,32},{64,80},{80,64},{96,112},{112,96},{1... | collective-permute-start | bytes 884744 | tf_op jit(solution)/shard_map/ppermute | solution.py:38
  35.3 6.0 %copy-start.4 = (f32[1,1,8,2,2,128,128]{6,5,4,3,2,1,0:T(8,128)S(1)}, f32[1,1,8,2,2,128,128]{6,5,4,3,2,1,0:T(8,128)}, u32[]{:S(2)}) copy-start(f32[1,1,8,2,2,128,128]{6,5,4,3,2,1,0:T(8,128)} %param.20) | copy-start | bytes 6291460
  39.3 2.0 %collective-permute-start.8 = (bf16[16,128,128]{2,1,0:T(8,128)(2,1)S(1)}, bf16[16,128,128]{2,1,0:T(8,128)(2,1)S(1)}, u32[]{:S(2)}, u32[]{:S(2)}) collective-permute-start(bf16[16,128,128]{2,1,0:T(8,128)(2,1)S(1)} %get-tuple-element.42.refs_12_.refs_0_.refs_16_.refs_7_), channel_id=1, source_target_pairs={{0,1},{2,3},{4,5},{6,7},{8,9},{10,11},{12,13},{14,15},{1,0},{3,2},... | collective-permute-start | bytes 1572872 | tf_op jit(solution)/shard_map/ppermute | solution.py:48
  39.4 14.3 %collective-permute-start.12 = (bf16[16,128,128]{2,1,0:T(8,128)(2,1)S(1)}, bf16[16,128,128]{2,1,0:T(8,128)(2,1)S(1)}, u32[]{:S(2)}, u32[]{:S(2)}) collective-permute-start(bf16[16,128,128]{2,1,0:T(8,128)(2,1)S(1)} %get-tuple-element.42.refs_12_.refs_0_.refs_16_.refs_7_), channel_id=1, source_target_pairs={{0,16},{16,0},{32,48},{48,32},{64,80},{80,64},{96,112},{112,96},{1... | collective-permute-start | bytes 1572872 | tf_op jit(solution)/shard_map/ppermute | solution.py:38
  42.1 11.6 %collective-permute-start.9 = (bf16[4,128,128]{2,1,0:T(8,128)(2,1)S(1)}, bf16[4,128,128]{2,1,0:T(8,128)(2,1)S(1)}, u32[]{:S(2)}, u32[]{:S(2)}) collective-permute-start(bf16[4,128,128]{2,1,0:T(8,128)(2,1)S(1)} %get-tuple-element.44), channel_id=1, source_target_pairs={{0,32},{16,48},{32,64},{48,80},{64,96},{80,112},{96,0},{112,16},{1... | collective-permute-start | bytes 393224 | tf_op jit(solution)/shard_map/ppermute | solution.py:43
  43.3 10.4 %collective-permute-start.10 = (bf16[4,128,128]{2,1,0:T(8,128)(2,1)S(1)}, bf16[4,128,128]{2,1,0:T(8,128)(2,1)S(1)}, u32[]{:S(2)}, u32[]{:S(2)}) collective-permute-start(bf16[4,128,128]{2,1,0:T(8,128)(2,1)S(1)} %get-tuple-element.45), channel_id=1, source_target_pairs={{0,96},{16,112},{32,0},{48,16},{64,32},{80,48},{96,64},{112,80},{1... | collective-permute-start | bytes 393224 | tf_op jit(solution)/shard_map/ppermute | solution.py:43
  44.2 9.6 %collective-permute-start.11 = (bf16[4,128,128]{2,1,0:T(8,128)(2,1)S(1)}, bf16[4,128,128]{2,1,0:T(8,128)(2,1)S(1)}, u32[]{:S(2)}, u32[]{:S(2)}) collective-permute-start(bf16[4,128,128]{2,1,0:T(8,128)(2,1)S(1)} %get-tuple-element.46), channel_id=1, source_target_pairs={{0,64},{16,80},{32,96},{48,112},{64,0},{80,16},{96,32},{112,48},{1... | collective-permute-start | bytes 393224 | tf_op jit(solution)/shard_map/ppermute | solution.py:43
  46.1 20.4 %collective-permute-start.15 = (bf16[16,128,128]{2,1,0:T(8,128)(2,1)S(1)}, bf16[16,128,128]{2,1,0:T(8,128)(2,1)S(1)}, u32[]{:S(2)}, u32[]{:S(2)}) collective-permute-start(bf16[16,128,128]{2,1,0:T(8,128)(2,1)S(1)} %get-tuple-element.42.refs_12_.refs_0_.refs_16_.refs_7_), channel_id=1, source_target_pairs={{1,2},{3,4},{5,6},{7,8},{9,10},{11,12},{13,14},{2,1},{4,3},{6,5},{... | collective-permute-start | bytes 1572872 | tf_op jit(solution)/shard_map/ppermute | solution.py:48
  54.2 15.4 %collective-permute-start.14 = (bf16[16,128,128]{2,1,0:T(8,128)(2,1)S(1)}, bf16[16,128,128]{2,1,0:T(8,128)(2,1)S(1)}, u32[]{:S(2)}, u32[]{:S(2)}) collective-permute-start(bf16[16,128,128]{2,1,0:T(8,128)(2,1)S(1)} %get-tuple-element.50.after.refs_2_), channel_id=1, source_target_pairs={{48,16},{80,48},{112,80},{0,32},{32,64},{64,96},{49,17},{81,49},{1... | collective-permute-start | bytes 1572872 | tf_op jit(solution)/shard_map/ppermute | solution.py:54
  57.2 7.6 %collective-permute-start.13 = (bf16[8,128,128]{2,1,0:T(8,128)(2,1)S(1)}, bf16[8,128,128]{2,1,0:T(8,128)(2,1)S(1)}, u32[]{:S(2)}, u32[]{:S(2)}) collective-permute-start(bf16[8,128,128]{2,1,0:T(8,128)(2,1)S(1)} %get-tuple-element.47), channel_id=1, source_target_pairs={{0,16},{16,0},{32,48},{48,32},{64,80},{80,64},{96,112},{112,96},{1... | collective-permute-start | bytes 786440 | tf_op jit(solution)/shard_map/ppermute | solution.py:38
  72.5 2.0 %collective-permute-start.16 = (bf16[16,128,128]{2,1,0:T(8,128)(2,1)S(1)}, bf16[16,128,128]{2,1,0:T(8,128)(2,1)S(1)}, u32[]{:S(2)}, u32[]{:S(2)}) collective-permute-start(bf16[16,128,128]{2,1,0:T(8,128)(2,1)S(1)} %get-tuple-element.55.refs_14_.refs_0_.refs_5_), channel_id=1, source_target_pairs={{0,1},{2,3},{4,5},{6,7},{8,9},{10,11},{12,13},{14,15},{1,0},{3,2},... | collective-permute-start | bytes 1572872 | tf_op jit(solution)/shard_map/ppermute | solution.py:48
  72.6 14.3 %collective-permute-start.17 = (bf16[16,128,128]{2,1,0:T(8,128)(2,1)S(1)}, bf16[16,128,128]{2,1,0:T(8,128)(2,1)S(1)}, u32[]{:S(2)}, u32[]{:S(2)}) collective-permute-start(bf16[16,128,128]{2,1,0:T(8,128)(2,1)S(1)} %get-tuple-element.55.refs_14_.refs_0_.refs_5_), channel_id=1, source_target_pairs={{0,16},{16,0},{32,48},{48,32},{64,80},{80,64},{96,112},{112,96},{1... | collective-permute-start | bytes 1572872 | tf_op jit(solution)/shard_map/ppermute | solution.py:38
  79.7 10.3 %collective-permute-start.20 = (bf16[4,256,128]{2,1,0:T(8,128)(2,1)S(1)}, bf16[4,256,128]{2,1,0:T(8,128)(2,1)S(1)}, u32[]{:S(2)}, u32[]{:S(2)}) collective-permute-start(bf16[4,256,128]{2,1,0:T(8,128)(2,1)S(1)} %get-tuple-element.59), channel_id=1, source_target_pairs={{0,32},{16,48},{32,64},{48,80},{64,96},{80,112},{96,0},{112,16},{1... | collective-permute-start | bytes 786440 | tf_op jit(solution)/shard_map/ppermute | solution.py:43
  80.9 9.1 %collective-permute-start.21 = (bf16[4,256,128]{2,1,0:T(8,128)(2,1)S(1)}, bf16[4,256,128]{2,1,0:T(8,128)(2,1)S(1)}, u32[]{:S(2)}, u32[]{:S(2)}) collective-permute-start(bf16[4,256,128]{2,1,0:T(8,128)(2,1)S(1)} %get-tuple-element.60), channel_id=1, source_target_pairs={{0,96},{16,112},{32,0},{48,16},{64,32},{80,48},{96,64},{112,80},{1... | collective-permute-start | bytes 786440 | tf_op jit(solution)/shard_map/ppermute | solution.py:43
  81.7 13.2 %collective-permute-start.22 = (bf16[4,256,128]{2,1,0:T(8,128)(2,1)S(1)}, bf16[4,256,128]{2,1,0:T(8,128)(2,1)S(1)}, u32[]{:S(2)}, u32[]{:S(2)}) collective-permute-start(bf16[4,256,128]{2,1,0:T(8,128)(2,1)S(1)} %get-tuple-element.61), channel_id=1, source_target_pairs={{0,64},{16,80},{32,96},{48,112},{64,0},{80,16},{96,32},{112,48},{1... | collective-permute-start | bytes 786440 | tf_op jit(solution)/shard_map/ppermute | solution.py:43
  83.3 16.4 %collective-permute-start.19 = (bf16[16,128,128]{2,1,0:T(8,128)(2,1)S(1)}, bf16[16,128,128]{2,1,0:T(8,128)(2,1)S(1)}, u32[]{:S(2)}, u32[]{:S(2)}) collective-permute-start(bf16[16,128,128]{2,1,0:T(8,128)(2,1)S(1)} %get-tuple-element.55.refs_14_.refs_0_.refs_5_), channel_id=1, source_target_pairs={{1,2},{3,4},{5,6},{7,8},{9,10},{11,12},{13,14},{2,1},{4,3},{6,5},{... | collective-permute-start | bytes 1572872 | tf_op jit(solution)/shard_map/ppermute | solution.py:48
  86.9 17.8 %collective-permute-start.18 = (bf16[16,128,128]{2,1,0:T(8,128)(2,1)S(1)}, bf16[16,128,128]{2,1,0:T(8,128)(2,1)S(1)}, u32[]{:S(2)}, u32[]{:S(2)}) collective-permute-start(bf16[16,128,128]{2,1,0:T(8,128)(2,1)S(1)} %collective-permute-done.17.refs_2_.refs_4_), channel_id=1, source_target_pairs={{48,16},{80,48},{112,80},{0,32},{32,64},{64,96},{49,17},{81,49},{1... | collective-permute-start | bytes 1572872 | tf_op jit(solution)/shard_map/ppermute | solution.py:54
  95.6 16.0 %collective-permute-start.23 = (bf16[8,256,128]{2,1,0:T(8,128)(2,1)S(1)}, bf16[8,256,128]{2,1,0:T(8,128)(2,1)S(1)}, u32[]{:S(2)}, u32[]{:S(2)}) collective-permute-start(bf16[8,256,128]{2,1,0:T(8,128)(2,1)S(1)} %turned.5), channel_id=1, source_target_pairs={{0,16},{16,0},{32,48},{48,32},{64,80},{80,64},{96,112},{112,96},{1... | collective-permute-start | bytes 1572872 | tf_op jit(solution)/shard_map/ppermute | solution.py:38

commit v3 on v2

--- a/solution.py
+++ b/solution.py
@@ -43,11 +43,6 @@
     return lax.ppermute(value, "gx", [(i, (i + 2 * steps) % count) for i in range(count)])
 
 
-def along_gy(value, first):
-    pairs = [(i, i + 1) for i in range(first, lax.axis_size("gy") - 1, 2)]
-    return lax.ppermute(value, "gy", pairs + [(j, i) for i, j in pairs])
-
-
 def passed_on(across):
     gx = lax.axis_size("gx")
     on = [(i, i - 2) for i in range(3, gx, 2)] + [(i, i + 2) for i in range(0, gx - 2, 2)]
@@ -55,7 +50,10 @@
 
 
 def beside_of(exports):
-    return other_x(exports), along_gy(exports, 0), along_gy(exports, 1)
+    count = lax.axis_size("gy")
+    core = lax.ppermute(exports, "gy", [(i, i ^ 1) for i in range(count)])
+    on = [(i, i + 2) for i in range(0, count - 2, 2)] + [(i, i - 2) for i in range(3, count, 2)]
+    return other_x(exports), core, lax.ppermute(core, "gy", on)
 
 
 def position():
@@ -539,7 +537,7 @@
 
     across, core, beside = beside_of(e3)
     around = (across, passed_on(across), core, beside)
-    p2_other, o3 = other_blocks(order, index, tiles, base, pool, blocks - exports, core, "others_2")
+    p2_other, o3 = other_blocks(order, index, tiles, base, pool, blocks - exports, e3, "others_2")
     p2 = (p2_first, p2_other)
     rounded = ((e3, o3), (e2, o2), (e1, o1))
     walls = over_y(walls_of(wall_at, message, rounded, (core,)))

time: 116 us -> 115 us (level)
  starting transfers between devices: 37.4 us -> 42.9 us
  waiting for transfers between devices: 35.6 us -> 31.1 us
  Pallas kernels: 37.8 us -> 36.5 us
    ppermute x6, starting transfers between devices: 5.98 us -> 11.6 us  [the longest x3 11.4 us: beside_of(): return (other_x(exports), core, lax.ppermute(core, 'gy', on))]
    ppermute x6, waiting for transfers between devices: 17.8 us -> 12.9 us  [other_x(): return lax.ppermute(value, 'gx', [(i, i ^ 1) for i in range(count)])]
    ppermute x3, waiting for transfers between devices: 10.8 us -> 12.7 us  [passed_on(): return lax.ppermute(across, 'gx', on)]
    ppermute x9, waiting for transfers between devices: 6.08 us -> 4.91 us  [along_y(): lax.ppermute(value, 'gx', [(i, (i + 2 * steps) % count) for i in range(co...]
  transfers between devices with their start and end apart: 24 -> 24, of which waited for: 13 -> 12; matrix products, arithmetic and copies ran while one was open for 0% -> 0% of each run, Pallas kernels for 23% -> 22%
where the time goes in v3:
time: 115 us; the launch traced here: 114 us
  starting transfers between devices  42.9 us (37%)
  Pallas kernels  36.5 us (32%)
  waiting for transfers between devices  31.1 us (27%)
  local copies, waits for them, and re-layouts  1.89 us (2%)
    ppermute x6, waiting for transfers between devices, other_x(): return lax.ppermute(value, 'gx', [(i, i ^ 1) for i in range(count)])  12.9 us
    ppermute x3, waiting for transfers between devices, passed_on(): return lax.ppermute(across, 'gx', on)  12.7 us
    ppermute x9, starting transfers between devices, along_y(): lax.ppermute(value, 'gx', [(i, (i + 2 * steps) % count) for i in range(co...  11.5 us
    ppermute x3, starting transfers between devices, beside_of(): return (other_x(exports), core, lax.ppermute(core, 'gy', on))  11.4 us
    ppermute x6, starting transfers between devices, other_x(): return lax.ppermute(value, 'gx', [(i, i ^ 1) for i in range(count)])  10.5 us
    ppermute x3, starting transfers between devices, passed_on(): return lax.ppermute(across, 'gx', on)  9.32 us
    pallas_call x2, Pallas kernels, other_blocks(): pl.pallas_call(other_kernel, out_shape=(jax.ShapeDtypeStruct((count, rows...  7.23 us
    pallas_call x1, Pallas kernels, last_blocks(): pl.pallas_call(last_kernel, out_shape=jax.ShapeDtypeStruct((blocks, rows,...  6.95 us
  transfers between devices with their start and end apart: 24, of which 12 were waited for; matrix products, arithmetic and copies ran while one was open for 0% of the time, Pallas kernels for 22%

profile of v3, /device:TPU:40, one launch (start us, length us, event | category | flops | bytes accessed | tf_op | source)
XLA Modules:
  0.0 113.6 jit_solution(14946830770747112441)
XLA Ops:
  0.7 3.0 %exports.1.refs_5_.refs_0_.refs_14_.refs_18_.refs_9_ = bf16[16,128,128]{2,1,0:T(8,128)(2,1)} custom-call(s32[16]{0:T(128)} %ids.3, f32[40,128,128]{2,1,0:T(8,128)} %pressure.9), custom_call_target="tpu_custom_call" | custom-call | flops 3000000000 | tf_op jit(solution)/shard_map/exports/pallas_call | solution.py:131
  3.7 0.0 copy-start.1
  3.7 0.1 collective-permute-start
  3.8 1.6 %collective-permute-start.4 = (bf16[16,128,128]{2,1,0:T(8,128)(2,1)}, bf16[16,128,128]{2,1,0:T(8,128)(2,1)S(1)}, u32[]{:S(2)}, u32[]{:S(2)}) collective-permute-start(bf16[16,128,128]{2,1,0:T(8,128)(2,1)} %exports.1.refs_5_.refs_0_.refs_14_.refs_18_.refs_9_), channel_id=1, source_target_pairs={{0,16},{16,0},{32,48},{48,32},{64,80},{80,64},{96,112},{112,96},{1... | collective-permute-start | bytes 1572872 | tf_op jit(solution)/shard_map/ppermute | solution.py:38
  5.4 0.1 reshape.35
  5.5 0.1 reshape.33
  5.6 0.1 reshape.32
  5.6 0.1 pad_maximum_fusion.table
  5.7 0.3 collective-permute-done.after.refs_4_
  6.1 1.6 %copy-done.3 = f32[1,1,8,2,2,128,128]{6,5,4,3,2,1,0:T(8,128)S(1)} copy-done((f32[1,1,8,2,2,128,128]{6,5,4,3,2,1,0:T(8,128)S(1)}, f32[1,1,8,2,2,128,128]{6,5,4,3,2,1,0:T(8,128)}, u32[]{:S(2)}) %copy-start.3) | copy-done | bytes 2097176
  7.6 0.8 responses_1.1
  8.5 1.6 %collective-permute-start.1 = (bf16[4,144,128]{2,1,0:T(8,128)(2,1)S(1)}, bf16[4,144,128]{2,1,0:T(8,128)(2,1)S(1)}, u32[]{:S(2)}, u32[]{:S(2)}) collective-permute-start(bf16[4,144,128]{2,1,0:T(8,128)(2,1)S(1)} %get-tuple-element.33), channel_id=1, source_target_pairs={{0,32},{16,48},{32,64},{48,80},{64,96},{80,112},{96,0},{112,16},{1... | collective-permute-start | bytes 442376 | tf_op jit(solution)/shard_map/ppermute | solution.py:43
  10.1 0.5 collective-permute-start.2
  10.6 2.3 %collective-permute-start.3 = (bf16[4,144,128]{2,1,0:T(8,128)(2,1)S(1)}, bf16[4,144,128]{2,1,0:T(8,128)(2,1)S(1)}, u32[]{:S(2)}, u32[]{:S(2)}) collective-permute-start(bf16[4,144,128]{2,1,0:T(8,128)(2,1)S(1)} %get-tuple-element.35), channel_id=1, source_target_pairs={{0,64},{16,80},{32,96},{48,112},{64,0},{80,16},{96,32},{112,48},{1... | collective-permute-start | bytes 442376 | tf_op jit(solution)/shard_map/ppermute | solution.py:43
  12.9 3.8 %collective-permute-start.7 = (bf16[16,128,128]{2,1,0:T(8,128)(2,1)}, bf16[16,128,128]{2,1,0:T(8,128)(2,1)S(1)}, u32[]{:S(2)}, u32[]{:S(2)}) collective-permute-start(bf16[16,128,128]{2,1,0:T(8,128)(2,1)} %collective-permute-done.after.refs_4_), channel_id=1, source_target_pairs={{0,2},{2,4},{4,6},{6,8},{8,10},{10,12},{12,14},{3,1},{5,3},{7,5},{... | collective-permute-start | bytes 1572872 | tf_op jit(solution)/shard_map/ppermute | solution.py:56
  16.7 1.7 %collective-permute-done.4.refs_4_ = bf16[16,128,128]{2,1,0:T(8,128)(2,1)S(1)} collective-permute-done((bf16[16,128,128]{2,1,0:T(8,128)(2,1)}, bf16[16,128,128]{2,1,0:T(8,128)(2,1)S(1)}, u32[]{:S(2)}, u32[]{:S(2)}) %collective-permute-start.4) | collective-permute-done | bytes 524320 | tf_op jit(solution)/shard_map/ppermute | solution.py:38
  18.4 0.0 collective-permute-done.1.refs_1_
  18.4 0.0 collective-permute-done.2.refs_2_
  18.4 1.2 %collective-permute-done.3.refs_3_ = bf16[4,144,128]{2,1,0:T(8,128)(2,1)S(1)} collective-permute-done((bf16[4,144,128]{2,1,0:T(8,128)(2,1)S(1)}, bf16[4,144,128]{2,1,0:T(8,128)(2,1)S(1)}, u32[]{:S(2)}, u32[]{:S(2)}) %collective-permute-start.3) | collective-permute-done | bytes 147488 | tf_op jit(solution)/shard_map/ppermute | solution.py:43
  19.6 0.4 turned.3
  20.0 2.7 %collective-permute-start.6 = (bf16[16,128,128]{2,1,0:T(8,128)(2,1)S(1)}, bf16[16,128,128]{2,1,0:T(8,128)(2,1)S(1)}, u32[]{:S(2)}, u32[]{:S(2)}) collective-permute-start(bf16[16,128,128]{2,1,0:T(8,128)(2,1)S(1)} %get-tuple-element.36.after.refs_2_), channel_id=1, source_target_pairs={{48,16},{80,48},{112,80},{0,32},{32,64},{64,96},{49,17},{81,49},{1... | collective-permute-start | bytes 1572872 | tf_op jit(solution)/shard_map/ppermute | solution.py:49
  22.7 2.1 %collective-permute-start.5 = (bf16[8,144,128]{2,1,0:T(8,128)(2,1)S(1)}, bf16[8,144,128]{2,1,0:T(8,128)(2,1)S(1)}, u32[]{:S(2)}, u32[]{:S(2)}) collective-permute-start(bf16[8,144,128]{2,1,0:T(8,128)(2,1)S(1)} %get-tuple-element.40), channel_id=1, source_target_pairs={{0,16},{16,0},{32,48},{48,32},{64,80},{80,64},{96,112},{112,96},{1... | collective-permute-start | bytes 884744 | tf_op jit(solution)/shard_map/ppermute | solution.py:38
  24.8 2.1 %prepare.1 = (s32[40]{0:T(128)S(1)}, s32[12,40]{1,0:T(8,128)S(1)}, s32[2,8]{1,0:T(2,128)S(1)}, bf16[24,128,128]{2,1,0:T(8,128)(2,1)S(1)}) custom-call(s32[16]{0:T(128)S(1)} %copy-done.12, s32[12,40]{1,0:T(8,128)S(1)} %bitcast.28, s32[12,40]{1,0:T(8,128)S(1)} %bitcast.29, s32[2,8]{1,0:T(2,128)S(1)} %bitcast.32, f32[40,128,128]{2,1,0:T(8,128)S(1)} %copy-done.1, ...), custom_call_target="tpu_custom_call" | custom-call | flops 2100000000 | tf_op jit(solution)/shard_map/prepare/pallas_call | solution.py:185
  27.0 4.1 %collective-permute-done.5.refs_4_ = bf16[8,144,128]{2,1,0:T(8,128)(2,1)S(1)} collective-permute-done((bf16[8,144,128]{2,1,0:T(8,128)(2,1)S(1)}, bf16[8,144,128]{2,1,0:T(8,128)(2,1)S(1)}, u32[]{:S(2)}, u32[]{:S(2)}) %collective-permute-start.5) | collective-permute-done | bytes 294944 | tf_op jit(solution)/shard_map/ppermute | solution.py:38
  31.1 1.2 %base_1.1.base = f32[40,128,128]{2,1,0:T(8,128)S(1)} custom-call(s32[2,8]{1,0:T(2,128)S(1)} %get-tuple-element.39.wall_at, s32[40]{0:T(128)S(1)} %get-tuple-element.37.order, f32[40,128,128]{2,1,0:T(8,128)S(1)} %copy-done.1, bf16[4,144,128]{2,1,0:T(8,128)(2,1)S(1)} %get-tuple-element.32.refs_0_, bf16[4,144,128]{2,1,0:T(8,128)(2,1)S(1)} %collective-permute-done.1.refs_1_, ...), custom_call_target="tpu_custom_call" | custom-call | flops 1600000000 | tf_op jit(solution)/shard_map/base_1/pallas_call | solution.py:310
  32.3 0.0 collective-permute-done.7.refs_5_
  32.3 2.8 %collective-permute-done.6.refs_3_ = bf16[16,128,128]{2,1,0:T(8,128)(2,1)S(1)} collective-permute-done((bf16[16,128,128]{2,1,0:T(8,128)(2,1)S(1)}, bf16[16,128,128]{2,1,0:T(8,128)(2,1)S(1)}, u32[]{:S(2)}, u32[]{:S(2)}) %collective-permute-start.6) | collective-permute-done | bytes 524320 | tf_op jit(solution)/shard_map/ppermute | solution.py:49
  35.1 3.9 %exports_1.1 = (f32[16,128,128]{2,1,0:T(8,128)S(1)}, bf16[16,128,128]{2,1,0:T(8,128)(2,1)S(1)}, bf16[104,128,128]{2,1,0:T(8,128)(2,1)S(1)}) custom-call(s32[40]{0:T(128)S(1)} %get-tuple-element.37.order, s32[12,40]{1,0:T(8,128)S(1)} %get-tuple-element.38.index, bf16[40,1536,128]{2,1,0:T(8,128)(2,1)S(1)} %bitcast.15, f32[40,128,128]{2,1,0:T(8,128)S(1)} %base_1.1.base, ...), custom_call_target="tpu_custom_call" | custom-call | flops 3100000000 | tf_op jit(solution)/shard_map/exports_1/pallas_call | solution.py:422
  39.0 0.1 collective-permute-start.8
  39.1 1.6 %collective-permute-start.12 = (bf16[16,128,128]{2,1,0:T(8,128)(2,1)S(1)}, bf16[16,128,128]{2,1,0:T(8,128)(2,1)S(1)}, u32[]{:S(2)}, u32[]{:S(2)}) collective-permute-start(bf16[16,128,128]{2,1,0:T(8,128)(2,1)S(1)} %get-tuple-element.42.refs_12_.refs_0_.refs_16_.refs_7_), channel_id=1, source_target_pairs={{0,16},{16,0},{32,48},{48,32},{64,80},{80,64},{96,112},{112,96},{1... | collective-permute-start | bytes 1572872 | tf_op jit(solution)/shard_map/ppermute | solution.py:38
  40.7 0.3 collective-permute-done.8.after.refs_4_
  41.0 0.8 responses_2.1
  41.8 1.1 collective-permute-start.9
  42.9 1.0 collective-permute-start.10
  43.9 1.7 %collective-permute-start.11 = (bf16[4,128,128]{2,1,0:T(8,128)(2,1)S(1)}, bf16[4,128,128]{2,1,0:T(8,128)(2,1)S(1)}, u32[]{:S(2)}, u32[]{:S(2)}) collective-permute-start(bf16[4,128,128]{2,1,0:T(8,128)(2,1)S(1)} %get-tuple-element.46), channel_id=1, source_target_pairs={{0,64},{16,80},{32,96},{48,112},{64,0},{80,16},{96,32},{112,48},{1... | collective-permute-start | bytes 393224 | tf_op jit(solution)/shard_map/ppermute | solution.py:43
  45.7 3.8 %collective-permute-start.15 = (bf16[16,128,128]{2,1,0:T(8,128)(2,1)S(1)}, bf16[16,128,128]{2,1,0:T(8,128)(2,1)S(1)}, u32[]{:S(2)}, u32[]{:S(2)}) collective-permute-start(bf16[16,128,128]{2,1,0:T(8,128)(2,1)S(1)} %collective-permute-done.8.after.refs_4_), channel_id=1, source_target_pairs={{0,2},{2,4},{4,6},{6,8},{8,10},{10,12},{12,14},{3,1},{5,3},{7,5},{... | collective-permute-start | bytes 1572872 | tf_op jit(solution)/shard_map/ppermute | solution.py:56
  49.5 4.0 %collective-permute-done.12.refs_4_ = bf16[16,128,128]{2,1,0:T(8,128)(2,1)S(1)} collective-permute-done((bf16[16,128,128]{2,1,0:T(8,128)(2,1)S(1)}, bf16[16,128,128]{2,1,0:T(8,128)(2,1)S(1)}, u32[]{:S(2)}, u32[]{:S(2)}) %collective-permute-start.12) | collective-permute-done | bytes 524320 | tf_op jit(solution)/shard_map/ppermute | solution.py:38
  53.5 0.4 turned.4
  53.9 2.9 %collective-permute-start.14 = (bf16[16,128,128]{2,1,0:T(8,128)(2,1)S(1)}, bf16[16,128,128]{2,1,0:T(8,128)(2,1)S(1)}, u32[]{:S(2)}, u32[]{:S(2)}) collective-permute-start(bf16[16,128,128]{2,1,0:T(8,128)(2,1)S(1)} %get-tuple-element.50.after.refs_2_), channel_id=1, source_target_pairs={{48,16},{80,48},{112,80},{0,32},{32,64},{64,96},{49,17},{81,49},{1... | collective-permute-start | bytes 1572872 | tf_op jit(solution)/shard_map/ppermute | solution.py:49
  56.8 1.8 %collective-permute-start.13 = (bf16[8,128,128]{2,1,0:T(8,128)(2,1)S(1)}, bf16[8,128,128]{2,1,0:T(8,128)(2,1)S(1)}, u32[]{:S(2)}, u32[]{:S(2)}) collective-permute-start(bf16[8,128,128]{2,1,0:T(8,128)(2,1)S(1)} %get-tuple-element.47), channel_id=1, source_target_pairs={{0,16},{16,0},{32,48},{48,32},{64,80},{80,64},{96,112},{112,96},{1... | collective-permute-start | bytes 786440 | tf_op jit(solution)/shard_map/ppermute | solution.py:38
  58.6 3.6 %others_1.1 = (f32[24,128,128]{2,1,0:T(8,128)S(1)}, bf16[24,128,128]{2,1,0:T(8,128)(2,1)S(1)}) custom-call(s32[40]{0:T(128)S(1)} %get-tuple-element.37.order, s32[12,40]{1,0:T(8,128)S(1)} %get-tuple-element.38.index, bf16[40,1536,128]{2,1,0:T(8,128)(2,1)S(1)} %bitcast.16, f32[40,128,128]{2,1,0:T(8,128)S(1)} %base_1.1.base, ...), custom_call_target="tpu_custom_call" | custom-call | tf_op jit(solution)/shard_map/others_1/pallas_call | solution.py:452
  62.2 2.3 %collective-permute-done.13.refs_9_ = bf16[8,128,128]{2,1,0:T(8,128)(2,1)S(1)} collective-permute-done((bf16[8,128,128]{2,1,0:T(8,128)(2,1)S(1)}, bf16[8,128,128]{2,1,0:T(8,128)(2,1)S(1)}, u32[]{:S(2)}, u32[]{:S(2)}) %collective-permute-start.13) | collective-permute-done | bytes 262176 | tf_op jit(solution)/shard_map/ppermute | solution.py:38
  64.4 1.3 %base_2.1.base = f32[40,128,128]{2,1,0:T(8,128)S(1)} custom-call(s32[2,8]{1,0:T(2,128)S(1)} %get-tuple-element.39.wall_at, s32[40]{0:T(128)S(1)} %get-tuple-element.37.order, f32[40,128,128]{2,1,0:T(8,128)S(1)} %copy-done.1, bf16[4,144,128]{2,1,0:T(8,128)(2,1)S(1)} %get-tuple-element.32.refs_0_, bf16[4,144,128]{2,1,0:T(8,128)(2,1)S(1)} %collective-permute-done.1.refs_1_, ...), custom_call_target="tpu_custom_call" | custom-call | tf_op jit(solution)/shard_map/base_2/pallas_call | solution.py:310
  65.8 0.0 collective-permute-done.15.refs_5_
  65.8 3.4 %collective-permute-done.14.refs_3_ = bf16[16,128,128]{2,1,0:T(8,128)(2,1)S(1)} collective-permute-done((bf16[16,128,128]{2,1,0:T(8,128)(2,1)S(1)}, bf16[16,128,128]{2,1,0:T(8,128)(2,1)S(1)}, u32[]{:S(2)}, u32[]{:S(2)}) %collective-permute-start.14) | collective-permute-done | bytes 524320 | tf_op jit(solution)/shard_map/ppermute | solution.py:49
  69.2 2.9 %exports_2.1 = (f32[16,128,128]{2,1,0:T(8,128)S(1)}, bf16[16,128,128]{2,1,0:T(8,128)(2,1)S(1)}, bf16[104,128,128]{2,1,0:T(8,128)(2,1)S(1)}) custom-call(s32[40]{0:T(128)S(1)} %get-tuple-element.37.order, s32[12,40]{1,0:T(8,128)S(1)} %get-tuple-element.38.index, bf16[40,1536,128]{2,1,0:T(8,128)(2,1)S(1)} %bitcast.17, f32[40,128,128]{2,1,0:T(8,128)S(1)} %base_2.1.base, ...), custom_call_target="tpu_custom_call" | custom-call | flops 3100000000 | tf_op jit(solution)/shard_map/exports_2/pallas_call | solution.py:422
  72.2 0.1 collective-permute-start.18
  72.3 1.6 %collective-permute-start.16 = (bf16[16,128,128]{2,1,0:T(8,128)(2,1)S(1)}, bf16[16,128,128]{2,1,0:T(8,128)(2,1)S(1)}, u32[]{:S(2)}, u32[]{:S(2)}) collective-permute-start(bf16[16,128,128]{2,1,0:T(8,128)(2,1)S(1)} %get-tuple-element.55.after.refs_14_.refs_0_.refs_5_), channel_id=1, source_target_pairs={{0,16},{16,0},{32,48},{48,32},{64,80},{80,64},{96,112},{112,96},{1... | collective-permute-start | bytes 1572872 | tf_op jit(solution)/shard_map/ppermute | solution.py:38
  73.8 3.6 %others_2.1 = (f32[24,128,128]{2,1,0:T(8,128)S(1)}, bf16[24,128,128]{2,1,0:T(8,128)(2,1)S(1)}) custom-call(s32[40]{0:T(128)S(1)} %get-tuple-element.37.order, s32[12,40]{1,0:T(8,128)S(1)} %get-tuple-element.38.index, bf16[40,1536,128]{2,1,0:T(8,128)(2,1)S(1)} %bitcast.18, f32[40,128,128]{2,1,0:T(8,128)S(1)} %base_2.1.base, ...), custom_call_target="tpu_custom_call" | custom-call | tf_op jit(solution)/shard_map/others_2/pallas_call | solution.py:452
  77.5 1.3 %walls.1 = (bf16[4,256,128]{2,1,0:T(8,128)(2,1)S(1)}, bf16[4,256,128]{2,1,0:T(8,128)(2,1)S(1)}, bf16[4,256,128]{2,1,0:T(8,128)(2,1)S(1)}, bf16[4,256,128]{2,1,0:T(8,128)(2,1)S(1)}) custom-call(s32[2,8]{1,0:T(2,128)S(1)} %get-tuple-element.39.wall_at, bf16[4,144,128]{2,1,0:T(8,128)(2,1)S(1)} %get-tuple-element.32.refs_0_, ...), custom_call_target="tpu_custom_call" | custom-call | tf_op jit(solution)/shard_map/walls/pallas_call | solution.py:347
  78.7 1.3 %collective-permute-start.20 = (bf16[4,256,128]{2,1,0:T(8,128)(2,1)S(1)}, bf16[4,256,128]{2,1,0:T(8,128)(2,1)S(1)}, u32[]{:S(2)}, u32[]{:S(2)}) collective-permute-start(bf16[4,256,128]{2,1,0:T(8,128)(2,1)S(1)} %get-tuple-element.59), channel_id=1, source_target_pairs={{0,32},{16,48},{32,64},{48,80},{64,96},{80,112},{96,0},{112,16},{1... | collective-permute-start | bytes 786440 | tf_op jit(solution)/shard_map/ppermute | solution.py:43
  80.0 0.8 collective-permute-start.21
  80.8 1.2 %collective-permute-start.22 = (bf16[4,256,128]{2,1,0:T(8,128)(2,1)S(1)}, bf16[4,256,128]{2,1,0:T(8,128)(2,1)S(1)}, u32[]{:S(2)}, u32[]{:S(2)}) collective-permute-start(bf16[4,256,128]{2,1,0:T(8,128)(2,1)S(1)} %get-tuple-element.61), channel_id=1, source_target_pairs={{0,64},{16,80},{32,96},{48,112},{64,0},{80,16},{96,32},{112,48},{1... | collective-permute-start | bytes 786440 | tf_op jit(solution)/shard_map/ppermute | solution.py:43
  82.0 3.7 %collective-permute-start.19 = (bf16[16,128,128]{2,1,0:T(8,128)(2,1)S(1)}, bf16[16,128,128]{2,1,0:T(8,128)(2,1)S(1)}, u32[]{:S(2)}, u32[]{:S(2)}) collective-permute-start(bf16[16,128,128]{2,1,0:T(8,128)(2,1)S(1)} %collective-permute-done.18.refs_4_.refs_11_), channel_id=1, source_target_pairs={{0,2},{2,4},{4,6},{6,8},{8,10},{10,12},{12,14},{3,1},{5,3},{7,5},{... | collective-permute-start | bytes 1572872 | tf_op jit(solution)/shard_map/ppermute | solution.py:56
  85.7 0.8 collective-permute-done.16.refs_2_.refs_4_
  86.6 3.7 %collective-permute-start.17 = (bf16[16,128,128]{2,1,0:T(8,128)(2,1)S(1)}, bf16[16,128,128]{2,1,0:T(8,128)(2,1)S(1)}, u32[]{:S(2)}, u32[]{:S(2)}) collective-permute-start(bf16[16,128,128]{2,1,0:T(8,128)(2,1)S(1)} %collective-permute-done.16.refs_2_.refs_4_), channel_id=1, source_target_pairs={{48,16},{80,48},{112,80},{0,32},{32,64},{64,96},{49,17},{81,49},{1... | collective-permute-start | bytes 1572872 | tf_op jit(solution)/shard_map/ppermute | solution.py:49
  90.3 0.0 collective-permute-done.20.refs_1_
  90.3 3.6 %collective-permute-done.22.refs_3_ = bf16[4,256,128]{2,1,0:T(8,128)(2,1)S(1)} collective-permute-done((bf16[4,256,128]{2,1,0:T(8,128)(2,1)S(1)}, bf16[4,256,128]{2,1,0:T(8,128)(2,1)S(1)}, u32[]{:S(2)}, u32[]{:S(2)}) %collective-permute-start.22) | collective-permute-done | bytes 262176 | tf_op jit(solution)/shard_map/ppermute | solution.py:43
  94.0 0.7 turned.5
  94.7 1.9 %collective-permute-start.23 = (bf16[8,256,128]{2,1,0:T(8,128)(2,1)S(1)}, bf16[8,256,128]{2,1,0:T(8,128)(2,1)S(1)}, u32[]{:S(2)}, u32[]{:S(2)}) collective-permute-start(bf16[8,256,128]{2,1,0:T(8,128)(2,1)S(1)} %turned.5), channel_id=1, source_target_pairs={{0,16},{16,0},{32,48},{48,32},{64,80},{80,64},{96,112},{112,96},{1... | collective-permute-start | bytes 1572872 | tf_op jit(solution)/shard_map/ppermute | solution.py:38
  96.6 1.4 %base_3.1.base = f32[40,128,128]{2,1,0:T(8,128)S(1)} custom-call(s32[2,8]{1,0:T(2,128)S(1)} %get-tuple-element.39.wall_at, s32[40]{0:T(128)S(1)} %get-tuple-element.37.order, f32[40,128,128]{2,1,0:T(8,128)S(1)} %copy-done.1, bf16[4,144,128]{2,1,0:T(8,128)(2,1)S(1)} %get-tuple-element.32.refs_0_, bf16[4,144,128]{2,1,0:T(8,128)(2,1)S(1)} %collective-permute-done.1.refs_1_, ...), custom_call_target="tpu_custom_call" | custom-call | tf_op jit(solution)/shard_map/base_3/pallas_call | solution.py:310
  98.0 6.4 %collective-permute-done.17.refs_3_ = bf16[16,128,128]{2,1,0:T(8,128)(2,1)S(1)} collective-permute-done((bf16[16,128,128]{2,1,0:T(8,128)(2,1)S(1)}, bf16[16,128,128]{2,1,0:T(8,128)(2,1)S(1)}, u32[]{:S(2)}, u32[]{:S(2)}) %collective-permute-start.17) | collective-permute-done | bytes 524320 | tf_op jit(solution)/shard_map/ppermute | solution.py:49
  104.4 6.9 %last.1 = f32[40,128,128]{2,1,0:T(8,128)} custom-call(s32[40]{0:T(128)S(1)} %get-tuple-element.37.order, s32[12,40]{1,0:T(8,128)S(1)} %get-tuple-element.38.index, bf16[40,1536,128]{2,1,0:T(8,128)(2,1)S(1)} %bitcast.19, f32[40,128,128]{2,1,0:T(8,128)S(1)} %base_3.1.base, bf16[16,128,128]{2,1,0:T(8,128)(2,1)S(1)} %get-tuple-element.55.after.refs_14_.refs_0_.refs_5_, ...), custom_call_target="tpu_custom_call" | custom-call | tf_op jit(solution)/shard_map/last/pallas_call | solution.py:486
  111.3 2.1 %states_after.1 = f32[16,2,128,128]{3,2,1,0:T(8,128)} custom-call(s32[2,8]{1,0:T(2,128)S(1)} %bitcast.23, f32[2,16]{1,0:T(2,128)S(1)} %bitcast.27, f32[2,16]{1,0:T(2,128)S(1)} %bitcast.25, f32[16,2,128,128]{3,2,1,0:T(8,128)S(1)} %bitcast.22, bf16[4,256,128]{2,1,0:T(8,128)(2,1)S(1)} %get-tuple-element.58.refs_0_, ...), custom_call_target="tpu_custom_call" | custom-call | tf_op jit(solution)/shard_map/states_after/pallas_call | solution.py:378
  (34 shorter events, 0.1 us)
Async XLA Ops:
  0.6 4.7 %copy-start.5 = (s32[1,1,8,2]{2,3,1,0:T(2,128)S(1)}, s32[1,1,8,2]{2,3,1,0:T(2,128)}, u32[]{:S(2)}) copy-start(s32[1,1,8,2]{2,3,1,0:T(2,128)} %param.19) | copy-start | bytes 196
  0.6 4.8 %copy-start.6 = (f32[16,2]{0,1:T(2,128)S(1)}, f32[16,2]{0,1:T(2,128)}, u32[]{:S(2)}) copy-start(f32[16,2]{0,1:T(2,128)} %param.22) | copy-start | bytes 388
  0.7 4.9 %copy-start.7 = (f32[16,2]{0,1:T(2,128)S(1)}, f32[16,2]{0,1:T(2,128)}, u32[]{:S(2)}) copy-start(f32[16,2]{0,1:T(2,128)} %param.21) | copy-start | bytes 388
  0.7 5.0 %copy-start.13 = (f32[16]{0:T(128)S(1)}, f32[16]{0:T(128)}, u32[]{:S(2)}) copy-start(f32[16]{0:T(128)} %param.23) | copy-start | bytes 196
  0.7 5.4 %copy-start.10 = (f32[1,1,8,2,128]{4,3,2,1,0:T(2,128)S(1)}, f32[1,1,8,2,128]{4,3,2,1,0:T(2,128)}, u32[]{:S(2)}) copy-start(f32[1,1,8,2,128]{4,3,2,1,0:T(2,128)} %param.18) | copy-start | bytes 24580
  0.7 24.1 %copy-start.8 = (s32[40,12]{0,1:T(8,128)S(1)}, s32[40,12]{0,1:T(8,128)}, u32[]{:S(2)}) copy-start(s32[40,12]{0,1:T(8,128)} %param.14) | copy-start | bytes 5764
  0.7 24.1 %copy-start.9 = (s32[40,12]{0,1:T(8,128)S(1)}, s32[40,12]{0,1:T(8,128)}, u32[]{:S(2)}) copy-start(s32[40,12]{0,1:T(8,128)} %param.15) | copy-start | bytes 5764
  0.7 24.1 %copy-start.11 = (s32[1,1,8,2]{2,3,1,0:T(2,128)S(1)}, s32[1,1,8,2]{2,3,1,0:T(2,128)}, u32[]{:S(2)}) copy-start(s32[1,1,8,2]{2,3,1,0:T(2,128)} %param.17) | copy-start | bytes 196
  0.7 24.1 %copy-start.12 = (s32[16]{0:T(128)S(1)}, s32[16]{0:T(128)}, u32[]{:S(2)}) copy-start(s32[16]{0:T(128)} %ids.3) | copy-start | bytes 196
  3.7 21.1 %copy-start.1 = (f32[40,128,128]{2,1,0:T(8,128)S(1)}, f32[40,128,128]{2,1,0:T(8,128)}, u32[]{:S(2)}) copy-start(f32[40,128,128]{2,1,0:T(8,128)} %pressure.9) | copy-start | bytes 7864324
  3.7 2.3 %collective-permute-start = (bf16[16,128,128]{2,1,0:T(8,128)(2,1)}, bf16[16,128,128]{2,1,0:T(8,128)(2,1)}, u32[]{:S(2)}, u32[]{:S(2)}) collective-permute-start(bf16[16,128,128]{2,1,0:T(8,128)(2,1)} %exports.1.refs_5_.refs_0_.refs_14_.refs_18_.refs_9_), channel_id=1, source_target_pairs={{0,1},{1,0},{2,3},{3,2},{4,5},{5,4},{6,7},{7,6},{8,9},{9,8},{10,11... | collective-permute-start | bytes 1572872 | tf_op jit(solution)/shard_map/ppermute | solution.py:54
  3.8 14.5 %collective-permute-start.4 = (bf16[16,128,128]{2,1,0:T(8,128)(2,1)}, bf16[16,128,128]{2,1,0:T(8,128)(2,1)S(1)}, u32[]{:S(2)}, u32[]{:S(2)}) collective-permute-start(bf16[16,128,128]{2,1,0:T(8,128)(2,1)} %exports.1.refs_5_.refs_0_.refs_14_.refs_18_.refs_9_), channel_id=1, source_target_pairs={{0,16},{16,0},{32,48},{48,32},{64,80},{80,64},{96,112},{112,96},{1... | collective-permute-start | bytes 1572872 | tf_op jit(solution)/shard_map/ppermute | solution.py:38
  6.0 1.6 %copy-start.3 = (f32[1,1,8,2,2,128,128]{6,5,4,3,2,1,0:T(8,128)S(1)}, f32[1,1,8,2,2,128,128]{6,5,4,3,2,1,0:T(8,128)}, u32[]{:S(2)}) copy-start(f32[1,1,8,2,2,128,128]{6,5,4,3,2,1,0:T(8,128)} %param.20) | copy-start | bytes 6291460
  7.6 23.4 %copy-start.2 = (bf16[16,128,128]{2,1,0:T(8,128)(2,1)S(1)}, bf16[16,128,128]{2,1,0:T(8,128)(2,1)}, u32[]{:S(2)}) copy-start(bf16[16,128,128]{2,1,0:T(8,128)(2,1)} %exports.1.refs_5_.refs_0_.refs_14_.refs_18_.refs_9_) | copy-start | bytes 1572868
  8.5 9.9 %collective-permute-start.1 = (bf16[4,144,128]{2,1,0:T(8,128)(2,1)S(1)}, bf16[4,144,128]{2,1,0:T(8,128)(2,1)S(1)}, u32[]{:S(2)}, u32[]{:S(2)}) collective-permute-start(bf16[4,144,128]{2,1,0:T(8,128)(2,1)S(1)} %get-tuple-element.33), channel_id=1, source_target_pairs={{0,32},{16,48},{32,64},{48,80},{64,96},{80,112},{96,0},{112,16},{1... | collective-permute-start | bytes 442376 | tf_op jit(solution)/shard_map/ppermute | solution.py:43
  10.1 8.2 %collective-permute-start.2 = (bf16[4,144,128]{2,1,0:T(8,128)(2,1)S(1)}, bf16[4,144,128]{2,1,0:T(8,128)(2,1)S(1)}, u32[]{:S(2)}, u32[]{:S(2)}) collective-permute-start(bf16[4,144,128]{2,1,0:T(8,128)(2,1)S(1)} %get-tuple-element.34), channel_id=1, source_target_pairs={{0,96},{16,112},{32,0},{48,16},{64,32},{80,48},{96,64},{112,80},{1... | collective-permute-start | bytes 442376 | tf_op jit(solution)/shard_map/ppermute | solution.py:43
  10.6 9.0 %collective-permute-start.3 = (bf16[4,144,128]{2,1,0:T(8,128)(2,1)S(1)}, bf16[4,144,128]{2,1,0:T(8,128)(2,1)S(1)}, u32[]{:S(2)}, u32[]{:S(2)}) collective-permute-start(bf16[4,144,128]{2,1,0:T(8,128)(2,1)S(1)} %get-tuple-element.35), channel_id=1, source_target_pairs={{0,64},{16,80},{32,96},{48,112},{64,0},{80,16},{96,32},{112,48},{1... | collective-permute-start | bytes 442376 | tf_op jit(solution)/shard_map/ppermute | solution.py:43
  12.9 19.4 %collective-permute-start.7 = (bf16[16,128,128]{2,1,0:T(8,128)(2,1)}, bf16[16,128,128]{2,1,0:T(8,128)(2,1)S(1)}, u32[]{:S(2)}, u32[]{:S(2)}) collective-permute-start(bf16[16,128,128]{2,1,0:T(8,128)(2,1)} %collective-permute-done.after.refs_4_), channel_id=1, source_target_pairs={{0,2},{2,4},{4,6},{6,8},{8,10},{10,12},{12,14},{3,1},{5,3},{7,5},{... | collective-permute-start | bytes 1572872 | tf_op jit(solution)/shard_map/ppermute | solution.py:56
  19.6 15.5 %copy-start = (bf16[40,12,128,128]{3,2,1,0:T(8,128)(2,1)S(1)}, bf16[40,12,128,128]{3,2,1,0:T(8,128)(2,1)}, u32[]{:S(2)}) copy-start(bf16[40,12,128,128]{3,2,1,0:T(8,128)(2,1)} %param.13) | copy-start | bytes 47185924
  20.0 15.1 %collective-permute-start.6 = (bf16[16,128,128]{2,1,0:T(8,128)(2,1)S(1)}, bf16[16,128,128]{2,1,0:T(8,128)(2,1)S(1)}, u32[]{:S(2)}, u32[]{:S(2)}) collective-permute-start(bf16[16,128,128]{2,1,0:T(8,128)(2,1)S(1)} %get-tuple-element.36.after.refs_2_), channel_id=1, source_target_pairs={{48,16},{80,48},{112,80},{0,32},{32,64},{64,96},{49,17},{81,49},{1... | collective-permute-start | bytes 1572872 | tf_op jit(solution)/shard_map/ppermute | solution.py:49
  22.7 8.4 %collective-permute-start.5 = (bf16[8,144,128]{2,1,0:T(8,128)(2,1)S(1)}, bf16[8,144,128]{2,1,0:T(8,128)(2,1)S(1)}, u32[]{:S(2)}, u32[]{:S(2)}) collective-permute-start(bf16[8,144,128]{2,1,0:T(8,128)(2,1)S(1)} %get-tuple-element.40), channel_id=1, source_target_pairs={{0,16},{16,0},{32,48},{48,32},{64,80},{80,64},{96,112},{112,96},{1... | collective-permute-start | bytes 884744 | tf_op jit(solution)/shard_map/ppermute | solution.py:38
  35.1 5.9 %copy-start.4 = (f32[1,1,8,2,2,128,128]{6,5,4,3,2,1,0:T(8,128)S(1)}, f32[1,1,8,2,2,128,128]{6,5,4,3,2,1,0:T(8,128)}, u32[]{:S(2)}) copy-start(f32[1,1,8,2,2,128,128]{6,5,4,3,2,1,0:T(8,128)} %param.20) | copy-start | bytes 6291460
  39.0 2.0 %collective-permute-start.8 = (bf16[16,128,128]{2,1,0:T(8,128)(2,1)S(1)}, bf16[16,128,128]{2,1,0:T(8,128)(2,1)S(1)}, u32[]{:S(2)}, u32[]{:S(2)}) collective-permute-start(bf16[16,128,128]{2,1,0:T(8,128)(2,1)S(1)} %get-tuple-element.42.refs_12_.refs_0_.refs_16_.refs_7_), channel_id=1, source_target_pairs={{0,1},{1,0},{2,3},{3,2},{4,5},{5,4},{6,7},{7,6},{8,9},{9,8},{10,11... | collective-permute-start | bytes 1572872 | tf_op jit(solution)/shard_map/ppermute | solution.py:54
  39.1 14.3 %collective-permute-start.12 = (bf16[16,128,128]{2,1,0:T(8,128)(2,1)S(1)}, bf16[16,128,128]{2,1,0:T(8,128)(2,1)S(1)}, u32[]{:S(2)}, u32[]{:S(2)}) collective-permute-start(bf16[16,128,128]{2,1,0:T(8,128)(2,1)S(1)} %get-tuple-element.42.refs_12_.refs_0_.refs_16_.refs_7_), channel_id=1, source_target_pairs={{0,16},{16,0},{32,48},{48,32},{64,80},{80,64},{96,112},{112,96},{1... | collective-permute-start | bytes 1572872 | tf_op jit(solution)/shard_map/ppermute | solution.py:38
  41.8 11.6 %collective-permute-start.9 = (bf16[4,128,128]{2,1,0:T(8,128)(2,1)S(1)}, bf16[4,128,128]{2,1,0:T(8,128)(2,1)S(1)}, u32[]{:S(2)}, u32[]{:S(2)}) collective-permute-start(bf16[4,128,128]{2,1,0:T(8,128)(2,1)S(1)} %get-tuple-element.44), channel_id=1, source_target_pairs={{0,32},{16,48},{32,64},{48,80},{64,96},{80,112},{96,0},{112,16},{1... | collective-permute-start | bytes 393224 | tf_op jit(solution)/shard_map/ppermute | solution.py:43
  42.9 10.5 %collective-permute-start.10 = (bf16[4,128,128]{2,1,0:T(8,128)(2,1)S(1)}, bf16[4,128,128]{2,1,0:T(8,128)(2,1)S(1)}, u32[]{:S(2)}, u32[]{:S(2)}) collective-permute-start(bf16[4,128,128]{2,1,0:T(8,128)(2,1)S(1)} %get-tuple-element.45), channel_id=1, source_target_pairs={{0,96},{16,112},{32,0},{48,16},{64,32},{80,48},{96,64},{112,80},{1... | collective-permute-start | bytes 393224 | tf_op jit(solution)/shard_map/ppermute | solution.py:43
  43.9 9.6 %collective-permute-start.11 = (bf16[4,128,128]{2,1,0:T(8,128)(2,1)S(1)}, bf16[4,128,128]{2,1,0:T(8,128)(2,1)S(1)}, u32[]{:S(2)}, u32[]{:S(2)}) collective-permute-start(bf16[4,128,128]{2,1,0:T(8,128)(2,1)S(1)} %get-tuple-element.46), channel_id=1, source_target_pairs={{0,64},{16,80},{32,96},{48,112},{64,0},{80,16},{96,32},{112,48},{1... | collective-permute-start | bytes 393224 | tf_op jit(solution)/shard_map/ppermute | solution.py:43
  45.7 20.1 %collective-permute-start.15 = (bf16[16,128,128]{2,1,0:T(8,128)(2,1)S(1)}, bf16[16,128,128]{2,1,0:T(8,128)(2,1)S(1)}, u32[]{:S(2)}, u32[]{:S(2)}) collective-permute-start(bf16[16,128,128]{2,1,0:T(8,128)(2,1)S(1)} %collective-permute-done.8.after.refs_4_), channel_id=1, source_target_pairs={{0,2},{2,4},{4,6},{6,8},{8,10},{10,12},{12,14},{3,1},{5,3},{7,5},{... | collective-permute-start | bytes 1572872 | tf_op jit(solution)/shard_map/ppermute | solution.py:56
  53.9 15.4 %collective-permute-start.14 = (bf16[16,128,128]{2,1,0:T(8,128)(2,1)S(1)}, bf16[16,128,128]{2,1,0:T(8,128)(2,1)S(1)}, u32[]{:S(2)}, u32[]{:S(2)}) collective-permute-start(bf16[16,128,128]{2,1,0:T(8,128)(2,1)S(1)} %get-tuple-element.50.after.refs_2_), channel_id=1, source_target_pairs={{48,16},{80,48},{112,80},{0,32},{32,64},{64,96},{49,17},{81,49},{1... | collective-permute-start | bytes 1572872 | tf_op jit(solution)/shard_map/ppermute | solution.py:49
  56.8 7.6 %collective-permute-start.13 = (bf16[8,128,128]{2,1,0:T(8,128)(2,1)S(1)}, bf16[8,128,128]{2,1,0:T(8,128)(2,1)S(1)}, u32[]{:S(2)}, u32[]{:S(2)}) collective-permute-start(bf16[8,128,128]{2,1,0:T(8,128)(2,1)S(1)} %get-tuple-element.47), channel_id=1, source_target_pairs={{0,16},{16,0},{32,48},{48,32},{64,80},{80,64},{96,112},{112,96},{1... | collective-permute-start | bytes 786440 | tf_op jit(solution)/shard_map/ppermute | solution.py:38
  72.2 5.3 %collective-permute-start.18 = (bf16[16,128,128]{2,1,0:T(8,128)(2,1)S(1)}, bf16[16,128,128]{2,1,0:T(8,128)(2,1)S(1)}, u32[]{:S(2)}, u32[]{:S(2)}) collective-permute-start(bf16[16,128,128]{2,1,0:T(8,128)(2,1)S(1)} %get-tuple-element.55.after.refs_14_.refs_0_.refs_5_), channel_id=1, source_target_pairs={{0,1},{1,0},{2,3},{3,2},{4,5},{5,4},{6,7},{7,6},{8,9},{9,8},{10,11... | collective-permute-start | bytes 1572872 | tf_op jit(solution)/shard_map/ppermute | solution.py:54
  72.3 14.3 %collective-permute-start.16 = (bf16[16,128,128]{2,1,0:T(8,128)(2,1)S(1)}, bf16[16,128,128]{2,1,0:T(8,128)(2,1)S(1)}, u32[]{:S(2)}, u32[]{:S(2)}) collective-permute-start(bf16[16,128,128]{2,1,0:T(8,128)(2,1)S(1)} %get-tuple-element.55.after.refs_14_.refs_0_.refs_5_), channel_id=1, source_target_pairs={{0,16},{16,0},{32,48},{48,32},{64,80},{80,64},{96,112},{112,96},{1... | collective-permute-start | bytes 1572872 | tf_op jit(solution)/shard_map/ppermute | solution.py:38
  78.7 11.6 %collective-permute-start.20 = (bf16[4,256,128]{2,1,0:T(8,128)(2,1)S(1)}, bf16[4,256,128]{2,1,0:T(8,128)(2,1)S(1)}, u32[]{:S(2)}, u32[]{:S(2)}) collective-permute-start(bf16[4,256,128]{2,1,0:T(8,128)(2,1)S(1)} %get-tuple-element.59), channel_id=1, source_target_pairs={{0,32},{16,48},{32,64},{48,80},{64,96},{80,112},{96,0},{112,16},{1... | collective-permute-start | bytes 786440 | tf_op jit(solution)/shard_map/ppermute | solution.py:43
  80.0 10.3 %collective-permute-start.21 = (bf16[4,256,128]{2,1,0:T(8,128)(2,1)S(1)}, bf16[4,256,128]{2,1,0:T(8,128)(2,1)S(1)}, u32[]{:S(2)}, u32[]{:S(2)}) collective-permute-start(bf16[4,256,128]{2,1,0:T(8,128)(2,1)S(1)} %get-tuple-element.60), channel_id=1, source_target_pairs={{0,96},{16,112},{32,0},{48,16},{64,32},{80,48},{96,64},{112,80},{1... | collective-permute-start | bytes 786440 | tf_op jit(solution)/shard_map/ppermute | solution.py:43
  80.8 13.1 %collective-permute-start.22 = (bf16[4,256,128]{2,1,0:T(8,128)(2,1)S(1)}, bf16[4,256,128]{2,1,0:T(8,128)(2,1)S(1)}, u32[]{:S(2)}, u32[]{:S(2)}) collective-permute-start(bf16[4,256,128]{2,1,0:T(8,128)(2,1)S(1)} %get-tuple-element.61), channel_id=1, source_target_pairs={{0,64},{16,80},{32,96},{48,112},{64,0},{80,16},{96,32},{112,48},{1... | collective-permute-start | bytes 786440 | tf_op jit(solution)/shard_map/ppermute | solution.py:43
  82.0 22.4 %collective-permute-start.19 = (bf16[16,128,128]{2,1,0:T(8,128)(2,1)S(1)}, bf16[16,128,128]{2,1,0:T(8,128)(2,1)S(1)}, u32[]{:S(2)}, u32[]{:S(2)}) collective-permute-start(bf16[16,128,128]{2,1,0:T(8,128)(2,1)S(1)} %collective-permute-done.18.refs_4_.refs_11_), channel_id=1, source_target_pairs={{0,2},{2,4},{4,6},{6,8},{8,10},{10,12},{12,14},{3,1},{5,3},{7,5},{... | collective-permute-start | bytes 1572872 | tf_op jit(solution)/shard_map/ppermute | solution.py:56
  86.6 17.8 %collective-permute-start.17 = (bf16[16,128,128]{2,1,0:T(8,128)(2,1)S(1)}, bf16[16,128,128]{2,1,0:T(8,128)(2,1)S(1)}, u32[]{:S(2)}, u32[]{:S(2)}) collective-permute-start(bf16[16,128,128]{2,1,0:T(8,128)(2,1)S(1)} %collective-permute-done.16.refs_2_.refs_4_), channel_id=1, source_target_pairs={{48,16},{80,48},{112,80},{0,32},{32,64},{64,96},{49,17},{81,49},{1... | collective-permute-start | bytes 1572872 | tf_op jit(solution)/shard_map/ppermute | solution.py:49
  94.7 16.7 %collective-permute-start.23 = (bf16[8,256,128]{2,1,0:T(8,128)(2,1)S(1)}, bf16[8,256,128]{2,1,0:T(8,128)(2,1)S(1)}, u32[]{:S(2)}, u32[]{:S(2)}) collective-permute-start(bf16[8,256,128]{2,1,0:T(8,128)(2,1)S(1)} %turned.5), channel_id=1, source_target_pairs={{0,16},{16,0},{32,48},{48,32},{64,80},{80,64},{96,112},{112,96},{1... | collective-permute-start | bytes 1572872 | tf_op jit(solution)/shard_map/ppermute | solution.py:38

commit v4 on v3

--- a/solution.py
+++ b/solution.py
@@ -239,7 +239,7 @@
     return pl.pallas_call(
         functools.partial(respond_kernel, power),
         out_shape=[jax.ShapeDtypeStruct((2 * cap, height, cells), BF16)] * len(TURNS),
-        in_specs=[spec(SMEM), spec(VMEM), spec(VMEM), spec(pl.ANY)],
+        in_specs=[spec(SMEM), spec(VMEM), spec(VMEM), spec(VMEM)],
         out_specs=[spec(VMEM)] * len(TURNS),
         compiler_params=params(8),
         cost_estimate=cost(1),
@@ -409,7 +409,7 @@
     parts, (field, exports, pool, sems) = refs[:-4], refs[-4:]
     fill_pool(parts, pool, sems)
 
-    @pl.loop(0, exports.shape[0], unroll=8)
+    @pl.loop(0, exports.shape[0], unroll=16)
     def _(i):
         value = base[i] - 0.5 * interior(pool, index, order, tiles, i)
         field[i] = value
@@ -440,7 +440,7 @@
     count = others.shape[0]
     exports = order.shape[0] - count
 
-    @pl.loop(0, count, unroll=8)
+    @pl.loop(0, count, unroll=12)
     def _(i):
         value = base[i + exports] - 0.5 * interior(pool, index, order, tiles, i + exports)
         field[i] = value
@@ -471,7 +471,7 @@
     def copy(i):
         return pltpu.make_async_copy(fresh.at[i], out.at[order[i]], out_sems.at[i])
 
-    @pl.loop(0, count, unroll=8)
+    @pl.loop(0, count, unroll=20)
     def _(i):
         fresh[i] = base[i] - 0.5 * interior(pool, index, order, tiles, i)
         copy(i).start()

time: 115 us -> 114 us (level)
  no operation moved by 1% of the time
where the time goes in v4:
time: 114 us; the launch traced here: 113 us
  starting transfers between devices  42.7 us (37%)
  Pallas kernels  36.2 us (32%)
  waiting for transfers between devices  31.1 us (27%)
  local copies, waits for them, and re-layouts  1.89 us (2%)
    ppermute x6, waiting for transfers between devices, other_x(): return lax.ppermute(value, 'gx', [(i, i ^ 1) for i in range(count)])  12.7 us
    ppermute x3, waiting for transfers between devices, passed_on(): return lax.ppermute(across, 'gx', on)  12.5 us
    ppermute x3, starting transfers between devices, beside_of(): return (other_x(exports), core, lax.ppermute(core, 'gy', on))  11.5 us
    ppermute x9, starting transfers between devices, along_y(): lax.ppermute(value, 'gx', [(i, (i + 2 * steps) % count) for i in range(co...  11.2 us
    ppermute x6, starting transfers between devices, other_x(): return lax.ppermute(value, 'gx', [(i, i ^ 1) for i in range(count)])  11 us
    ppermute x3, starting transfers between devices, passed_on(): return lax.ppermute(across, 'gx', on)  8.53 us
    pallas_call x2, Pallas kernels, other_blocks(): pl.pallas_call(other_kernel, out_shape=(jax.ShapeDtypeStruct((count, rows...  6.94 us
    pallas_call x2, Pallas kernels, first_blocks(): pl.pallas_call(first_kernel, out_shape=(jax.ShapeDtypeStruct((exports, ro...  6.52 us
  transfers between devices with their start and end apart: 24, of which 12 were waited for; matrix products, arithmetic and copies ran while one was open for 0% of the time, Pallas kernels for 22%

profile of v4, /device:TPU:40, one launch (start us, length us, event | category | flops | bytes accessed | tf_op | source)
XLA Modules:
  0.0 113.1 jit_solution(7911854970856791769)
XLA Ops:
  0.7 3.0 %exports.1.refs_5_.refs_0_.refs_14_.refs_18_.refs_9_ = bf16[16,128,128]{2,1,0:T(8,128)(2,1)} custom-call(s32[16]{0:T(128)} %ids.3, f32[40,128,128]{2,1,0:T(8,128)} %pressure.9), custom_call_target="tpu_custom_call" | custom-call | flops 3000000000 | tf_op jit(solution)/shard_map/exports/pallas_call | solution.py:131
  3.7 0.0 copy-start.1
  3.7 0.1 collective-permute-start
  3.8 1.6 %collective-permute-start.4 = (bf16[16,128,128]{2,1,0:T(8,128)(2,1)}, bf16[16,128,128]{2,1,0:T(8,128)(2,1)S(1)}, u32[]{:S(2)}, u32[]{:S(2)}) collective-permute-start(bf16[16,128,128]{2,1,0:T(8,128)(2,1)} %exports.1.refs_5_.refs_0_.refs_14_.refs_18_.refs_9_), channel_id=1, source_target_pairs={{0,16},{16,0},{32,48},{48,32},{64,80},{80,64},{96,112},{112,96},{1... | collective-permute-start | bytes 1572872 | tf_op jit(solution)/shard_map/ppermute | solution.py:38
  5.4 0.1 reshape.35
  5.5 0.1 reshape.33
  5.6 0.1 reshape.32
  5.6 0.1 pad_maximum_fusion.table
  5.7 0.3 collective-permute-done.after.refs_4_
  6.1 1.6 %copy-done.3 = f32[1,1,8,2,2,128,128]{6,5,4,3,2,1,0:T(8,128)S(1)} copy-done((f32[1,1,8,2,2,128,128]{6,5,4,3,2,1,0:T(8,128)S(1)}, f32[1,1,8,2,2,128,128]{6,5,4,3,2,1,0:T(8,128)}, u32[]{:S(2)}) %copy-start.3) | copy-done | bytes 2097176
  7.6 1.4 %responses_1.1 = (bf16[4,144,128]{2,1,0:T(8,128)(2,1)S(1)}, bf16[4,144,128]{2,1,0:T(8,128)(2,1)S(1)}, bf16[4,144,128]{2,1,0:T(8,128)(2,1)S(1)}, bf16[4,144,128]{2,1,0:T(8,128)(2,1)S(1)}) custom-call(f32[96]{0:T(128)S(1)} %pad_maximum_fusion.table, f32[16,2,128,128]{3,2,1,0:T(8,128)S(1)} %bitcast.20, f32[16,1,128]{2,1,0:T(1,128)S(1)} %bitcast.30, ...), custom_call_target="tpu_custom_call" | custom-call | flops 1000000000 | tf_op jit(solution)/shard_map/responses_1/pallas_call | solution.py:239
  9.0 1.6 %collective-permute-start.1 = (bf16[4,144,128]{2,1,0:T(8,128)(2,1)S(1)}, bf16[4,144,128]{2,1,0:T(8,128)(2,1)S(1)}, u32[]{:S(2)}, u32[]{:S(2)}) collective-permute-start(bf16[4,144,128]{2,1,0:T(8,128)(2,1)S(1)} %get-tuple-element.33), channel_id=1, source_target_pairs={{0,32},{16,48},{32,64},{48,80},{64,96},{80,112},{96,0},{112,16},{1... | collective-permute-start | bytes 442376 | tf_op jit(solution)/shard_map/ppermute | solution.py:43
  10.7 0.5 collective-permute-start.2
  11.1 2.3 %collective-permute-start.3 = (bf16[4,144,128]{2,1,0:T(8,128)(2,1)S(1)}, bf16[4,144,128]{2,1,0:T(8,128)(2,1)S(1)}, u32[]{:S(2)}, u32[]{:S(2)}) collective-permute-start(bf16[4,144,128]{2,1,0:T(8,128)(2,1)S(1)} %get-tuple-element.35), channel_id=1, source_target_pairs={{0,64},{16,80},{32,96},{48,112},{64,0},{80,16},{96,32},{112,48},{1... | collective-permute-start | bytes 442376 | tf_op jit(solution)/shard_map/ppermute | solution.py:43
  13.4 3.8 %collective-permute-start.7 = (bf16[16,128,128]{2,1,0:T(8,128)(2,1)}, bf16[16,128,128]{2,1,0:T(8,128)(2,1)S(1)}, u32[]{:S(2)}, u32[]{:S(2)}) collective-permute-start(bf16[16,128,128]{2,1,0:T(8,128)(2,1)} %collective-permute-done.after.refs_4_), channel_id=1, source_target_pairs={{0,2},{2,4},{4,6},{6,8},{8,10},{10,12},{12,14},{3,1},{5,3},{7,5},{... | collective-permute-start | bytes 1572872 | tf_op jit(solution)/shard_map/ppermute | solution.py:56
  17.3 1.1 collective-permute-done.4.refs_4_
  18.4 0.0 collective-permute-done.1.refs_1_
  18.4 0.0 collective-permute-done.2.refs_2_
  18.4 1.8 %collective-permute-done.3.refs_3_ = bf16[4,144,128]{2,1,0:T(8,128)(2,1)S(1)} collective-permute-done((bf16[4,144,128]{2,1,0:T(8,128)(2,1)S(1)}, bf16[4,144,128]{2,1,0:T(8,128)(2,1)S(1)}, u32[]{:S(2)}, u32[]{:S(2)}) %collective-permute-start.3) | collective-permute-done | bytes 147488 | tf_op jit(solution)/shard_map/ppermute | solution.py:43
  20.2 0.4 turned.3
  20.6 2.3 %collective-permute-start.6 = (bf16[16,128,128]{2,1,0:T(8,128)(2,1)S(1)}, bf16[16,128,128]{2,1,0:T(8,128)(2,1)S(1)}, u32[]{:S(2)}, u32[]{:S(2)}) collective-permute-start(bf16[16,128,128]{2,1,0:T(8,128)(2,1)S(1)} %get-tuple-element.36.after.refs_2_), channel_id=1, source_target_pairs={{48,16},{80,48},{112,80},{0,32},{32,64},{64,96},{49,17},{81,49},{1... | collective-permute-start | bytes 1572872 | tf_op jit(solution)/shard_map/ppermute | solution.py:49
  22.9 2.4 %collective-permute-start.5 = (bf16[8,144,128]{2,1,0:T(8,128)(2,1)S(1)}, bf16[8,144,128]{2,1,0:T(8,128)(2,1)S(1)}, u32[]{:S(2)}, u32[]{:S(2)}) collective-permute-start(bf16[8,144,128]{2,1,0:T(8,128)(2,1)S(1)} %get-tuple-element.40), channel_id=1, source_target_pairs={{0,16},{16,0},{32,48},{48,32},{64,80},{80,64},{96,112},{112,96},{1... | collective-permute-start | bytes 884744 | tf_op jit(solution)/shard_map/ppermute | solution.py:38
  25.4 2.1 %prepare.1 = (s32[40]{0:T(128)S(1)}, s32[12,40]{1,0:T(8,128)S(1)}, s32[2,8]{1,0:T(2,128)S(1)}, bf16[24,128,128]{2,1,0:T(8,128)(2,1)S(1)}) custom-call(s32[16]{0:T(128)S(1)} %copy-done.12, s32[12,40]{1,0:T(8,128)S(1)} %bitcast.28, s32[12,40]{1,0:T(8,128)S(1)} %bitcast.29, s32[2,8]{1,0:T(2,128)S(1)} %bitcast.32, f32[40,128,128]{2,1,0:T(8,128)S(1)} %copy-done.1, ...), custom_call_target="tpu_custom_call" | custom-call | flops 2100000000 | tf_op jit(solution)/shard_map/prepare/pallas_call | solution.py:185
  27.5 4.0 %collective-permute-done.5.refs_4_ = bf16[8,144,128]{2,1,0:T(8,128)(2,1)S(1)} collective-permute-done((bf16[8,144,128]{2,1,0:T(8,128)(2,1)S(1)}, bf16[8,144,128]{2,1,0:T(8,128)(2,1)S(1)}, u32[]{:S(2)}, u32[]{:S(2)}) %collective-permute-start.5) | collective-permute-done | bytes 294944 | tf_op jit(solution)/shard_map/ppermute | solution.py:38
  31.6 1.3 %base_1.1.base = f32[40,128,128]{2,1,0:T(8,128)S(1)} custom-call(s32[2,8]{1,0:T(2,128)S(1)} %get-tuple-element.39.wall_at, s32[40]{0:T(128)S(1)} %get-tuple-element.37.order, f32[40,128,128]{2,1,0:T(8,128)S(1)} %copy-done.1, bf16[4,144,128]{2,1,0:T(8,128)(2,1)S(1)} %get-tuple-element.32.refs_0_, bf16[4,144,128]{2,1,0:T(8,128)(2,1)S(1)} %collective-permute-done.1.refs_1_, ...), custom_call_target="tpu_custom_call" | custom-call | flops 1600000000 | tf_op jit(solution)/shard_map/base_1/pallas_call | solution.py:310
  32.8 0.0 collective-permute-done.7.refs_5_
  32.8 2.8 %collective-permute-done.6.refs_3_ = bf16[16,128,128]{2,1,0:T(8,128)(2,1)S(1)} collective-permute-done((bf16[16,128,128]{2,1,0:T(8,128)(2,1)S(1)}, bf16[16,128,128]{2,1,0:T(8,128)(2,1)S(1)}, u32[]{:S(2)}, u32[]{:S(2)}) %collective-permute-start.6) | collective-permute-done | bytes 524320 | tf_op jit(solution)/shard_map/ppermute | solution.py:49
  35.7 3.7 %exports_1.1 = (f32[16,128,128]{2,1,0:T(8,128)S(1)}, bf16[16,128,128]{2,1,0:T(8,128)(2,1)S(1)}, bf16[104,128,128]{2,1,0:T(8,128)(2,1)S(1)}) custom-call(s32[40]{0:T(128)S(1)} %get-tuple-element.37.order, s32[12,40]{1,0:T(8,128)S(1)} %get-tuple-element.38.index, bf16[40,1536,128]{2,1,0:T(8,128)(2,1)S(1)} %bitcast.15, f32[40,128,128]{2,1,0:T(8,128)S(1)} %base_1.1.base, ...), custom_call_target="tpu_custom_call" | custom-call | flops 3100000000 | tf_op jit(solution)/shard_map/exports_1/pallas_call | solution.py:422
  39.4 0.1 collective-permute-start.8
  39.5 1.6 %collective-permute-start.12 = (bf16[16,128,128]{2,1,0:T(8,128)(2,1)S(1)}, bf16[16,128,128]{2,1,0:T(8,128)(2,1)S(1)}, u32[]{:S(2)}, u32[]{:S(2)}) collective-permute-start(bf16[16,128,128]{2,1,0:T(8,128)(2,1)S(1)} %get-tuple-element.42.refs_12_.refs_0_.refs_16_.refs_7_), channel_id=1, source_target_pairs={{0,16},{16,0},{32,48},{48,32},{64,80},{80,64},{96,112},{112,96},{1... | collective-permute-start | bytes 1572872 | tf_op jit(solution)/shard_map/ppermute | solution.py:38
  41.1 0.3 collective-permute-done.8.after.refs_4_
  41.4 0.8 responses_2.1
  42.2 0.5 collective-permute-start.9
  42.8 1.6 %collective-permute-start.10 = (bf16[4,128,128]{2,1,0:T(8,128)(2,1)S(1)}, bf16[4,128,128]{2,1,0:T(8,128)(2,1)S(1)}, u32[]{:S(2)}, u32[]{:S(2)}) collective-permute-start(bf16[4,128,128]{2,1,0:T(8,128)(2,1)S(1)} %get-tuple-element.45), channel_id=1, source_target_pairs={{0,96},{16,112},{32,0},{48,16},{64,32},{80,48},{96,64},{112,80},{1... | collective-permute-start | bytes 393224 | tf_op jit(solution)/shard_map/ppermute | solution.py:43
  44.3 1.2 %collective-permute-start.11 = (bf16[4,128,128]{2,1,0:T(8,128)(2,1)S(1)}, bf16[4,128,128]{2,1,0:T(8,128)(2,1)S(1)}, u32[]{:S(2)}, u32[]{:S(2)}) collective-permute-start(bf16[4,128,128]{2,1,0:T(8,128)(2,1)S(1)} %get-tuple-element.46), channel_id=1, source_target_pairs={{0,64},{16,80},{32,96},{48,112},{64,0},{80,16},{96,32},{112,48},{1... | collective-permute-start | bytes 393224 | tf_op jit(solution)/shard_map/ppermute | solution.py:43
  45.6 3.8 %collective-permute-start.15 = (bf16[16,128,128]{2,1,0:T(8,128)(2,1)S(1)}, bf16[16,128,128]{2,1,0:T(8,128)(2,1)S(1)}, u32[]{:S(2)}, u32[]{:S(2)}) collective-permute-start(bf16[16,128,128]{2,1,0:T(8,128)(2,1)S(1)} %collective-permute-done.8.after.refs_4_), channel_id=1, source_target_pairs={{0,2},{2,4},{4,6},{6,8},{8,10},{10,12},{12,14},{3,1},{5,3},{7,5},{... | collective-permute-start | bytes 1572872 | tf_op jit(solution)/shard_map/ppermute | solution.py:56
  49.4 4.5 %collective-permute-done.12.refs_4_ = bf16[16,128,128]{2,1,0:T(8,128)(2,1)S(1)} collective-permute-done((bf16[16,128,128]{2,1,0:T(8,128)(2,1)S(1)}, bf16[16,128,128]{2,1,0:T(8,128)(2,1)S(1)}, u32[]{:S(2)}, u32[]{:S(2)}) %collective-permute-start.12) | collective-permute-done | bytes 524320 | tf_op jit(solution)/shard_map/ppermute | solution.py:38
  53.9 0.0 collective-permute-done.9.refs_1_.refs_6_
  53.9 0.4 turned.4
  54.3 2.4 %collective-permute-start.14 = (bf16[16,128,128]{2,1,0:T(8,128)(2,1)S(1)}, bf16[16,128,128]{2,1,0:T(8,128)(2,1)S(1)}, u32[]{:S(2)}, u32[]{:S(2)}) collective-permute-start(bf16[16,128,128]{2,1,0:T(8,128)(2,1)S(1)} %get-tuple-element.50.after.refs_2_), channel_id=1, source_target_pairs={{48,16},{80,48},{112,80},{0,32},{32,64},{64,96},{49,17},{81,49},{1... | collective-permute-start | bytes 1572872 | tf_op jit(solution)/shard_map/ppermute | solution.py:49
  56.6 2.3 %collective-permute-start.13 = (bf16[8,128,128]{2,1,0:T(8,128)(2,1)S(1)}, bf16[8,128,128]{2,1,0:T(8,128)(2,1)S(1)}, u32[]{:S(2)}, u32[]{:S(2)}) collective-permute-start(bf16[8,128,128]{2,1,0:T(8,128)(2,1)S(1)} %get-tuple-element.47), channel_id=1, source_target_pairs={{0,16},{16,0},{32,48},{48,32},{64,80},{80,64},{96,112},{112,96},{1... | collective-permute-start | bytes 786440 | tf_op jit(solution)/shard_map/ppermute | solution.py:38
  59.0 3.5 %others_1.1 = (f32[24,128,128]{2,1,0:T(8,128)S(1)}, bf16[24,128,128]{2,1,0:T(8,128)(2,1)S(1)}) custom-call(s32[40]{0:T(128)S(1)} %get-tuple-element.37.order, s32[12,40]{1,0:T(8,128)S(1)} %get-tuple-element.38.index, bf16[40,1536,128]{2,1,0:T(8,128)(2,1)S(1)} %bitcast.16, f32[40,128,128]{2,1,0:T(8,128)S(1)} %base_1.1.base, ...), custom_call_target="tpu_custom_call" | custom-call | tf_op jit(solution)/shard_map/others_1/pallas_call | solution.py:452
  62.4 2.4 %collective-permute-done.13.refs_9_ = bf16[8,128,128]{2,1,0:T(8,128)(2,1)S(1)} collective-permute-done((bf16[8,128,128]{2,1,0:T(8,128)(2,1)S(1)}, bf16[8,128,128]{2,1,0:T(8,128)(2,1)S(1)}, u32[]{:S(2)}, u32[]{:S(2)}) %collective-permute-start.13) | collective-permute-done | bytes 262176 | tf_op jit(solution)/shard_map/ppermute | solution.py:38
  64.8 1.4 %base_2.1.base = f32[40,128,128]{2,1,0:T(8,128)S(1)} custom-call(s32[2,8]{1,0:T(2,128)S(1)} %get-tuple-element.39.wall_at, s32[40]{0:T(128)S(1)} %get-tuple-element.37.order, f32[40,128,128]{2,1,0:T(8,128)S(1)} %copy-done.1, bf16[4,144,128]{2,1,0:T(8,128)(2,1)S(1)} %get-tuple-element.32.refs_0_, bf16[4,144,128]{2,1,0:T(8,128)(2,1)S(1)} %collective-permute-done.1.refs_1_, ...), custom_call_target="tpu_custom_call" | custom-call | tf_op jit(solution)/shard_map/base_2/pallas_call | solution.py:310
  66.2 3.4 %collective-permute-done.14.refs_3_ = bf16[16,128,128]{2,1,0:T(8,128)(2,1)S(1)} collective-permute-done((bf16[16,128,128]{2,1,0:T(8,128)(2,1)S(1)}, bf16[16,128,128]{2,1,0:T(8,128)(2,1)S(1)}, u32[]{:S(2)}, u32[]{:S(2)}) %collective-permute-start.14) | collective-permute-done | bytes 524320 | tf_op jit(solution)/shard_map/ppermute | solution.py:49
  69.6 2.8 %exports_2.1 = (f32[16,128,128]{2,1,0:T(8,128)S(1)}, bf16[16,128,128]{2,1,0:T(8,128)(2,1)S(1)}, bf16[104,128,128]{2,1,0:T(8,128)(2,1)S(1)}) custom-call(s32[40]{0:T(128)S(1)} %get-tuple-element.37.order, s32[12,40]{1,0:T(8,128)S(1)} %get-tuple-element.38.index, bf16[40,1536,128]{2,1,0:T(8,128)(2,1)S(1)} %bitcast.17, f32[40,128,128]{2,1,0:T(8,128)S(1)} %base_2.1.base, ...), custom_call_target="tpu_custom_call" | custom-call | flops 3100000000 | tf_op jit(solution)/shard_map/exports_2/pallas_call | solution.py:422
  72.4 0.3 collective-permute-start.18
  72.7 1.6 %collective-permute-start.16 = (bf16[16,128,128]{2,1,0:T(8,128)(2,1)S(1)}, bf16[16,128,128]{2,1,0:T(8,128)(2,1)S(1)}, u32[]{:S(2)}, u32[]{:S(2)}) collective-permute-start(bf16[16,128,128]{2,1,0:T(8,128)(2,1)S(1)} %get-tuple-element.55.after.refs_14_.refs_0_.refs_5_), channel_id=1, source_target_pairs={{0,16},{16,0},{32,48},{48,32},{64,80},{80,64},{96,112},{112,96},{1... | collective-permute-start | bytes 1572872 | tf_op jit(solution)/shard_map/ppermute | solution.py:38
  74.3 3.5 %others_2.1 = (f32[24,128,128]{2,1,0:T(8,128)S(1)}, bf16[24,128,128]{2,1,0:T(8,128)(2,1)S(1)}) custom-call(s32[40]{0:T(128)S(1)} %get-tuple-element.37.order, s32[12,40]{1,0:T(8,128)S(1)} %get-tuple-element.38.index, bf16[40,1536,128]{2,1,0:T(8,128)(2,1)S(1)} %bitcast.18, f32[40,128,128]{2,1,0:T(8,128)S(1)} %base_2.1.base, ...), custom_call_target="tpu_custom_call" | custom-call | tf_op jit(solution)/shard_map/others_2/pallas_call | solution.py:452
  77.8 1.2 %walls.1 = (bf16[4,256,128]{2,1,0:T(8,128)(2,1)S(1)}, bf16[4,256,128]{2,1,0:T(8,128)(2,1)S(1)}, bf16[4,256,128]{2,1,0:T(8,128)(2,1)S(1)}, bf16[4,256,128]{2,1,0:T(8,128)(2,1)S(1)}) custom-call(s32[2,8]{1,0:T(2,128)S(1)} %get-tuple-element.39.wall_at, bf16[4,144,128]{2,1,0:T(8,128)(2,1)S(1)} %get-tuple-element.32.refs_0_, ...), custom_call_target="tpu_custom_call" | custom-call | tf_op jit(solution)/shard_map/walls/pallas_call | solution.py:347
  78.9 0.4 collective-permute-start.20
  79.4 1.7 %collective-permute-start.21 = (bf16[4,256,128]{2,1,0:T(8,128)(2,1)S(1)}, bf16[4,256,128]{2,1,0:T(8,128)(2,1)S(1)}, u32[]{:S(2)}, u32[]{:S(2)}) collective-permute-start(bf16[4,256,128]{2,1,0:T(8,128)(2,1)S(1)} %get-tuple-element.60), channel_id=1, source_target_pairs={{0,96},{16,112},{32,0},{48,16},{64,32},{80,48},{96,64},{112,80},{1... | collective-permute-start | bytes 786440 | tf_op jit(solution)/shard_map/ppermute | solution.py:43
  81.0 1.4 %collective-permute-start.22 = (bf16[4,256,128]{2,1,0:T(8,128)(2,1)S(1)}, bf16[4,256,128]{2,1,0:T(8,128)(2,1)S(1)}, u32[]{:S(2)}, u32[]{:S(2)}) collective-permute-start(bf16[4,256,128]{2,1,0:T(8,128)(2,1)S(1)} %get-tuple-element.61), channel_id=1, source_target_pairs={{0,64},{16,80},{32,96},{48,112},{64,0},{80,16},{96,32},{112,48},{1... | collective-permute-start | bytes 786440 | tf_op jit(solution)/shard_map/ppermute | solution.py:43
  82.4 3.9 %collective-permute-start.19 = (bf16[16,128,128]{2,1,0:T(8,128)(2,1)S(1)}, bf16[16,128,128]{2,1,0:T(8,128)(2,1)S(1)}, u32[]{:S(2)}, u32[]{:S(2)}) collective-permute-start(bf16[16,128,128]{2,1,0:T(8,128)(2,1)S(1)} %collective-permute-done.18.refs_4_.refs_11_), channel_id=1, source_target_pairs={{0,2},{2,4},{4,6},{6,8},{8,10},{10,12},{12,14},{3,1},{5,3},{7,5},{... | collective-permute-start | bytes 1572872 | tf_op jit(solution)/shard_map/ppermute | solution.py:56
  86.3 0.7 collective-permute-done.16.refs_2_.refs_4_
  87.0 3.8 %collective-permute-start.17 = (bf16[16,128,128]{2,1,0:T(8,128)(2,1)S(1)}, bf16[16,128,128]{2,1,0:T(8,128)(2,1)S(1)}, u32[]{:S(2)}, u32[]{:S(2)}) collective-permute-start(bf16[16,128,128]{2,1,0:T(8,128)(2,1)S(1)} %collective-permute-done.16.refs_2_.refs_4_), channel_id=1, source_target_pairs={{48,16},{80,48},{112,80},{0,32},{32,64},{64,96},{49,17},{81,49},{1... | collective-permute-start | bytes 1572872 | tf_op jit(solution)/shard_map/ppermute | solution.py:49
  90.9 3.4 %collective-permute-done.22.refs_3_ = bf16[4,256,128]{2,1,0:T(8,128)(2,1)S(1)} collective-permute-done((bf16[4,256,128]{2,1,0:T(8,128)(2,1)S(1)}, bf16[4,256,128]{2,1,0:T(8,128)(2,1)S(1)}, u32[]{:S(2)}, u32[]{:S(2)}) %collective-permute-start.22) | collective-permute-done | bytes 262176 | tf_op jit(solution)/shard_map/ppermute | solution.py:43
  94.3 0.7 turned.5
  95.0 1.5 %collective-permute-start.23 = (bf16[8,256,128]{2,1,0:T(8,128)(2,1)S(1)}, bf16[8,256,128]{2,1,0:T(8,128)(2,1)S(1)}, u32[]{:S(2)}, u32[]{:S(2)}) collective-permute-start(bf16[8,256,128]{2,1,0:T(8,128)(2,1)S(1)} %turned.5), channel_id=1, source_target_pairs={{0,16},{16,0},{32,48},{48,32},{64,80},{80,64},{96,112},{112,96},{1... | collective-permute-start | bytes 1572872 | tf_op jit(solution)/shard_map/ppermute | solution.py:38
  96.5 1.5 %base_3.1.base = f32[40,128,128]{2,1,0:T(8,128)S(1)} custom-call(s32[2,8]{1,0:T(2,128)S(1)} %get-tuple-element.39.wall_at, s32[40]{0:T(128)S(1)} %get-tuple-element.37.order, f32[40,128,128]{2,1,0:T(8,128)S(1)} %copy-done.1, bf16[4,144,128]{2,1,0:T(8,128)(2,1)S(1)} %get-tuple-element.32.refs_0_, bf16[4,144,128]{2,1,0:T(8,128)(2,1)S(1)} %collective-permute-done.1.refs_1_, ...), custom_call_target="tpu_custom_call" | custom-call | tf_op jit(solution)/shard_map/base_3/pallas_call | solution.py:310
  98.0 6.3 %collective-permute-done.17.refs_3_ = bf16[16,128,128]{2,1,0:T(8,128)(2,1)S(1)} collective-permute-done((bf16[16,128,128]{2,1,0:T(8,128)(2,1)S(1)}, bf16[16,128,128]{2,1,0:T(8,128)(2,1)S(1)}, u32[]{:S(2)}, u32[]{:S(2)}) %collective-permute-start.17) | collective-permute-done | bytes 524320 | tf_op jit(solution)/shard_map/ppermute | solution.py:49
  104.3 0.0 collective-permute-done.19.refs_5_
  104.3 6.5 %last.1 = f32[40,128,128]{2,1,0:T(8,128)} custom-call(s32[40]{0:T(128)S(1)} %get-tuple-element.37.order, s32[12,40]{1,0:T(8,128)S(1)} %get-tuple-element.38.index, bf16[40,1536,128]{2,1,0:T(8,128)(2,1)S(1)} %bitcast.19, f32[40,128,128]{2,1,0:T(8,128)S(1)} %base_3.1.base, bf16[16,128,128]{2,1,0:T(8,128)(2,1)S(1)} %get-tuple-element.55.after.refs_14_.refs_0_.refs_5_, ...), custom_call_target="tpu_custom_call" | custom-call | tf_op jit(solution)/shard_map/last/pallas_call | solution.py:486
  110.8 2.1 %states_after.1 = f32[16,2,128,128]{3,2,1,0:T(8,128)} custom-call(s32[2,8]{1,0:T(2,128)S(1)} %bitcast.23, f32[2,16]{1,0:T(2,128)S(1)} %bitcast.27, f32[2,16]{1,0:T(2,128)S(1)} %bitcast.25, f32[16,2,128,128]{3,2,1,0:T(8,128)S(1)} %bitcast.22, bf16[4,256,128]{2,1,0:T(8,128)(2,1)S(1)} %get-tuple-element.58.refs_0_, ...), custom_call_target="tpu_custom_call" | custom-call | tf_op jit(solution)/shard_map/states_after/pallas_call | solution.py:378
  (34 shorter events, 0.1 us)
Async XLA Ops:
  0.6 4.7 %copy-start.5 = (s32[1,1,8,2]{2,3,1,0:T(2,128)S(1)}, s32[1,1,8,2]{2,3,1,0:T(2,128)}, u32[]{:S(2)}) copy-start(s32[1,1,8,2]{2,3,1,0:T(2,128)} %param.19) | copy-start | bytes 196
  0.6 4.8 %copy-start.6 = (f32[16,2]{0,1:T(2,128)S(1)}, f32[16,2]{0,1:T(2,128)}, u32[]{:S(2)}) copy-start(f32[16,2]{0,1:T(2,128)} %param.22) | copy-start | bytes 388
  0.7 4.9 %copy-start.7 = (f32[16,2]{0,1:T(2,128)S(1)}, f32[16,2]{0,1:T(2,128)}, u32[]{:S(2)}) copy-start(f32[16,2]{0,1:T(2,128)} %param.21) | copy-start | bytes 388
  0.7 5.0 %copy-start.13 = (f32[16]{0:T(128)S(1)}, f32[16]{0:T(128)}, u32[]{:S(2)}) copy-start(f32[16]{0:T(128)} %param.23) | copy-start | bytes 196
  0.7 5.4 %copy-start.10 = (f32[1,1,8,2,128]{4,3,2,1,0:T(2,128)S(1)}, f32[1,1,8,2,128]{4,3,2,1,0:T(2,128)}, u32[]{:S(2)}) copy-start(f32[1,1,8,2,128]{4,3,2,1,0:T(2,128)} %param.18) | copy-start | bytes 24580
  0.7 24.7 %copy-start.8 = (s32[40,12]{0,1:T(8,128)S(1)}, s32[40,12]{0,1:T(8,128)}, u32[]{:S(2)}) copy-start(s32[40,12]{0,1:T(8,128)} %param.14) | copy-start | bytes 5764
  0.7 24.7 %copy-start.9 = (s32[40,12]{0,1:T(8,128)S(1)}, s32[40,12]{0,1:T(8,128)}, u32[]{:S(2)}) copy-start(s32[40,12]{0,1:T(8,128)} %param.15) | copy-start | bytes 5764
  0.7 24.7 %copy-start.11 = (s32[1,1,8,2]{2,3,1,0:T(2,128)S(1)}, s32[1,1,8,2]{2,3,1,0:T(2,128)}, u32[]{:S(2)}) copy-start(s32[1,1,8,2]{2,3,1,0:T(2,128)} %param.17) | copy-start | bytes 196
  0.7 24.6 %copy-start.12 = (s32[16]{0:T(128)S(1)}, s32[16]{0:T(128)}, u32[]{:S(2)}) copy-start(s32[16]{0:T(128)} %ids.3) | copy-start | bytes 196
  3.7 21.7 %copy-start.1 = (f32[40,128,128]{2,1,0:T(8,128)S(1)}, f32[40,128,128]{2,1,0:T(8,128)}, u32[]{:S(2)}) copy-start(f32[40,128,128]{2,1,0:T(8,128)} %pressure.9) | copy-start | bytes 7864324
  3.7 2.3 %collective-permute-start = (bf16[16,128,128]{2,1,0:T(8,128)(2,1)}, bf16[16,128,128]{2,1,0:T(8,128)(2,1)}, u32[]{:S(2)}, u32[]{:S(2)}) collective-permute-start(bf16[16,128,128]{2,1,0:T(8,128)(2,1)} %exports.1.refs_5_.refs_0_.refs_14_.refs_18_.refs_9_), channel_id=1, source_target_pairs={{0,1},{1,0},{2,3},{3,2},{4,5},{5,4},{6,7},{7,6},{8,9},{9,8},{10,11... | collective-permute-start | bytes 1572872 | tf_op jit(solution)/shard_map/ppermute | solution.py:54
  3.8 14.5 %collective-permute-start.4 = (bf16[16,128,128]{2,1,0:T(8,128)(2,1)}, bf16[16,128,128]{2,1,0:T(8,128)(2,1)S(1)}, u32[]{:S(2)}, u32[]{:S(2)}) collective-permute-start(bf16[16,128,128]{2,1,0:T(8,128)(2,1)} %exports.1.refs_5_.refs_0_.refs_14_.refs_18_.refs_9_), channel_id=1, source_target_pairs={{0,16},{16,0},{32,48},{48,32},{64,80},{80,64},{96,112},{112,96},{1... | collective-permute-start | bytes 1572872 | tf_op jit(solution)/shard_map/ppermute | solution.py:38
  6.0 1.6 %copy-start.3 = (f32[1,1,8,2,2,128,128]{6,5,4,3,2,1,0:T(8,128)S(1)}, f32[1,1,8,2,2,128,128]{6,5,4,3,2,1,0:T(8,128)}, u32[]{:S(2)}) copy-start(f32[1,1,8,2,2,128,128]{6,5,4,3,2,1,0:T(8,128)} %param.20) | copy-start | bytes 6291460
  7.6 23.9 %copy-start.2 = (bf16[16,128,128]{2,1,0:T(8,128)(2,1)S(1)}, bf16[16,128,128]{2,1,0:T(8,128)(2,1)}, u32[]{:S(2)}) copy-start(bf16[16,128,128]{2,1,0:T(8,128)(2,1)} %exports.1.refs_5_.refs_0_.refs_14_.refs_18_.refs_9_) | copy-start | bytes 1572868
  9.0 9.3 %collective-permute-start.1 = (bf16[4,144,128]{2,1,0:T(8,128)(2,1)S(1)}, bf16[4,144,128]{2,1,0:T(8,128)(2,1)S(1)}, u32[]{:S(2)}, u32[]{:S(2)}) collective-permute-start(bf16[4,144,128]{2,1,0:T(8,128)(2,1)S(1)} %get-tuple-element.33), channel_id=1, source_target_pairs={{0,32},{16,48},{32,64},{48,80},{64,96},{80,112},{96,0},{112,16},{1... | collective-permute-start | bytes 442376 | tf_op jit(solution)/shard_map/ppermute | solution.py:43
  10.7 7.7 %collective-permute-start.2 = (bf16[4,144,128]{2,1,0:T(8,128)(2,1)S(1)}, bf16[4,144,128]{2,1,0:T(8,128)(2,1)S(1)}, u32[]{:S(2)}, u32[]{:S(2)}) collective-permute-start(bf16[4,144,128]{2,1,0:T(8,128)(2,1)S(1)} %get-tuple-element.34), channel_id=1, source_target_pairs={{0,96},{16,112},{32,0},{48,16},{64,32},{80,48},{96,64},{112,80},{1... | collective-permute-start | bytes 442376 | tf_op jit(solution)/shard_map/ppermute | solution.py:43
  11.1 9.0 %collective-permute-start.3 = (bf16[4,144,128]{2,1,0:T(8,128)(2,1)S(1)}, bf16[4,144,128]{2,1,0:T(8,128)(2,1)S(1)}, u32[]{:S(2)}, u32[]{:S(2)}) collective-permute-start(bf16[4,144,128]{2,1,0:T(8,128)(2,1)S(1)} %get-tuple-element.35), channel_id=1, source_target_pairs={{0,64},{16,80},{32,96},{48,112},{64,0},{80,16},{96,32},{112,48},{1... | collective-permute-start | bytes 442376 | tf_op jit(solution)/shard_map/ppermute | solution.py:43
  13.4 19.4 %collective-permute-start.7 = (bf16[16,128,128]{2,1,0:T(8,128)(2,1)}, bf16[16,128,128]{2,1,0:T(8,128)(2,1)S(1)}, u32[]{:S(2)}, u32[]{:S(2)}) collective-permute-start(bf16[16,128,128]{2,1,0:T(8,128)(2,1)} %collective-permute-done.after.refs_4_), channel_id=1, source_target_pairs={{0,2},{2,4},{4,6},{6,8},{8,10},{10,12},{12,14},{3,1},{5,3},{7,5},{... | collective-permute-start | bytes 1572872 | tf_op jit(solution)/shard_map/ppermute | solution.py:56
  20.2 15.5 %copy-start = (bf16[40,12,128,128]{3,2,1,0:T(8,128)(2,1)S(1)}, bf16[40,12,128,128]{3,2,1,0:T(8,128)(2,1)}, u32[]{:S(2)}) copy-start(bf16[40,12,128,128]{3,2,1,0:T(8,128)(2,1)} %param.13) | copy-start | bytes 47185924
  20.6 15.1 %collective-permute-start.6 = (bf16[16,128,128]{2,1,0:T(8,128)(2,1)S(1)}, bf16[16,128,128]{2,1,0:T(8,128)(2,1)S(1)}, u32[]{:S(2)}, u32[]{:S(2)}) collective-permute-start(bf16[16,128,128]{2,1,0:T(8,128)(2,1)S(1)} %get-tuple-element.36.after.refs_2_), channel_id=1, source_target_pairs={{48,16},{80,48},{112,80},{0,32},{32,64},{64,96},{49,17},{81,49},{1... | collective-permute-start | bytes 1572872 | tf_op jit(solution)/shard_map/ppermute | solution.py:49
  22.9 8.6 %collective-permute-start.5 = (bf16[8,144,128]{2,1,0:T(8,128)(2,1)S(1)}, bf16[8,144,128]{2,1,0:T(8,128)(2,1)S(1)}, u32[]{:S(2)}, u32[]{:S(2)}) collective-permute-start(bf16[8,144,128]{2,1,0:T(8,128)(2,1)S(1)} %get-tuple-element.40), channel_id=1, source_target_pairs={{0,16},{16,0},{32,48},{48,32},{64,80},{80,64},{96,112},{112,96},{1... | collective-permute-start | bytes 884744 | tf_op jit(solution)/shard_map/ppermute | solution.py:38
  35.7 5.7 %copy-start.4 = (f32[1,1,8,2,2,128,128]{6,5,4,3,2,1,0:T(8,128)S(1)}, f32[1,1,8,2,2,128,128]{6,5,4,3,2,1,0:T(8,128)}, u32[]{:S(2)}) copy-start(f32[1,1,8,2,2,128,128]{6,5,4,3,2,1,0:T(8,128)} %param.20) | copy-start | bytes 6291460
  39.4 2.0 %collective-permute-start.8 = (bf16[16,128,128]{2,1,0:T(8,128)(2,1)S(1)}, bf16[16,128,128]{2,1,0:T(8,128)(2,1)S(1)}, u32[]{:S(2)}, u32[]{:S(2)}) collective-permute-start(bf16[16,128,128]{2,1,0:T(8,128)(2,1)S(1)} %get-tuple-element.42.refs_12_.refs_0_.refs_16_.refs_7_), channel_id=1, source_target_pairs={{0,1},{1,0},{2,3},{3,2},{4,5},{5,4},{6,7},{7,6},{8,9},{9,8},{10,11... | collective-permute-start | bytes 1572872 | tf_op jit(solution)/shard_map/ppermute | solution.py:54
  39.5 14.3 %collective-permute-start.12 = (bf16[16,128,128]{2,1,0:T(8,128)(2,1)S(1)}, bf16[16,128,128]{2,1,0:T(8,128)(2,1)S(1)}, u32[]{:S(2)}, u32[]{:S(2)}) collective-permute-start(bf16[16,128,128]{2,1,0:T(8,128)(2,1)S(1)} %get-tuple-element.42.refs_12_.refs_0_.refs_16_.refs_7_), channel_id=1, source_target_pairs={{0,16},{16,0},{32,48},{48,32},{64,80},{80,64},{96,112},{112,96},{1... | collective-permute-start | bytes 1572872 | tf_op jit(solution)/shard_map/ppermute | solution.py:38
  42.2 11.6 %collective-permute-start.9 = (bf16[4,128,128]{2,1,0:T(8,128)(2,1)S(1)}, bf16[4,128,128]{2,1,0:T(8,128)(2,1)S(1)}, u32[]{:S(2)}, u32[]{:S(2)}) collective-permute-start(bf16[4,128,128]{2,1,0:T(8,128)(2,1)S(1)} %get-tuple-element.44), channel_id=1, source_target_pairs={{0,32},{16,48},{32,64},{48,80},{64,96},{80,112},{96,0},{112,16},{1... | collective-permute-start | bytes 393224 | tf_op jit(solution)/shard_map/ppermute | solution.py:43
  42.8 11.1 %collective-permute-start.10 = (bf16[4,128,128]{2,1,0:T(8,128)(2,1)S(1)}, bf16[4,128,128]{2,1,0:T(8,128)(2,1)S(1)}, u32[]{:S(2)}, u32[]{:S(2)}) collective-permute-start(bf16[4,128,128]{2,1,0:T(8,128)(2,1)S(1)} %get-tuple-element.45), channel_id=1, source_target_pairs={{0,96},{16,112},{32,0},{48,16},{64,32},{80,48},{96,64},{112,80},{1... | collective-permute-start | bytes 393224 | tf_op jit(solution)/shard_map/ppermute | solution.py:43
  44.3 9.6 %collective-permute-start.11 = (bf16[4,128,128]{2,1,0:T(8,128)(2,1)S(1)}, bf16[4,128,128]{2,1,0:T(8,128)(2,1)S(1)}, u32[]{:S(2)}, u32[]{:S(2)}) collective-permute-start(bf16[4,128,128]{2,1,0:T(8,128)(2,1)S(1)} %get-tuple-element.46), channel_id=1, source_target_pairs={{0,64},{16,80},{32,96},{48,112},{64,0},{80,16},{96,32},{112,48},{1... | collective-permute-start | bytes 393224 | tf_op jit(solution)/shard_map/ppermute | solution.py:43
  45.6 20.7 %collective-permute-start.15 = (bf16[16,128,128]{2,1,0:T(8,128)(2,1)S(1)}, bf16[16,128,128]{2,1,0:T(8,128)(2,1)S(1)}, u32[]{:S(2)}, u32[]{:S(2)}) collective-permute-start(bf16[16,128,128]{2,1,0:T(8,128)(2,1)S(1)} %collective-permute-done.8.after.refs_4_), channel_id=1, source_target_pairs={{0,2},{2,4},{4,6},{6,8},{8,10},{10,12},{12,14},{3,1},{5,3},{7,5},{... | collective-permute-start | bytes 1572872 | tf_op jit(solution)/shard_map/ppermute | solution.py:56
  54.3 15.4 %collective-permute-start.14 = (bf16[16,128,128]{2,1,0:T(8,128)(2,1)S(1)}, bf16[16,128,128]{2,1,0:T(8,128)(2,1)S(1)}, u32[]{:S(2)}, u32[]{:S(2)}) collective-permute-start(bf16[16,128,128]{2,1,0:T(8,128)(2,1)S(1)} %get-tuple-element.50.after.refs_2_), channel_id=1, source_target_pairs={{48,16},{80,48},{112,80},{0,32},{32,64},{64,96},{49,17},{81,49},{1... | collective-permute-start | bytes 1572872 | tf_op jit(solution)/shard_map/ppermute | solution.py:49
  56.6 8.1 %collective-permute-start.13 = (bf16[8,128,128]{2,1,0:T(8,128)(2,1)S(1)}, bf16[8,128,128]{2,1,0:T(8,128)(2,1)S(1)}, u32[]{:S(2)}, u32[]{:S(2)}) collective-permute-start(bf16[8,128,128]{2,1,0:T(8,128)(2,1)S(1)} %get-tuple-element.47), channel_id=1, source_target_pairs={{0,16},{16,0},{32,48},{48,32},{64,80},{80,64},{96,112},{112,96},{1... | collective-permute-start | bytes 786440 | tf_op jit(solution)/shard_map/ppermute | solution.py:38
  72.4 5.3 %collective-permute-start.18 = (bf16[16,128,128]{2,1,0:T(8,128)(2,1)S(1)}, bf16[16,128,128]{2,1,0:T(8,128)(2,1)S(1)}, u32[]{:S(2)}, u32[]{:S(2)}) collective-permute-start(bf16[16,128,128]{2,1,0:T(8,128)(2,1)S(1)} %get-tuple-element.55.after.refs_14_.refs_0_.refs_5_), channel_id=1, source_target_pairs={{0,1},{1,0},{2,3},{3,2},{4,5},{5,4},{6,7},{7,6},{8,9},{9,8},{10,11... | collective-permute-start | bytes 1572872 | tf_op jit(solution)/shard_map/ppermute | solution.py:54
  72.7 14.3 %collective-permute-start.16 = (bf16[16,128,128]{2,1,0:T(8,128)(2,1)S(1)}, bf16[16,128,128]{2,1,0:T(8,128)(2,1)S(1)}, u32[]{:S(2)}, u32[]{:S(2)}) collective-permute-start(bf16[16,128,128]{2,1,0:T(8,128)(2,1)S(1)} %get-tuple-element.55.after.refs_14_.refs_0_.refs_5_), channel_id=1, source_target_pairs={{0,16},{16,0},{32,48},{48,32},{64,80},{80,64},{96,112},{112,96},{1... | collective-permute-start | bytes 1572872 | tf_op jit(solution)/shard_map/ppermute | solution.py:38
  78.9 12.0 %collective-permute-start.20 = (bf16[4,256,128]{2,1,0:T(8,128)(2,1)S(1)}, bf16[4,256,128]{2,1,0:T(8,128)(2,1)S(1)}, u32[]{:S(2)}, u32[]{:S(2)}) collective-permute-start(bf16[4,256,128]{2,1,0:T(8,128)(2,1)S(1)} %get-tuple-element.59), channel_id=1, source_target_pairs={{0,32},{16,48},{32,64},{48,80},{64,96},{80,112},{96,0},{112,16},{1... | collective-permute-start | bytes 786440 | tf_op jit(solution)/shard_map/ppermute | solution.py:43
  79.4 11.5 %collective-permute-start.21 = (bf16[4,256,128]{2,1,0:T(8,128)(2,1)S(1)}, bf16[4,256,128]{2,1,0:T(8,128)(2,1)S(1)}, u32[]{:S(2)}, u32[]{:S(2)}) collective-permute-start(bf16[4,256,128]{2,1,0:T(8,128)(2,1)S(1)} %get-tuple-element.60), channel_id=1, source_target_pairs={{0,96},{16,112},{32,0},{48,16},{64,32},{80,48},{96,64},{112,80},{1... | collective-permute-start | bytes 786440 | tf_op jit(solution)/shard_map/ppermute | solution.py:43
  81.0 13.2 %collective-permute-start.22 = (bf16[4,256,128]{2,1,0:T(8,128)(2,1)S(1)}, bf16[4,256,128]{2,1,0:T(8,128)(2,1)S(1)}, u32[]{:S(2)}, u32[]{:S(2)}) collective-permute-start(bf16[4,256,128]{2,1,0:T(8,128)(2,1)S(1)} %get-tuple-element.61), channel_id=1, source_target_pairs={{0,64},{16,80},{32,96},{48,112},{64,0},{80,16},{96,32},{112,48},{1... | collective-permute-start | bytes 786440 | tf_op jit(solution)/shard_map/ppermute | solution.py:43
  82.4 21.9 %collective-permute-start.19 = (bf16[16,128,128]{2,1,0:T(8,128)(2,1)S(1)}, bf16[16,128,128]{2,1,0:T(8,128)(2,1)S(1)}, u32[]{:S(2)}, u32[]{:S(2)}) collective-permute-start(bf16[16,128,128]{2,1,0:T(8,128)(2,1)S(1)} %collective-permute-done.18.refs_4_.refs_11_), channel_id=1, source_target_pairs={{0,2},{2,4},{4,6},{6,8},{8,10},{10,12},{12,14},{3,1},{5,3},{7,5},{... | collective-permute-start | bytes 1572872 | tf_op jit(solution)/shard_map/ppermute | solution.py:56
  87.0 17.3 %collective-permute-start.17 = (bf16[16,128,128]{2,1,0:T(8,128)(2,1)S(1)}, bf16[16,128,128]{2,1,0:T(8,128)(2,1)S(1)}, u32[]{:S(2)}, u32[]{:S(2)}) collective-permute-start(bf16[16,128,128]{2,1,0:T(8,128)(2,1)S(1)} %collective-permute-done.16.refs_2_.refs_4_), channel_id=1, source_target_pairs={{48,16},{80,48},{112,80},{0,32},{32,64},{64,96},{49,17},{81,49},{1... | collective-permute-start | bytes 1572872 | tf_op jit(solution)/shard_map/ppermute | solution.py:49
  95.0 15.9 %collective-permute-start.23 = (bf16[8,256,128]{2,1,0:T(8,128)(2,1)S(1)}, bf16[8,256,128]{2,1,0:T(8,128)(2,1)S(1)}, u32[]{:S(2)}, u32[]{:S(2)}) collective-permute-start(bf16[8,256,128]{2,1,0:T(8,128)(2,1)S(1)} %turned.5), channel_id=1, source_target_pairs={{0,16},{16,0},{32,48},{48,32},{64,80},{80,64},{96,112},{112,96},{1... | collective-permute-start | bytes 1572872 | tf_op jit(solution)/shard_map/ppermute | solution.py:38

commit v5 on v4

--- a/solution.py
+++ b/solution.py
@@ -355,8 +355,118 @@
     )(wall_at, *arrays, *after)
 
 
-def states_kernel(mats, pole, res, states, *refs):
-    walls, (out, fresh, sems) = refs[:-3], refs[-3:]
+def interior(pool, index, order, tiles, i):
+    block = order[i]
+    neigh = index.shape[0]
+    sources = jnp.concatenate([pool[index[k, block]] for k in range(neigh)], axis=1)
+    return jnp.dot(sources, tiles[block], preferred_element_type=F32)
+
+
+def fill_pool(parts, pool, sems):
+    copies, at = [], 0
+    for i, part in enumerate(parts):
+        copies.append(pltpu.make_async_copy(part, pool.at[pl.ds(at, part.shape[0])], sems.at[i]))
+        at += part.shape[0]
+    for copy in copies:
+        copy.start()
+    for copy in copies:
+        copy.wait()
+
+
+def first_kernel(order, index, tiles, base, *refs):
+    parts, (field, exports, pool, sems) = refs[:-4], refs[-4:]
+    fill_pool(parts, pool, sems)
+
+    @pl.loop(0, exports.shape[0], unroll=16)
+    def _(i):
+        value = base[i] - 0.5 * interior(pool, index, order, tiles, i)
+        field[i] = value
+        exports[i] = value.astype(BF16)
+
+
+def first_blocks(order, index, tiles, base, pool, name):
+    rows, cells = base.shape[1:]
+    exports = pool[0].shape[0]
+    return pl.pallas_call(
+        first_kernel,
+        out_shape=(
+            jax.ShapeDtypeStruct((exports, rows, cells), F32),
+            jax.ShapeDtypeStruct((exports, rows, cells), BF16),
+            jax.ShapeDtypeStruct((sum(p.shape[0] for p in pool), rows, cells), BF16),
+        ),
+        in_specs=[spec(SMEM)] * 2 + [spec(VMEM)] * 2 + [spec(pl.ANY)] * len(pool),
+        out_specs=(spec(VMEM),) * 3,
+        scratch_shapes=[DMA((len(pool),))],
+        compiler_params=params(8),
+        cost_estimate=cost(3.1),
+        name=name,
+    )(order, index, tiles, base, *pool)
+
+
+def other_kernel(order, index, tiles, base, pool, after, field, others):
+    del after
+    count = others.shape[0]
+    exports = order.shape[0] - count
+
+    @pl.loop(0, count, unroll=12)
+    def _(i):
+        value = base[i + exports] - 0.5 * interior(pool, index, order, tiles, i + exports)
+        field[i] = value
+        others[i] = value.astype(BF16)
+
+
+def other_blocks(order, index, tiles, base, pool, count, after, name):
+    rows, cells = base.shape[1:]
+    return pl.pallas_call(
+        other_kernel,
+        out_shape=(
+            jax.ShapeDtypeStruct((count, rows, cells), F32),
+            jax.ShapeDtypeStruct((count, rows, cells), BF16),
+        ),
+        in_specs=[spec(SMEM)] * 2 + [spec(VMEM)] * 3 + [spec(pl.ANY)],
+        out_specs=(spec(VMEM),) * 2,
+        compiler_params=params(8),
+        cost_estimate=cost(0),
+        name=name,
+    )(order, index, tiles, base, pool, after)
+
+
+def last_kernel(count, order, index, tiles, base, *refs):
+    parts, (out, pool, fresh, pool_sems, out_sems) = refs[:-5], refs[-5:]
+    fill_pool(parts, pool, pool_sems)
+
+    def copy(i):
+        return pltpu.make_async_copy(fresh.at[i], out.at[order[i]], out_sems.at[i])
+
+    @pl.loop(0, count, unroll=12)
+    def _(i):
+        fresh[i] = base[i] - 0.5 * interior(pool, index, order, tiles, i)
+        copy(i).start()
+
+    @pl.loop(0, count)
+    def _(i):
+        copy(i).wait()
+
+
+def last_blocks(order, index, tiles, base, pool, count):
+    blocks, rows, cells = base.shape
+    return pl.pallas_call(
+        functools.partial(last_kernel, count),
+        out_shape=(
+            jax.ShapeDtypeStruct((blocks, rows, cells), F32),
+            jax.ShapeDtypeStruct((sum(p.shape[0] for p in pool), rows, cells), BF16),
+        ),
+        in_specs=[spec(SMEM)] * 2 + [spec(VMEM)] * 2 + [spec(pl.ANY)] * len(pool),
+        out_specs=(spec(pltpu.HBM), spec(VMEM)),
+        scratch_shapes=[VMEM((count, rows, cells), F32), DMA((len(pool),)), DMA((count,))],
+        compiler_params=params(8),
+        cost_estimate=cost(0),
+        name="last",
+    )(order, index, tiles, base, *pool)
+
+
+def end_kernel(count, order, index, mats, pole, res, tiles, base, pool, states, *refs):
+    walls, (_, out, held, fresh, fresh_held, out_sems, held_sems) = refs[:-7], refs[-7:]
     rows = states.shape[2]
     cap = mats.shape[0]
     copies = []
@@ -366,138 +476,64 @@
         second = slot[rows:, :].astype(F32)
         first = second + (p1 - p2) * slot[0:rows, :].astype(F32)
         n = len(copies)
-        fresh[n, 0] = (p1 * p1 * p1) * states[e, 0] + res[0, m] * first
-        fresh[n, 1] = (p2 * p2 * p2) * states[e, 1] + res[1, m] * second
-        copies.append(pltpu.make_async_copy(fresh.at[n], out.at[e], sems.at[n]))
+        fresh_held[n, 0] = (p1 * p1 * p1) * states[e, 0] + res[0, m] * first
+        fresh_held[n, 1] = (p2 * p2 * p2) * states[e, 1] + res[1, m] * second
+        copies.append(pltpu.make_async_copy(fresh_held.at[n], held.at[e], held_sems.at[n]))
         copies[-1].start()
-    for copy in copies:
-        copy.wait()
-
-
-def states_after(mats, pole, res, states, walls):
-    return pl.pallas_call(
-        states_kernel,
-        out_shape=jax.ShapeDtypeStruct(states.shape, F32),
-        in_specs=[spec(SMEM)] * 3 + [spec(VMEM)] * (1 + len(walls)),
-        out_specs=spec(pltpu.HBM),
-        scratch_shapes=[VMEM(states.shape, F32), DMA(states.shape[:1])],
-        compiler_params=params(8),
-        cost_estimate=cost(0),
-        name="states_after",
-    )(mats, pole, res, states, *walls)
-
-
-def interior(pool, index, order, tiles, i):
-    block = order[i]
-    neigh = index.shape[0]
-    sources = jnp.concatenate([pool[index[k, block]] for k in range(neigh)], axis=1)
-    return jnp.dot(sources, tiles[block], preferred_element_type=F32)
-
-
-def fill_pool(parts, pool, sems):
-    copies, at = [], 0
-    for i, part in enumerate(parts):
-        copies.append(pltpu.make_async_copy(part, pool.at[pl.ds(at, part.shape[0])], sems.at[i]))
-        at += part.shape[0]
-    for copy in copies:
-        copy.start()
-    for copy in copies:
-        copy.wait()
-
-
-def first_kernel(order, index, tiles, base, *refs):
-    parts, (field, exports, pool, sems) = refs[:-4], refs[-4:]
-    fill_pool(parts, pool, sems)
-
-    @pl.loop(0, exports.shape[0], unroll=16)
+
+    def copy(i):
+        return pltpu.make_async_copy(fresh.at[i], out.at[order[i + count]], out_sems.at[i])
+
+    @pl.loop(0, fresh.shape[0], unroll=16)
     def _(i):
-        value = base[i] - 0.5 * interior(pool, index, order, tiles, i)
-        field[i] = value
-        exports[i] = value.astype(BF16)
-
-
-def first_blocks(order, index, tiles, base, pool, name):
-    rows, cells = base.shape[1:]
-    exports = pool[0].shape[0]
-    return pl.pallas_call(
-        first_kernel,
-        out_shape=(
-            jax.ShapeDtypeStruct((exports, rows, cells), F32),
-            jax.ShapeDtypeStruct((exports, rows, cells), BF16),
-            jax.ShapeDtypeStruct((sum(p.shape[0] for p in pool), rows, cells), BF16),
-        ),
-        in_specs=[spec(SMEM)] * 2 + [spec(VMEM)] * 2 + [spec(pl.ANY)] * len(pool),
-        out_specs=(spec(VMEM),) * 3,
-        scratch_shapes=[DMA((len(pool),))],
-        compiler_params=params(8),
-        cost_estimate=cost(3.1),
-        name=name,
-    )(order, index, tiles, base, *pool)
-
-
-def other_kernel(order, index, tiles, base, pool, after, field, others):
-    del after
-    count = others.shape[0]
-    exports = order.shape[0] - count
-
-    @pl.loop(0, count, unroll=12)
-    def _(i):
-        value = base[i + exports] - 0.5 * interior(pool, index, order, tiles, i + exports)
-        field[i] = value
-        others[i] = value.astype(BF16)
-
-
-def other_blocks(order, index, tiles, base, pool, count, after, name):
-    rows, cells = base.shape[1:]
-    return pl.pallas_call(
-        other_kernel,
-        out_shape=(
-            jax.ShapeDtypeStruct((count, rows, cells), F32),
-            jax.ShapeDtypeStruct((count, rows, cells), BF16),
-        ),
-        in_specs=[spec(SMEM)] * 2 + [spec(VMEM)] * 3 + [spec(pl.ANY)],
-        out_specs=(spec(VMEM),) * 2,
-        compiler_params=params(8),
-        cost_estimate=cost(0),
-        name=name,
-    )(order, index, tiles, base, pool, after)
-
-
-def last_kernel(order, index, tiles, base, *refs):
-    parts, (out, pool, fresh, pool_sems, out_sems) = refs[:-5], refs[-5:]
-    fill_pool(parts, pool, pool_sems)
-    count = out.shape[0]
-
-    def copy(i):
-        return pltpu.make_async_copy(fresh.at[i], out.at[order[i]], out_sems.at[i])
-
-    @pl.loop(0, count, unroll=20)
-    def _(i):
-        fresh[i] = base[i] - 0.5 * interior(pool, index, order, tiles, i)
+        fresh[i] = base[i + count] - 0.5 * interior(pool, index, order, tiles, i + count)
         copy(i).start()
 
-    @pl.loop(0, count)
+    @pl.loop(0, fresh.shape[0])
     def _(i):
         copy(i).wait()
 
-
-def last_blocks(order, index, tiles, base, pool):
+    for copy_held in copies:
+        copy_held.wait()
+
+
+def end_blocks(order, index, owned, tiles, base, pool, states, walls, field, count):
     blocks, rows, cells = base.shape
     return pl.pallas_call(
-        last_kernel,
-        out_shape=jax.ShapeDtypeStruct((blocks, rows, cells), F32),
-        in_specs=[spec(SMEM)] * 2 + [spec(VMEM)] * 2 + [spec(pl.ANY)] * len(pool),
-        out_specs=spec(pltpu.HBM),
+        functools.partial(end_kernel, count),
+        out_shape=(jax.ShapeDtypeStruct(base.shape, F32), jax.ShapeDtypeStruct(states.shape, F32)),
+        in_specs=[spec(SMEM)] * 5 + [spec(VMEM)] * (4 + len(walls)) + [spec(pltpu.HBM)],
+        out_specs=(spec(pltpu.HBM),) * 2,
         scratch_shapes=[
-            VMEM((sum(p.shape[0] for p in pool), rows, cells), BF16),
-            VMEM((blocks, rows, cells), F32),
-            DMA((len(pool),)),
-            DMA((blocks,)),
+            VMEM((blocks - count, rows, cells), F32),
+            VMEM(states.shape, F32),
+            DMA((blocks - count,)),
+            DMA(states.shape[:1]),
         ],
-        compiler_params=params(10),
+        input_output_aliases={9 + len(walls): 0},
+        compiler_params=params(8),
         cost_estimate=cost(0),
-        name="last",
-    )(order, index, tiles, base, *pool)
+        name="end",
+    )(order, index, *owned, tiles, base, pool, states, *walls, field)
+
+
+def copy_kernel(value, out, sem):
+    copy = pltpu.make_async_copy(value, out, sem)
+    copy.start()
+    copy.wait()
+
+
+def copied(value):
+    return pl.pallas_call(
+        copy_kernel,
+        out_shape=jax.ShapeDtypeStruct(value.shape, value.dtype),
+        in_specs=[spec(pl.ANY)],
+        out_specs=spec(VMEM),
+        scratch_shapes=[DMA],
+        compiler_params=params(8),
+        cost_estimate=cost(1),
+        name="copied",
+    )(value)
 
 
 def per_device(
@@ -520,7 +556,7 @@
 
     across, core, beside = beside_of(e1)
     message, across = over_x(over_y(responses(1, *walled, core)), (across,))
-    around = (across, passed_on(across), core, beside)
+    around = (across, passed_on(across), copied(core), beside)
     order, index, wall_at, o1 = prepare(
         export_ids, nbr_dir.T, nbr_idx.T, bnd_blk.reshape(owners, cap).T, pressure, across
     )
@@ -543,8 +579,9 @@
     walls = over_y(walls_of(wall_at, message, rounded, (core,)))
     (walls,) = over_x(walls, (), (across,))
     base = base_of(3, wall_at, order, (message, later), pressure, (p2, p1), rounded)
-    p3 = last_blocks(order, index, tiles, base, (e3, o3) + around)
-    held = states_after(*owned, held, walls)
+    ahead = blocks - exports
+    p3, pool = last_blocks(order, index, tiles, base, (e3, o3) + around, ahead)
+    p3, held = end_blocks(order, index, owned, tiles, base, pool, held, walls, p3, ahead)
     return p3, held.reshape(states.shape)
 
 

time: 114 us -> 113 us (level)
  local copies, waits for them, and re-layouts: 1.89 us -> 0.31 us
    ppermute x6, waiting for transfers between devices: 12.7 us -> 16.9 us  [other_x(): return lax.ppermute(value, 'gx', [(i, i ^ 1) for i in range(count)])]
    ppermute x6, starting transfers between devices: 11 us -> 7.85 us  [other_x(): return lax.ppermute(value, 'gx', [(i, i ^ 1) for i in range(count)])]
    ppermute x3, waiting for transfers between devices: 12.5 us -> 10.5 us  [passed_on(): return lax.ppermute(across, 'gx', on)]
    ppermute x3, starting transfers between devices: 8.53 us -> 10.4 us  [passed_on(): return lax.ppermute(across, 'gx', on)]
    unnamed x28 -> x26, local copies, waits for them, and re-layouts: 1.65 us -> 0.07 us
    pallas_call x2 -> x3, Pallas kernels: 8.59 us -> 9.26 us  [the longest x1 4.78 us: last_blocks(): pl.pallas_call(functools.partial(last_kernel, count), out_shape=(jax.Shap...]
  transfers between devices with their start and end apart: 24 -> 24, of which waited for: 12 -> 11; matrix products, arithmetic and copies ran while one was open for 0% -> 0% of each run, Pallas kernels for 22% -> 20%
where the time goes in v5:
time: 113 us; the launch traced here: 112 us
  starting transfers between devices  42.3 us (37%)
  Pallas kernels  35.8 us (32%)
  waiting for transfers between devices  31.9 us (28%)
  between operations  1.18 us (1%)
    ppermute x6, waiting for transfers between devices, other_x(): return lax.ppermute(value, 'gx', [(i, i ^ 1) for i in range(count)])  16.9 us
    ppermute x9, starting transfers between devices, along_y(): lax.ppermute(value, 'gx', [(i, (i + 2 * steps) % count) for i in range(co...  11.9 us
    ppermute x3, starting transfers between devices, beside_of(): return (other_x(exports), core, lax.ppermute(core, 'gy', on))  11.7 us
    ppermute x3, waiting for transfers between devices, passed_on(): return lax.ppermute(across, 'gx', on)  10.5 us
    ppermute x3, starting transfers between devices, passed_on(): return lax.ppermute(across, 'gx', on)  10.4 us
    ppermute x6, starting transfers between devices, other_x(): return lax.ppermute(value, 'gx', [(i, i ^ 1) for i in range(count)])  7.85 us
    pallas_call x2, Pallas kernels, other_blocks(): pl.pallas_call(other_kernel, out_shape=(jax.ShapeDtypeStruct((count, rows...  7.12 us
    pallas_call x2, Pallas kernels, first_blocks(): pl.pallas_call(first_kernel, out_shape=(jax.ShapeDtypeStruct((exports, ro...  5.69 us
  transfers between devices with their start and end apart: 24, of which 11 were waited for; matrix products, arithmetic and copies ran while one was open for 0% of the time, Pallas kernels for 20%

profile of v5, /device:TPU:40, one launch (start us, length us, event | category | flops | bytes accessed | tf_op | source)
XLA Modules:
  0.0 111.6 jit_solution(6889406769041824487)
XLA Ops:
  0.7 3.0 %exports.1.refs_5_.refs_0_.refs_14_.refs_18_.refs_9_ = bf16[16,128,128]{2,1,0:T(8,128)(2,1)} custom-call(s32[16]{0:T(128)} %ids.3, f32[40,128,128]{2,1,0:T(8,128)} %pressure.9), custom_call_target="tpu_custom_call" | custom-call | flops 3000000000 | tf_op jit(solution)/shard_map/exports/pallas_call | solution.py:131
  3.7 0.1 collective-permute-start
  3.8 1.6 %collective-permute-start.4 = (bf16[16,128,128]{2,1,0:T(8,128)(2,1)}, bf16[16,128,128]{2,1,0:T(8,128)(2,1)S(1)}, u32[]{:S(2)}, u32[]{:S(2)}) collective-permute-start(bf16[16,128,128]{2,1,0:T(8,128)(2,1)} %exports.1.refs_5_.refs_0_.refs_14_.refs_18_.refs_9_), channel_id=1, source_target_pairs={{0,16},{16,0},{32,48},{48,32},{64,80},{80,64},{96,112},{112,96},{1... | collective-permute-start | bytes 1572872 | tf_op jit(solution)/shard_map/ppermute | solution.py:38
  5.3 0.1 reshape.35
  5.4 0.1 reshape.33
  5.5 0.1 reshape.32
  5.6 0.1 pad_maximum_fusion.table
  5.7 0.2 collective-permute-done.after.value
  5.9 0.8 responses_1.1
  6.7 0.0 copy-start.1
  6.7 0.0 copy-start.7
  6.7 0.0 copy-start.8
  6.7 0.0 copy-start.10
  6.8 0.0 copy-start.11
  6.8 1.6 %collective-permute-start.1 = (bf16[4,144,128]{2,1,0:T(8,128)(2,1)S(1)}, bf16[4,144,128]{2,1,0:T(8,128)(2,1)S(1)}, u32[]{:S(2)}, u32[]{:S(2)}) collective-permute-start(bf16[4,144,128]{2,1,0:T(8,128)(2,1)S(1)} %get-tuple-element.37), channel_id=1, source_target_pairs={{0,32},{16,48},{32,64},{48,80},{64,96},{80,112},{96,0},{112,16},{1... | collective-permute-start | bytes 442376 | tf_op jit(solution)/shard_map/ppermute | solution.py:43
  8.4 0.5 collective-permute-start.2
  8.9 2.3 %collective-permute-start.3 = (bf16[4,144,128]{2,1,0:T(8,128)(2,1)S(1)}, bf16[4,144,128]{2,1,0:T(8,128)(2,1)S(1)}, u32[]{:S(2)}, u32[]{:S(2)}) collective-permute-start(bf16[4,144,128]{2,1,0:T(8,128)(2,1)S(1)} %get-tuple-element.39), channel_id=1, source_target_pairs={{0,64},{16,80},{32,96},{48,112},{64,0},{80,16},{96,32},{112,48},{1... | collective-permute-start | bytes 442376 | tf_op jit(solution)/shard_map/ppermute | solution.py:43
  11.2 3.8 %collective-permute-start.7 = (bf16[16,128,128]{2,1,0:T(8,128)(2,1)S(1)}, bf16[16,128,128]{2,1,0:T(8,128)(2,1)S(1)}, u32[]{:S(2)}, u32[]{:S(2)}) collective-permute-start(bf16[16,128,128]{2,1,0:T(8,128)(2,1)S(1)} %collective-permute-done.after.value), channel_id=1, source_target_pairs={{0,2},{2,4},{4,6},{6,8},{8,10},{10,12},{12,14},{3,1},{5,3},{7,5},{... | collective-permute-start | bytes 1572872 | tf_op jit(solution)/shard_map/ppermute | solution.py:56
  15.0 3.3 %collective-permute-done.4.refs_4_ = bf16[16,128,128]{2,1,0:T(8,128)(2,1)S(1)} collective-permute-done((bf16[16,128,128]{2,1,0:T(8,128)(2,1)}, bf16[16,128,128]{2,1,0:T(8,128)(2,1)S(1)}, u32[]{:S(2)}, u32[]{:S(2)}) %collective-permute-start.4) | collective-permute-done | bytes 524320 | tf_op jit(solution)/shard_map/ppermute | solution.py:38
  18.3 0.0 collective-permute-done.1.refs_1_
  18.3 0.0 collective-permute-done.2.refs_2_
  18.3 0.0 copy-start.2
  18.3 0.4 turned.3
  18.8 3.5 %collective-permute-start.6 = (bf16[16,128,128]{2,1,0:T(8,128)(2,1)S(1)}, bf16[16,128,128]{2,1,0:T(8,128)(2,1)S(1)}, u32[]{:S(2)}, u32[]{:S(2)}) collective-permute-start(bf16[16,128,128]{2,1,0:T(8,128)(2,1)S(1)} %get-tuple-element.40.after.refs_2_), channel_id=1, source_target_pairs={{48,16},{80,48},{112,80},{0,32},{32,64},{64,96},{49,17},{81,49},{1... | collective-permute-start | bytes 1572872 | tf_op jit(solution)/shard_map/ppermute | solution.py:49
  22.3 0.4 collective-permute-start.5
  22.8 2.1 %prepare.1 = (s32[40]{0:T(128)S(1)}, s32[12,40]{1,0:T(8,128)S(1)}, s32[2,8]{1,0:T(2,128)S(1)}, bf16[24,128,128]{2,1,0:T(8,128)(2,1)S(1)}) custom-call(s32[16]{0:T(128)S(1)} %copy-done.11, s32[12,40]{1,0:T(8,128)S(1)} %bitcast.29, s32[12,40]{1,0:T(8,128)S(1)} %bitcast.30, s32[2,8]{1,0:T(2,128)S(1)} %bitcast.33, f32[40,128,128]{2,1,0:T(8,128)S(1)} %copy-done.1, ...), custom_call_target="tpu_custom_call" | custom-call | flops 2100000000 | tf_op jit(solution)/shard_map/prepare/pallas_call | solution.py:185
  25.0 5.7 %collective-permute-done.5.refs_4_ = bf16[8,144,128]{2,1,0:T(8,128)(2,1)S(1)} collective-permute-done((bf16[8,144,128]{2,1,0:T(8,128)(2,1)S(1)}, bf16[8,144,128]{2,1,0:T(8,128)(2,1)S(1)}, u32[]{:S(2)}, u32[]{:S(2)}) %collective-permute-start.5) | collective-permute-done | bytes 294944 | tf_op jit(solution)/shard_map/ppermute | solution.py:38
  30.6 1.3 %base_1.1.base = f32[40,128,128]{2,1,0:T(8,128)S(1)} custom-call(s32[2,8]{1,0:T(2,128)S(1)} %get-tuple-element.43.wall_at, s32[40]{0:T(128)S(1)} %get-tuple-element.41.order, f32[40,128,128]{2,1,0:T(8,128)S(1)} %copy-done.1, bf16[4,144,128]{2,1,0:T(8,128)(2,1)S(1)} %get-tuple-element.36.refs_0_, bf16[4,144,128]{2,1,0:T(8,128)(2,1)S(1)} %collective-permute-done.1.refs_1_, ...), custom_call_target="tpu_custom_call" | custom-call | flops 1600000000 | tf_op jit(solution)/shard_map/base_1/pallas_call | solution.py:310
  31.9 2.2 %collective-permute-done.6.refs_3_ = bf16[16,128,128]{2,1,0:T(8,128)(2,1)S(1)} collective-permute-done((bf16[16,128,128]{2,1,0:T(8,128)(2,1)S(1)}, bf16[16,128,128]{2,1,0:T(8,128)(2,1)S(1)}, u32[]{:S(2)}, u32[]{:S(2)}) %collective-permute-start.6) | collective-permute-done | bytes 524320 | tf_op jit(solution)/shard_map/ppermute | solution.py:49
  34.1 2.8 %exports_1.1 = (f32[16,128,128]{2,1,0:T(8,128)S(1)}, bf16[16,128,128]{2,1,0:T(8,128)(2,1)S(1)}, bf16[104,128,128]{2,1,0:T(8,128)(2,1)S(1)}) custom-call(s32[40]{0:T(128)S(1)} %get-tuple-element.41.order, s32[12,40]{1,0:T(8,128)S(1)} %get-tuple-element.42.index, bf16[40,1536,128]{2,1,0:T(8,128)(2,1)S(1)} %bitcast.15, f32[40,128,128]{2,1,0:T(8,128)S(1)} %base_1.1.base, ...), custom_call_target="tpu_custom_call" | custom-call | flops 3100000000 | tf_op jit(solution)/shard_map/exports_1/pallas_call | solution.py:390
  36.9 0.1 collective-permute-start.8
  37.0 1.6 %collective-permute-start.12 = (bf16[16,128,128]{2,1,0:T(8,128)(2,1)S(1)}, bf16[16,128,128]{2,1,0:T(8,128)(2,1)S(1)}, u32[]{:S(2)}, u32[]{:S(2)}) collective-permute-start(bf16[16,128,128]{2,1,0:T(8,128)(2,1)S(1)} %get-tuple-element.46.refs_12_.refs_0_.refs_16_.refs_7_), channel_id=1, source_target_pairs={{0,16},{16,0},{32,48},{48,32},{64,80},{80,64},{96,112},{112,96},{1... | collective-permute-start | bytes 1572872 | tf_op jit(solution)/shard_map/ppermute | solution.py:38
  38.6 0.3 collective-permute-done.8.after.refs_4_
  38.9 0.8 responses_2.1
  39.7 1.6 %collective-permute-start.9 = (bf16[4,128,128]{2,1,0:T(8,128)(2,1)S(1)}, bf16[4,128,128]{2,1,0:T(8,128)(2,1)S(1)}, u32[]{:S(2)}, u32[]{:S(2)}) collective-permute-start(bf16[4,128,128]{2,1,0:T(8,128)(2,1)S(1)} %get-tuple-element.48), channel_id=1, source_target_pairs={{0,32},{16,48},{32,64},{48,80},{64,96},{80,112},{96,0},{112,16},{1... | collective-permute-start | bytes 393224 | tf_op jit(solution)/shard_map/ppermute | solution.py:43
  41.4 0.4 collective-permute-start.10
  41.8 2.3 %collective-permute-start.11 = (bf16[4,128,128]{2,1,0:T(8,128)(2,1)S(1)}, bf16[4,128,128]{2,1,0:T(8,128)(2,1)S(1)}, u32[]{:S(2)}, u32[]{:S(2)}) collective-permute-start(bf16[4,128,128]{2,1,0:T(8,128)(2,1)S(1)} %get-tuple-element.50), channel_id=1, source_target_pairs={{0,64},{16,80},{32,96},{48,112},{64,0},{80,16},{96,32},{112,48},{1... | collective-permute-start | bytes 393224 | tf_op jit(solution)/shard_map/ppermute | solution.py:43
  44.1 3.8 %collective-permute-start.15 = (bf16[16,128,128]{2,1,0:T(8,128)(2,1)S(1)}, bf16[16,128,128]{2,1,0:T(8,128)(2,1)S(1)}, u32[]{:S(2)}, u32[]{:S(2)}) collective-permute-start(bf16[16,128,128]{2,1,0:T(8,128)(2,1)S(1)} %collective-permute-done.8.after.refs_4_), channel_id=1, source_target_pairs={{0,2},{2,4},{4,6},{6,8},{8,10},{10,12},{12,14},{3,1},{5,3},{7,5},{... | collective-permute-start | bytes 1572872 | tf_op jit(solution)/shard_map/ppermute | solution.py:56
  47.9 3.4 %collective-permute-done.12.refs_4_ = bf16[16,128,128]{2,1,0:T(8,128)(2,1)S(1)} collective-permute-done((bf16[16,128,128]{2,1,0:T(8,128)(2,1)S(1)}, bf16[16,128,128]{2,1,0:T(8,128)(2,1)S(1)}, u32[]{:S(2)}, u32[]{:S(2)}) %collective-permute-start.12) | collective-permute-done | bytes 524320 | tf_op jit(solution)/shard_map/ppermute | solution.py:38
  51.4 0.4 turned.4
  51.8 3.5 %collective-permute-start.14 = (bf16[16,128,128]{2,1,0:T(8,128)(2,1)S(1)}, bf16[16,128,128]{2,1,0:T(8,128)(2,1)S(1)}, u32[]{:S(2)}, u32[]{:S(2)}) collective-permute-start(bf16[16,128,128]{2,1,0:T(8,128)(2,1)S(1)} %get-tuple-element.54.after.refs_2_), channel_id=1, source_target_pairs={{48,16},{80,48},{112,80},{0,32},{32,64},{64,96},{49,17},{81,49},{1... | collective-permute-start | bytes 1572872 | tf_op jit(solution)/shard_map/ppermute | solution.py:49
  55.3 0.4 collective-permute-start.13
  55.7 3.5 %others_1.1 = (f32[24,128,128]{2,1,0:T(8,128)S(1)}, bf16[24,128,128]{2,1,0:T(8,128)(2,1)S(1)}) custom-call(s32[40]{0:T(128)S(1)} %get-tuple-element.41.order, s32[12,40]{1,0:T(8,128)S(1)} %get-tuple-element.42.index, bf16[40,1536,128]{2,1,0:T(8,128)(2,1)S(1)} %bitcast.16, f32[40,128,128]{2,1,0:T(8,128)S(1)} %base_1.1.base, ...), custom_call_target="tpu_custom_call" | custom-call | tf_op jit(solution)/shard_map/others_1/pallas_call | solution.py:420
  59.2 3.7 %collective-permute-done.13.refs_9_ = bf16[8,128,128]{2,1,0:T(8,128)(2,1)S(1)} collective-permute-done((bf16[8,128,128]{2,1,0:T(8,128)(2,1)S(1)}, bf16[8,128,128]{2,1,0:T(8,128)(2,1)S(1)}, u32[]{:S(2)}, u32[]{:S(2)}) %collective-permute-start.13) | collective-permute-done | bytes 262176 | tf_op jit(solution)/shard_map/ppermute | solution.py:38
  62.9 1.5 %base_2.1.base = f32[40,128,128]{2,1,0:T(8,128)S(1)} custom-call(s32[2,8]{1,0:T(2,128)S(1)} %get-tuple-element.43.wall_at, s32[40]{0:T(128)S(1)} %get-tuple-element.41.order, f32[40,128,128]{2,1,0:T(8,128)S(1)} %copy-done.1, bf16[4,144,128]{2,1,0:T(8,128)(2,1)S(1)} %get-tuple-element.36.refs_0_, bf16[4,144,128]{2,1,0:T(8,128)(2,1)S(1)} %collective-permute-done.1.refs_1_, ...), custom_call_target="tpu_custom_call" | custom-call | tf_op jit(solution)/shard_map/base_2/pallas_call | solution.py:310
  64.4 2.7 %collective-permute-done.14.refs_3_ = bf16[16,128,128]{2,1,0:T(8,128)(2,1)S(1)} collective-permute-done((bf16[16,128,128]{2,1,0:T(8,128)(2,1)S(1)}, bf16[16,128,128]{2,1,0:T(8,128)(2,1)S(1)}, u32[]{:S(2)}, u32[]{:S(2)}) %collective-permute-start.14) | collective-permute-done | bytes 524320 | tf_op jit(solution)/shard_map/ppermute | solution.py:49
  67.1 2.9 %exports_2.1 = (f32[16,128,128]{2,1,0:T(8,128)S(1)}, bf16[16,128,128]{2,1,0:T(8,128)(2,1)S(1)}, bf16[104,128,128]{2,1,0:T(8,128)(2,1)S(1)}) custom-call(s32[40]{0:T(128)S(1)} %get-tuple-element.41.order, s32[12,40]{1,0:T(8,128)S(1)} %get-tuple-element.42.index, bf16[40,1536,128]{2,1,0:T(8,128)(2,1)S(1)} %bitcast.17, f32[40,128,128]{2,1,0:T(8,128)S(1)} %base_2.1.base, ...), custom_call_target="tpu_custom_call" | custom-call | flops 3100000000 | tf_op jit(solution)/shard_map/exports_2/pallas_call | solution.py:390
  70.0 0.3 collective-permute-start.18
  70.3 1.6 %collective-permute-start.16 = (bf16[16,128,128]{2,1,0:T(8,128)(2,1)S(1)}, bf16[16,128,128]{2,1,0:T(8,128)(2,1)S(1)}, u32[]{:S(2)}, u32[]{:S(2)}) collective-permute-start(bf16[16,128,128]{2,1,0:T(8,128)(2,1)S(1)} %get-tuple-element.59.after.refs_14_.refs_0_.refs_5_), channel_id=1, source_target_pairs={{0,16},{16,0},{32,48},{48,32},{64,80},{80,64},{96,112},{112,96},{1... | collective-permute-start | bytes 1572872 | tf_op jit(solution)/shard_map/ppermute | solution.py:38
  71.9 3.7 %others_2.1 = (f32[24,128,128]{2,1,0:T(8,128)S(1)}, bf16[24,128,128]{2,1,0:T(8,128)(2,1)S(1)}) custom-call(s32[40]{0:T(128)S(1)} %get-tuple-element.41.order, s32[12,40]{1,0:T(8,128)S(1)} %get-tuple-element.42.index, bf16[40,1536,128]{2,1,0:T(8,128)(2,1)S(1)} %bitcast.18, f32[40,128,128]{2,1,0:T(8,128)S(1)} %base_2.1.base, ...), custom_call_target="tpu_custom_call" | custom-call | tf_op jit(solution)/shard_map/others_2/pallas_call | solution.py:420
  75.6 1.2 %walls.1 = (bf16[4,256,128]{2,1,0:T(8,128)(2,1)S(1)}, bf16[4,256,128]{2,1,0:T(8,128)(2,1)S(1)}, bf16[4,256,128]{2,1,0:T(8,128)(2,1)S(1)}, bf16[4,256,128]{2,1,0:T(8,128)(2,1)S(1)}) custom-call(s32[2,8]{1,0:T(2,128)S(1)} %get-tuple-element.43.wall_at, bf16[4,144,128]{2,1,0:T(8,128)(2,1)S(1)} %get-tuple-element.36.refs_0_, ...), custom_call_target="tpu_custom_call" | custom-call | tf_op jit(solution)/shard_map/walls/pallas_call | solution.py:347
  76.8 1.6 %collective-permute-start.20 = (bf16[4,256,128]{2,1,0:T(8,128)(2,1)S(1)}, bf16[4,256,128]{2,1,0:T(8,128)(2,1)S(1)}, u32[]{:S(2)}, u32[]{:S(2)}) collective-permute-start(bf16[4,256,128]{2,1,0:T(8,128)(2,1)S(1)} %get-tuple-element.64), channel_id=1, source_target_pairs={{0,32},{16,48},{32,64},{48,80},{64,96},{80,112},{96,0},{112,16},{1... | collective-permute-start | bytes 786440 | tf_op jit(solution)/shard_map/ppermute | solution.py:43
  78.3 0.5 collective-permute-start.21
  78.9 1.0 collective-permute-start.22
  79.9 4.1 %collective-permute-start.19 = (bf16[16,128,128]{2,1,0:T(8,128)(2,1)S(1)}, bf16[16,128,128]{2,1,0:T(8,128)(2,1)S(1)}, u32[]{:S(2)}, u32[]{:S(2)}) collective-permute-start(bf16[16,128,128]{2,1,0:T(8,128)(2,1)S(1)} %collective-permute-done.18.refs_4_.refs_11_), channel_id=1, source_target_pairs={{0,2},{2,4},{4,6},{6,8},{8,10},{10,12},{12,14},{3,1},{5,3},{7,5},{... | collective-permute-start | bytes 1572872 | tf_op jit(solution)/shard_map/ppermute | solution.py:56
  83.9 0.7 collective-permute-done.16.refs_2_.refs_4_
  84.7 3.5 %collective-permute-start.17 = (bf16[16,128,128]{2,1,0:T(8,128)(2,1)S(1)}, bf16[16,128,128]{2,1,0:T(8,128)(2,1)S(1)}, u32[]{:S(2)}, u32[]{:S(2)}) collective-permute-start(bf16[16,128,128]{2,1,0:T(8,128)(2,1)S(1)} %collective-permute-done.16.refs_2_.refs_4_), channel_id=1, source_target_pairs={{48,16},{80,48},{112,80},{0,32},{32,64},{64,96},{49,17},{81,49},{1... | collective-permute-start | bytes 1572872 | tf_op jit(solution)/shard_map/ppermute | solution.py:49
  88.2 4.0 %collective-permute-done.21.refs_2_ = bf16[4,256,128]{2,1,0:T(8,128)(2,1)S(1)} collective-permute-done((bf16[4,256,128]{2,1,0:T(8,128)(2,1)S(1)}, bf16[4,256,128]{2,1,0:T(8,128)(2,1)S(1)}, u32[]{:S(2)}, u32[]{:S(2)}) %collective-permute-start.21) | collective-permute-done | bytes 262176 | tf_op jit(solution)/shard_map/ppermute | solution.py:43
  92.2 0.7 turned.5
  92.9 2.3 %collective-permute-start.23 = (bf16[8,256,128]{2,1,0:T(8,128)(2,1)S(1)}, bf16[8,256,128]{2,1,0:T(8,128)(2,1)S(1)}, u32[]{:S(2)}, u32[]{:S(2)}) collective-permute-start(bf16[8,256,128]{2,1,0:T(8,128)(2,1)S(1)} %turned.5), channel_id=1, source_target_pairs={{0,16},{16,0},{32,48},{48,32},{64,80},{80,64},{96,112},{112,96},{1... | collective-permute-start | bytes 1572872 | tf_op jit(solution)/shard_map/ppermute | solution.py:38
  95.2 1.6 %base_3.1.base = f32[40,128,128]{2,1,0:T(8,128)S(1)} custom-call(s32[2,8]{1,0:T(2,128)S(1)} %get-tuple-element.43.wall_at, s32[40]{0:T(128)S(1)} %get-tuple-element.41.order, f32[40,128,128]{2,1,0:T(8,128)S(1)} %copy-done.1, bf16[4,144,128]{2,1,0:T(8,128)(2,1)S(1)} %get-tuple-element.36.refs_0_, bf16[4,144,128]{2,1,0:T(8,128)(2,1)S(1)} %collective-permute-done.1.refs_1_, ...), custom_call_target="tpu_custom_call" | custom-call | tf_op jit(solution)/shard_map/base_3/pallas_call | solution.py:310
  96.7 5.5 %collective-permute-done.17.refs_3_ = bf16[16,128,128]{2,1,0:T(8,128)(2,1)S(1)} collective-permute-done((bf16[16,128,128]{2,1,0:T(8,128)(2,1)S(1)}, bf16[16,128,128]{2,1,0:T(8,128)(2,1)S(1)}, u32[]{:S(2)}, u32[]{:S(2)}) %collective-permute-start.17) | collective-permute-done | bytes 524320 | tf_op jit(solution)/shard_map/ppermute | solution.py:49
  102.2 4.8 %last.1 = (f32[40,128,128]{2,1,0:T(8,128)}, bf16[104,128,128]{2,1,0:T(8,128)(2,1)S(1)}) custom-call(s32[40]{0:T(128)S(1)} %get-tuple-element.41.order, s32[12,40]{1,0:T(8,128)S(1)} %get-tuple-element.42.index, bf16[40,1536,128]{2,1,0:T(8,128)(2,1)S(1)} %bitcast.19, f32[40,128,128]{2,1,0:T(8,128)S(1)} %base_3.1.base, ...), custom_call_target="tpu_custom_call" | custom-call | tf_op jit(solution)/shard_map/last/pallas_call | solution.py:453
  107.0 4.4 %end.1 = (f32[40,128,128]{2,1,0:T(8,128)}, f32[16,2,128,128]{3,2,1,0:T(8,128)}) custom-call(s32[40]{0:T(128)S(1)} %get-tuple-element.41.order, s32[12,40]{1,0:T(8,128)S(1)} %get-tuple-element.42.index, s32[2,8]{1,0:T(2,128)S(1)} %bitcast.24, f32[2,16]{1,0:T(2,128)S(1)} %bitcast.28, f32[2,16]{1,0:T(2,128)S(1)} %bitcast.26, ...), custom_call_target="tpu_custom_call", output_to_operand_aliasing={{0}: (14, {})} | custom-call | tf_op jit(solution)/shard_map/end/pallas_call | solution.py:502
  (33 shorter events, 0.1 us)
Async XLA Ops:
  0.6 4.7 %copy-start.4 = (s32[1,1,8,2]{2,3,1,0:T(2,128)S(1)}, s32[1,1,8,2]{2,3,1,0:T(2,128)}, u32[]{:S(2)}) copy-start(s32[1,1,8,2]{2,3,1,0:T(2,128)} %param.19) | copy-start | bytes 196
  0.6 4.8 %copy-start.5 = (f32[16,2]{0,1:T(2,128)S(1)}, f32[16,2]{0,1:T(2,128)}, u32[]{:S(2)}) copy-start(f32[16,2]{0,1:T(2,128)} %param.22) | copy-start | bytes 388
  0.7 4.9 %copy-start.6 = (f32[16,2]{0,1:T(2,128)S(1)}, f32[16,2]{0,1:T(2,128)}, u32[]{:S(2)}) copy-start(f32[16,2]{0,1:T(2,128)} %param.21) | copy-start | bytes 388
  0.7 4.9 %copy-start.12 = (f32[16]{0:T(128)S(1)}, f32[16]{0:T(128)}, u32[]{:S(2)}) copy-start(f32[16]{0:T(128)} %param.23) | copy-start | bytes 196
  0.7 5.2 %copy-start.3 = (f32[1,1,8,2,2,128,128]{6,5,4,3,2,1,0:T(8,128)S(1)}, f32[1,1,8,2,2,128,128]{6,5,4,3,2,1,0:T(8,128)}, u32[]{:S(2)}) copy-start(f32[1,1,8,2,2,128,128]{6,5,4,3,2,1,0:T(8,128)} %param.20) | copy-start | bytes 6291460
  0.7 5.2 %copy-start.9 = (f32[1,1,8,2,128]{4,3,2,1,0:T(2,128)S(1)}, f32[1,1,8,2,128]{4,3,2,1,0:T(2,128)}, u32[]{:S(2)}) copy-start(f32[1,1,8,2,128]{4,3,2,1,0:T(2,128)} %param.18) | copy-start | bytes 24580
  3.7 2.2 %collective-permute-start = (bf16[16,128,128]{2,1,0:T(8,128)(2,1)}, bf16[16,128,128]{2,1,0:T(8,128)(2,1)S(1)}, u32[]{:S(2)}, u32[]{:S(2)}) collective-permute-start(bf16[16,128,128]{2,1,0:T(8,128)(2,1)} %exports.1.refs_5_.refs_0_.refs_14_.refs_18_.refs_9_), channel_id=1, source_target_pairs={{0,1},{1,0},{2,3},{3,2},{4,5},{5,4},{6,7},{7,6},{8,9},{9,8},{10,11... | collective-permute-start | bytes 1572872 | tf_op jit(solution)/shard_map/ppermute | solution.py:54
  3.8 14.6 %collective-permute-start.4 = (bf16[16,128,128]{2,1,0:T(8,128)(2,1)}, bf16[16,128,128]{2,1,0:T(8,128)(2,1)S(1)}, u32[]{:S(2)}, u32[]{:S(2)}) collective-permute-start(bf16[16,128,128]{2,1,0:T(8,128)(2,1)} %exports.1.refs_5_.refs_0_.refs_14_.refs_18_.refs_9_), channel_id=1, source_target_pairs={{0,16},{16,0},{32,48},{48,32},{64,80},{80,64},{96,112},{112,96},{1... | collective-permute-start | bytes 1572872 | tf_op jit(solution)/shard_map/ppermute | solution.py:38
  6.7 16.1 %copy-start.1 = (f32[40,128,128]{2,1,0:T(8,128)S(1)}, f32[40,128,128]{2,1,0:T(8,128)}, u32[]{:S(2)}) copy-start(f32[40,128,128]{2,1,0:T(8,128)} %pressure.9) | copy-start | bytes 7864324
  6.7 16.1 %copy-start.7 = (s32[40,12]{0,1:T(8,128)S(1)}, s32[40,12]{0,1:T(8,128)}, u32[]{:S(2)}) copy-start(s32[40,12]{0,1:T(8,128)} %param.14) | copy-start | bytes 5764
  6.7 16.1 %copy-start.8 = (s32[40,12]{0,1:T(8,128)S(1)}, s32[40,12]{0,1:T(8,128)}, u32[]{:S(2)}) copy-start(s32[40,12]{0,1:T(8,128)} %param.15) | copy-start | bytes 5764
  6.7 16.1 %copy-start.10 = (s32[1,1,8,2]{2,3,1,0:T(2,128)S(1)}, s32[1,1,8,2]{2,3,1,0:T(2,128)}, u32[]{:S(2)}) copy-start(s32[1,1,8,2]{2,3,1,0:T(2,128)} %param.17) | copy-start | bytes 196
  6.8 16.1 %copy-start.11 = (s32[16]{0:T(128)S(1)}, s32[16]{0:T(128)}, u32[]{:S(2)}) copy-start(s32[16]{0:T(128)} %ids.3) | copy-start | bytes 196
  6.8 11.6 %collective-permute-start.1 = (bf16[4,144,128]{2,1,0:T(8,128)(2,1)S(1)}, bf16[4,144,128]{2,1,0:T(8,128)(2,1)S(1)}, u32[]{:S(2)}, u32[]{:S(2)}) collective-permute-start(bf16[4,144,128]{2,1,0:T(8,128)(2,1)S(1)} %get-tuple-element.37), channel_id=1, source_target_pairs={{0,32},{16,48},{32,64},{48,80},{64,96},{80,112},{96,0},{112,16},{1... | collective-permute-start | bytes 442376 | tf_op jit(solution)/shard_map/ppermute | solution.py:43
  8.4 9.9 %collective-permute-start.2 = (bf16[4,144,128]{2,1,0:T(8,128)(2,1)S(1)}, bf16[4,144,128]{2,1,0:T(8,128)(2,1)S(1)}, u32[]{:S(2)}, u32[]{:S(2)}) collective-permute-start(bf16[4,144,128]{2,1,0:T(8,128)(2,1)S(1)} %get-tuple-element.38), channel_id=1, source_target_pairs={{0,96},{16,112},{32,0},{48,16},{64,32},{80,48},{96,64},{112,80},{1... | collective-permute-start | bytes 442376 | tf_op jit(solution)/shard_map/ppermute | solution.py:43
  8.9 9.5 %collective-permute-start.3 = (bf16[4,144,128]{2,1,0:T(8,128)(2,1)S(1)}, bf16[4,144,128]{2,1,0:T(8,128)(2,1)S(1)}, u32[]{:S(2)}, u32[]{:S(2)}) collective-permute-start(bf16[4,144,128]{2,1,0:T(8,128)(2,1)S(1)} %get-tuple-element.39), channel_id=1, source_target_pairs={{0,64},{16,80},{32,96},{48,112},{64,0},{80,16},{96,32},{112,48},{1... | collective-permute-start | bytes 442376 | tf_op jit(solution)/shard_map/ppermute | solution.py:43
  11.2 20.8 %collective-permute-start.7 = (bf16[16,128,128]{2,1,0:T(8,128)(2,1)S(1)}, bf16[16,128,128]{2,1,0:T(8,128)(2,1)S(1)}, u32[]{:S(2)}, u32[]{:S(2)}) collective-permute-start(bf16[16,128,128]{2,1,0:T(8,128)(2,1)S(1)} %collective-permute-done.after.value), channel_id=1, source_target_pairs={{0,2},{2,4},{4,6},{6,8},{8,10},{10,12},{12,14},{3,1},{5,3},{7,5},{... | collective-permute-start | bytes 1572872 | tf_op jit(solution)/shard_map/ppermute | solution.py:56
  18.3 12.3 %copy-start.2 = (bf16[16,128,128]{2,1,0:T(8,128)(2,1)S(1)}, bf16[16,128,128]{2,1,0:T(8,128)(2,1)}, u32[]{:S(2)}) copy-start(bf16[16,128,128]{2,1,0:T(8,128)(2,1)} %exports.1.refs_5_.refs_0_.refs_14_.refs_18_.refs_9_) | copy-start | bytes 1572868
  18.8 15.4 %collective-permute-start.6 = (bf16[16,128,128]{2,1,0:T(8,128)(2,1)S(1)}, bf16[16,128,128]{2,1,0:T(8,128)(2,1)S(1)}, u32[]{:S(2)}, u32[]{:S(2)}) collective-permute-start(bf16[16,128,128]{2,1,0:T(8,128)(2,1)S(1)} %get-tuple-element.40.after.refs_2_), channel_id=1, source_target_pairs={{48,16},{80,48},{112,80},{0,32},{32,64},{64,96},{49,17},{81,49},{1... | collective-permute-start | bytes 1572872 | tf_op jit(solution)/shard_map/ppermute | solution.py:49
  22.3 8.4 %collective-permute-start.5 = (bf16[8,144,128]{2,1,0:T(8,128)(2,1)S(1)}, bf16[8,144,128]{2,1,0:T(8,128)(2,1)S(1)}, u32[]{:S(2)}, u32[]{:S(2)}) collective-permute-start(bf16[8,144,128]{2,1,0:T(8,128)(2,1)S(1)} %get-tuple-element.44), channel_id=1, source_target_pairs={{0,16},{16,0},{32,48},{48,32},{64,80},{80,64},{96,112},{112,96},{1... | collective-permute-start | bytes 884744 | tf_op jit(solution)/shard_map/ppermute | solution.py:38
  22.7 11.4 %copy-start = (bf16[40,12,128,128]{3,2,1,0:T(8,128)(2,1)S(1)}, bf16[40,12,128,128]{3,2,1,0:T(8,128)(2,1)}, u32[]{:S(2)}) copy-start(bf16[40,12,128,128]{3,2,1,0:T(8,128)(2,1)} %param.13) | copy-start | bytes 47185924
  36.9 2.0 %collective-permute-start.8 = (bf16[16,128,128]{2,1,0:T(8,128)(2,1)S(1)}, bf16[16,128,128]{2,1,0:T(8,128)(2,1)S(1)}, u32[]{:S(2)}, u32[]{:S(2)}) collective-permute-start(bf16[16,128,128]{2,1,0:T(8,128)(2,1)S(1)} %get-tuple-element.46.refs_12_.refs_0_.refs_16_.refs_7_), channel_id=1, source_target_pairs={{0,1},{1,0},{2,3},{3,2},{4,5},{5,4},{6,7},{7,6},{8,9},{9,8},{10,11... | collective-permute-start | bytes 1572872 | tf_op jit(solution)/shard_map/ppermute | solution.py:54
  37.0 14.3 %collective-permute-start.12 = (bf16[16,128,128]{2,1,0:T(8,128)(2,1)S(1)}, bf16[16,128,128]{2,1,0:T(8,128)(2,1)S(1)}, u32[]{:S(2)}, u32[]{:S(2)}) collective-permute-start(bf16[16,128,128]{2,1,0:T(8,128)(2,1)S(1)} %get-tuple-element.46.refs_12_.refs_0_.refs_16_.refs_7_), channel_id=1, source_target_pairs={{0,16},{16,0},{32,48},{48,32},{64,80},{80,64},{96,112},{112,96},{1... | collective-permute-start | bytes 1572872 | tf_op jit(solution)/shard_map/ppermute | solution.py:38
  39.7 11.6 %collective-permute-start.9 = (bf16[4,128,128]{2,1,0:T(8,128)(2,1)S(1)}, bf16[4,128,128]{2,1,0:T(8,128)(2,1)S(1)}, u32[]{:S(2)}, u32[]{:S(2)}) collective-permute-start(bf16[4,128,128]{2,1,0:T(8,128)(2,1)S(1)} %get-tuple-element.48), channel_id=1, source_target_pairs={{0,32},{16,48},{32,64},{48,80},{64,96},{80,112},{96,0},{112,16},{1... | collective-permute-start | bytes 393224 | tf_op jit(solution)/shard_map/ppermute | solution.py:43
  41.4 10.0 %collective-permute-start.10 = (bf16[4,128,128]{2,1,0:T(8,128)(2,1)S(1)}, bf16[4,128,128]{2,1,0:T(8,128)(2,1)S(1)}, u32[]{:S(2)}, u32[]{:S(2)}) collective-permute-start(bf16[4,128,128]{2,1,0:T(8,128)(2,1)S(1)} %get-tuple-element.49), channel_id=1, source_target_pairs={{0,96},{16,112},{32,0},{48,16},{64,32},{80,48},{96,64},{112,80},{1... | collective-permute-start | bytes 393224 | tf_op jit(solution)/shard_map/ppermute | solution.py:43
  41.8 9.6 %collective-permute-start.11 = (bf16[4,128,128]{2,1,0:T(8,128)(2,1)S(1)}, bf16[4,128,128]{2,1,0:T(8,128)(2,1)S(1)}, u32[]{:S(2)}, u32[]{:S(2)}) collective-permute-start(bf16[4,128,128]{2,1,0:T(8,128)(2,1)S(1)} %get-tuple-element.50), channel_id=1, source_target_pairs={{0,64},{16,80},{32,96},{48,112},{64,0},{80,16},{96,32},{112,48},{1... | collective-permute-start | bytes 393224 | tf_op jit(solution)/shard_map/ppermute | solution.py:43
  44.1 20.3 %collective-permute-start.15 = (bf16[16,128,128]{2,1,0:T(8,128)(2,1)S(1)}, bf16[16,128,128]{2,1,0:T(8,128)(2,1)S(1)}, u32[]{:S(2)}, u32[]{:S(2)}) collective-permute-start(bf16[16,128,128]{2,1,0:T(8,128)(2,1)S(1)} %collective-permute-done.8.after.refs_4_), channel_id=1, source_target_pairs={{0,2},{2,4},{4,6},{6,8},{8,10},{10,12},{12,14},{3,1},{5,3},{7,5},{... | collective-permute-start | bytes 1572872 | tf_op jit(solution)/shard_map/ppermute | solution.py:56
  51.8 15.4 %collective-permute-start.14 = (bf16[16,128,128]{2,1,0:T(8,128)(2,1)S(1)}, bf16[16,128,128]{2,1,0:T(8,128)(2,1)S(1)}, u32[]{:S(2)}, u32[]{:S(2)}) collective-permute-start(bf16[16,128,128]{2,1,0:T(8,128)(2,1)S(1)} %get-tuple-element.54.after.refs_2_), channel_id=1, source_target_pairs={{48,16},{80,48},{112,80},{0,32},{32,64},{64,96},{49,17},{81,49},{1... | collective-permute-start | bytes 1572872 | tf_op jit(solution)/shard_map/ppermute | solution.py:49
  55.3 7.6 %collective-permute-start.13 = (bf16[8,128,128]{2,1,0:T(8,128)(2,1)S(1)}, bf16[8,128,128]{2,1,0:T(8,128)(2,1)S(1)}, u32[]{:S(2)}, u32[]{:S(2)}) collective-permute-start(bf16[8,128,128]{2,1,0:T(8,128)(2,1)S(1)} %get-tuple-element.51), channel_id=1, source_target_pairs={{0,16},{16,0},{32,48},{48,32},{64,80},{80,64},{96,112},{112,96},{1... | collective-permute-start | bytes 786440 | tf_op jit(solution)/shard_map/ppermute | solution.py:38
  70.0 5.5 %collective-permute-start.18 = (bf16[16,128,128]{2,1,0:T(8,128)(2,1)S(1)}, bf16[16,128,128]{2,1,0:T(8,128)(2,1)S(1)}, u32[]{:S(2)}, u32[]{:S(2)}) collective-permute-start(bf16[16,128,128]{2,1,0:T(8,128)(2,1)S(1)} %get-tuple-element.59.after.refs_14_.refs_0_.refs_5_), channel_id=1, source_target_pairs={{0,1},{1,0},{2,3},{3,2},{4,5},{5,4},{6,7},{7,6},{8,9},{9,8},{10,11... | collective-permute-start | bytes 1572872 | tf_op jit(solution)/shard_map/ppermute | solution.py:54
  70.3 14.3 %collective-permute-start.16 = (bf16[16,128,128]{2,1,0:T(8,128)(2,1)S(1)}, bf16[16,128,128]{2,1,0:T(8,128)(2,1)S(1)}, u32[]{:S(2)}, u32[]{:S(2)}) collective-permute-start(bf16[16,128,128]{2,1,0:T(8,128)(2,1)S(1)} %get-tuple-element.59.after.refs_14_.refs_0_.refs_5_), channel_id=1, source_target_pairs={{0,16},{16,0},{32,48},{48,32},{64,80},{80,64},{96,112},{112,96},{1... | collective-permute-start | bytes 1572872 | tf_op jit(solution)/shard_map/ppermute | solution.py:38
  76.8 11.4 %collective-permute-start.20 = (bf16[4,256,128]{2,1,0:T(8,128)(2,1)S(1)}, bf16[4,256,128]{2,1,0:T(8,128)(2,1)S(1)}, u32[]{:S(2)}, u32[]{:S(2)}) collective-permute-start(bf16[4,256,128]{2,1,0:T(8,128)(2,1)S(1)} %get-tuple-element.64), channel_id=1, source_target_pairs={{0,32},{16,48},{32,64},{48,80},{64,96},{80,112},{96,0},{112,16},{1... | collective-permute-start | bytes 786440 | tf_op jit(solution)/shard_map/ppermute | solution.py:43
  78.3 13.9 %collective-permute-start.21 = (bf16[4,256,128]{2,1,0:T(8,128)(2,1)S(1)}, bf16[4,256,128]{2,1,0:T(8,128)(2,1)S(1)}, u32[]{:S(2)}, u32[]{:S(2)}) collective-permute-start(bf16[4,256,128]{2,1,0:T(8,128)(2,1)S(1)} %get-tuple-element.65), channel_id=1, source_target_pairs={{0,96},{16,112},{32,0},{48,16},{64,32},{80,48},{96,64},{112,80},{1... | collective-permute-start | bytes 786440 | tf_op jit(solution)/shard_map/ppermute | solution.py:43
  78.9 13.3 %collective-permute-start.22 = (bf16[4,256,128]{2,1,0:T(8,128)(2,1)S(1)}, bf16[4,256,128]{2,1,0:T(8,128)(2,1)S(1)}, u32[]{:S(2)}, u32[]{:S(2)}) collective-permute-start(bf16[4,256,128]{2,1,0:T(8,128)(2,1)S(1)} %get-tuple-element.66), channel_id=1, source_target_pairs={{0,64},{16,80},{32,96},{48,112},{64,0},{80,16},{96,32},{112,48},{1... | collective-permute-start | bytes 786440 | tf_op jit(solution)/shard_map/ppermute | solution.py:43
  79.9 22.4 %collective-permute-start.19 = (bf16[16,128,128]{2,1,0:T(8,128)(2,1)S(1)}, bf16[16,128,128]{2,1,0:T(8,128)(2,1)S(1)}, u32[]{:S(2)}, u32[]{:S(2)}) collective-permute-start(bf16[16,128,128]{2,1,0:T(8,128)(2,1)S(1)} %collective-permute-done.18.refs_4_.refs_11_), channel_id=1, source_target_pairs={{0,2},{2,4},{4,6},{6,8},{8,10},{10,12},{12,14},{3,1},{5,3},{7,5},{... | collective-permute-start | bytes 1572872 | tf_op jit(solution)/shard_map/ppermute | solution.py:56
  84.7 17.6 %collective-permute-start.17 = (bf16[16,128,128]{2,1,0:T(8,128)(2,1)S(1)}, bf16[16,128,128]{2,1,0:T(8,128)(2,1)S(1)}, u32[]{:S(2)}, u32[]{:S(2)}) collective-permute-start(bf16[16,128,128]{2,1,0:T(8,128)(2,1)S(1)} %collective-permute-done.16.refs_2_.refs_4_), channel_id=1, source_target_pairs={{48,16},{80,48},{112,80},{0,32},{32,64},{64,96},{49,17},{81,49},{1... | collective-permute-start | bytes 1572872 | tf_op jit(solution)/shard_map/ppermute | solution.py:49
  92.9 14.1 %collective-permute-start.23 = (bf16[8,256,128]{2,1,0:T(8,128)(2,1)S(1)}, bf16[8,256,128]{2,1,0:T(8,128)(2,1)S(1)}, u32[]{:S(2)}, u32[]{:S(2)}) collective-permute-start(bf16[8,256,128]{2,1,0:T(8,128)(2,1)S(1)} %turned.5), channel_id=1, source_target_pairs={{0,16},{16,0},{32,48},{48,32},{64,80},{80,64},{96,112},{112,96},{1... | collective-permute-start | bytes 1572872 | tf_op jit(solution)/shard_map/ppermute | solution.py:38

commit v6 on v5

--- a/solution.py
+++ b/solution.py
@@ -47,6 +47,12 @@
     gx = lax.axis_size("gx")
     on = [(i, i - 2) for i in range(3, gx, 2)] + [(i, i + 2) for i in range(0, gx - 2, 2)]
     return lax.ppermute(across, "gx", on)
+
+
+def passed_before(part):
+    gx = lax.axis_size("gx")
+    on = [(i, i - 2) for i in range(2, gx, 2)] + [(i, i + 2) for i in range(1, gx - 2, 2)]
+    return lax.ppermute(part, "gx", on)
 
 
 def beside_of(exports):
@@ -572,12 +578,14 @@
     p2_first, e3, pool = first_blocks(order, index, tiles, base, (e2, o2) + around, "exports_2")
 
     across, core, beside = beside_of(e3)
-    around = (across, passed_on(across), core, beside)
+    cut = 5 * exports // 8
+    turning = passed_before(e3[cut:])
+    around = (across, passed_on(across[:cut]), other_x(turning), core, beside)
     p2_other, o3 = other_blocks(order, index, tiles, base, pool, blocks - exports, e3, "others_2")
     p2 = (p2_first, p2_other)
     rounded = ((e3, o3), (e2, o2), (e1, o1))
-    walls = over_y(walls_of(wall_at, message, rounded, (core,)))
-    (walls,) = over_x(walls, (), (across,))
+    walls = over_y(walls_of(wall_at, message, rounded, (core, turning)))
+    (walls,) = over_x(walls, (), (across, around[2]))
     base = base_of(3, wall_at, order, (message, later), pressure, (p2, p1), rounded)
     ahead = blocks - exports
     p3, pool = last_blocks(order, index, tiles, base, (e3, o3) + around, ahead)

time: 113 us -> 122 us (1.080)
  the two profiles are of different devices: /device:TPU:40 before, /device:TPU:4 now
where the time goes in v6:
time: 122 us; the launch traced here: 123 us
  starting transfers between devices  48.6 us (40%)
  Pallas kernels  36.6 us (30%)
  waiting for transfers between devices  35.6 us (29%)
  between operations  1.24 us (1%)
    ppermute x7, waiting for transfers between devices, other_x(): return lax.ppermute(value, 'gx', [(i, i ^ 1) for i in range(count)])  21.3 us
    ppermute x9, starting transfers between devices, along_y(): lax.ppermute(value, 'gx', [(i, (i + 2 * steps) % count) for i in range(co...  16.5 us
    ppermute x3, starting transfers between devices, beside_of(): return (other_x(exports), core, lax.ppermute(core, 'gy', on))  11.4 us
    ppermute x3, starting transfers between devices, passed_on(): return lax.ppermute(across, 'gx', on)  10.9 us
    ppermute x7, starting transfers between devices, other_x(): return lax.ppermute(value, 'gx', [(i, i ^ 1) for i in range(count)])  8.07 us
    pallas_call x2, Pallas kernels, other_blocks(): pl.pallas_call(other_kernel, out_shape=(jax.ShapeDtypeStruct((count, rows...  6.94 us
    pallas_call x2, Pallas kernels, first_blocks(): pl.pallas_call(first_kernel, out_shape=(jax.ShapeDtypeStruct((exports, ro...  5.56 us
    ppermute x3, waiting for transfers between devices, beside_of(): return (other_x(exports), core, lax.ppermute(core, 'gy', on))  5.53 us
  transfers between devices with their start and end apart: 26, of which 10 were waited for; matrix products, arithmetic and copies ran while one was open for 0% of the time, Pallas kernels for 19%

profile of v6, /device:TPU:4, one launch (start us, length us, event | category | flops | bytes accessed | tf_op | source)
XLA Modules:
  0.0 122.6 jit_solution(4890992007959385001)
XLA Ops:
  0.7 3.0 %exports.1.refs_5_.refs_0_.refs_14_.refs_18_.refs_9_ = bf16[16,128,128]{2,1,0:T(8,128)(2,1)} custom-call(s32[16]{0:T(128)} %ids.3, f32[40,128,128]{2,1,0:T(8,128)} %pressure.9), custom_call_target="tpu_custom_call" | custom-call | flops 3000000000 | tf_op jit(solution)/shard_map/exports/pallas_call | solution.py:137
  3.7 0.1 collective-permute-start
  3.8 1.3 %collective-permute-start.4 = (bf16[16,128,128]{2,1,0:T(8,128)(2,1)}, bf16[16,128,128]{2,1,0:T(8,128)(2,1)S(1)}, u32[]{:S(2)}, u32[]{:S(2)}) collective-permute-start(bf16[16,128,128]{2,1,0:T(8,128)(2,1)} %exports.1.refs_5_.refs_0_.refs_14_.refs_18_.refs_9_), channel_id=1, source_target_pairs={{0,16},{16,0},{32,48},{48,32},{64,80},{80,64},{96,112},{112,96},{1... | collective-permute-start | bytes 1572872 | tf_op jit(solution)/shard_map/ppermute | solution.py:38
  5.0 0.1 reshape.35
  5.1 0.1 reshape.33
  5.2 0.1 reshape.32
  5.3 0.1 pad_maximum_fusion.table
  5.4 0.5 collective-permute-done.after.value
  5.9 0.8 responses_1.1
  6.7 0.0 copy-start.1
  6.7 0.0 copy-start.7
  6.7 0.0 copy-start.8
  6.7 0.0 copy-start.10
  6.8 0.0 copy-start.11
  6.8 1.6 %collective-permute-start.1 = (bf16[4,144,128]{2,1,0:T(8,128)(2,1)S(1)}, bf16[4,144,128]{2,1,0:T(8,128)(2,1)S(1)}, u32[]{:S(2)}, u32[]{:S(2)}) collective-permute-start(bf16[4,144,128]{2,1,0:T(8,128)(2,1)S(1)} %get-tuple-element.37), channel_id=1, source_target_pairs={{0,32},{16,48},{32,64},{48,80},{64,96},{80,112},{96,0},{112,16},{1... | collective-permute-start | bytes 442376 | tf_op jit(solution)/shard_map/ppermute | solution.py:43
  8.4 1.7 %collective-permute-start.2 = (bf16[4,144,128]{2,1,0:T(8,128)(2,1)S(1)}, bf16[4,144,128]{2,1,0:T(8,128)(2,1)S(1)}, u32[]{:S(2)}, u32[]{:S(2)}) collective-permute-start(bf16[4,144,128]{2,1,0:T(8,128)(2,1)S(1)} %get-tuple-element.38), channel_id=1, source_target_pairs={{0,96},{16,112},{32,0},{48,16},{64,32},{80,48},{96,64},{112,80},{1... | collective-permute-start | bytes 442376 | tf_op jit(solution)/shard_map/ppermute | solution.py:43
  10.1 2.0 %collective-permute-start.3 = (bf16[4,144,128]{2,1,0:T(8,128)(2,1)S(1)}, bf16[4,144,128]{2,1,0:T(8,128)(2,1)S(1)}, u32[]{:S(2)}, u32[]{:S(2)}) collective-permute-start(bf16[4,144,128]{2,1,0:T(8,128)(2,1)S(1)} %get-tuple-element.39), channel_id=1, source_target_pairs={{0,64},{16,80},{32,96},{48,112},{64,0},{80,16},{96,32},{112,48},{1... | collective-permute-start | bytes 442376 | tf_op jit(solution)/shard_map/ppermute | solution.py:43
  12.1 3.8 %collective-permute-start.7 = (bf16[16,128,128]{2,1,0:T(8,128)(2,1)S(1)}, bf16[16,128,128]{2,1,0:T(8,128)(2,1)S(1)}, u32[]{:S(2)}, u32[]{:S(2)}) collective-permute-start(bf16[16,128,128]{2,1,0:T(8,128)(2,1)S(1)} %collective-permute-done.after.value), channel_id=1, source_target_pairs={{0,2},{2,4},{4,6},{6,8},{8,10},{10,12},{12,14},{3,1},{5,3},{7,5},{... | collective-permute-start | bytes 1572872 | tf_op jit(solution)/shard_map/ppermute | solution.py:62
  15.9 2.4 %collective-permute-done.4.refs_4_ = bf16[16,128,128]{2,1,0:T(8,128)(2,1)S(1)} collective-permute-done((bf16[16,128,128]{2,1,0:T(8,128)(2,1)}, bf16[16,128,128]{2,1,0:T(8,128)(2,1)S(1)}, u32[]{:S(2)}, u32[]{:S(2)}) %collective-permute-start.4) | collective-permute-done | bytes 524320 | tf_op jit(solution)/shard_map/ppermute | solution.py:38
  18.3 0.0 collective-permute-done.3.refs_3_
  18.3 0.4 turned.3
  18.8 3.5 %collective-permute-start.6 = (bf16[16,128,128]{2,1,0:T(8,128)(2,1)S(1)}, bf16[16,128,128]{2,1,0:T(8,128)(2,1)S(1)}, u32[]{:S(2)}, u32[]{:S(2)}) collective-permute-start(bf16[16,128,128]{2,1,0:T(8,128)(2,1)S(1)} %get-tuple-element.40.after.refs_2_), channel_id=1, source_target_pairs={{48,16},{80,48},{112,80},{0,32},{32,64},{64,96},{49,17},{81,49},{1... | collective-permute-start | bytes 1572872 | tf_op jit(solution)/shard_map/ppermute | solution.py:49
  22.3 0.1 collective-permute-start.5
  22.4 0.0 copy-start
  22.5 2.1 %prepare.1 = (s32[40]{0:T(128)S(1)}, s32[12,40]{1,0:T(8,128)S(1)}, s32[2,8]{1,0:T(2,128)S(1)}, bf16[24,128,128]{2,1,0:T(8,128)(2,1)S(1)}) custom-call(s32[16]{0:T(128)S(1)} %copy-done.11, s32[12,40]{1,0:T(8,128)S(1)} %bitcast.29, s32[12,40]{1,0:T(8,128)S(1)} %bitcast.30, s32[2,8]{1,0:T(2,128)S(1)} %bitcast.33, f32[40,128,128]{2,1,0:T(8,128)S(1)} %copy-done.1, ...), custom_call_target="tpu_custom_call" | custom-call | flops 2100000000 | tf_op jit(solution)/shard_map/prepare/pallas_call | solution.py:191
  24.7 7.2 %collective-permute-done.5.refs_4_ = bf16[8,144,128]{2,1,0:T(8,128)(2,1)S(1)} collective-permute-done((bf16[8,144,128]{2,1,0:T(8,128)(2,1)S(1)}, bf16[8,144,128]{2,1,0:T(8,128)(2,1)S(1)}, u32[]{:S(2)}, u32[]{:S(2)}) %collective-permute-start.5) | collective-permute-done | bytes 294944 | tf_op jit(solution)/shard_map/ppermute | solution.py:38
  31.8 1.4 %base_1.1.base = f32[40,128,128]{2,1,0:T(8,128)S(1)} custom-call(s32[2,8]{1,0:T(2,128)S(1)} %get-tuple-element.43.wall_at, s32[40]{0:T(128)S(1)} %get-tuple-element.41.order, f32[40,128,128]{2,1,0:T(8,128)S(1)} %copy-done.1, bf16[4,144,128]{2,1,0:T(8,128)(2,1)S(1)} %get-tuple-element.36.refs_0_, bf16[4,144,128]{2,1,0:T(8,128)(2,1)S(1)} %collective-permute-done.1.refs_1_, ...), custom_call_target="tpu_custom_call" | custom-call | flops 1600000000 | tf_op jit(solution)/shard_map/base_1/pallas_call | solution.py:316
  33.3 2.8 %exports_1.1 = (f32[16,128,128]{2,1,0:T(8,128)S(1)}, bf16[16,128,128]{2,1,0:T(8,128)(2,1)S(1)}, bf16[104,128,128]{2,1,0:T(8,128)(2,1)S(1)}) custom-call(s32[40]{0:T(128)S(1)} %get-tuple-element.41.order, s32[12,40]{1,0:T(8,128)S(1)} %get-tuple-element.42.index, bf16[40,1536,128]{2,1,0:T(8,128)(2,1)S(1)} %bitcast.15, f32[40,128,128]{2,1,0:T(8,128)S(1)} %base_1.1.base, ...), custom_call_target="tpu_custom_call" | custom-call | flops 3100000000 | tf_op jit(solution)/shard_map/exports_1/pallas_call | solution.py:396
  36.1 0.1 collective-permute-start.8
  36.2 2.2 %collective-permute-start.12 = (bf16[16,128,128]{2,1,0:T(8,128)(2,1)S(1)}, bf16[16,128,128]{2,1,0:T(8,128)(2,1)S(1)}, u32[]{:S(2)}, u32[]{:S(2)}) collective-permute-start(bf16[16,128,128]{2,1,0:T(8,128)(2,1)S(1)} %get-tuple-element.46.refs_12_.refs_0_.refs_16_.refs_7_), channel_id=1, source_target_pairs={{0,16},{16,0},{32,48},{48,32},{64,80},{80,64},{96,112},{112,96},{1... | collective-permute-start | bytes 1572872 | tf_op jit(solution)/shard_map/ppermute | solution.py:38
  38.3 0.8 responses_2.1
  39.1 2.3 %collective-permute-start.9 = (bf16[4,128,128]{2,1,0:T(8,128)(2,1)S(1)}, bf16[4,128,128]{2,1,0:T(8,128)(2,1)S(1)}, u32[]{:S(2)}, u32[]{:S(2)}) collective-permute-start(bf16[4,128,128]{2,1,0:T(8,128)(2,1)S(1)} %get-tuple-element.48), channel_id=1, source_target_pairs={{0,32},{16,48},{32,64},{48,80},{64,96},{80,112},{96,0},{112,16},{1... | collective-permute-start | bytes 393224 | tf_op jit(solution)/shard_map/ppermute | solution.py:43
  41.4 1.5 %collective-permute-start.10 = (bf16[4,128,128]{2,1,0:T(8,128)(2,1)S(1)}, bf16[4,128,128]{2,1,0:T(8,128)(2,1)S(1)}, u32[]{:S(2)}, u32[]{:S(2)}) collective-permute-start(bf16[4,128,128]{2,1,0:T(8,128)(2,1)S(1)} %get-tuple-element.49), channel_id=1, source_target_pairs={{0,96},{16,112},{32,0},{48,16},{64,32},{80,48},{96,64},{112,80},{1... | collective-permute-start | bytes 393224 | tf_op jit(solution)/shard_map/ppermute | solution.py:43
  42.9 2.1 %collective-permute-start.11 = (bf16[4,128,128]{2,1,0:T(8,128)(2,1)S(1)}, bf16[4,128,128]{2,1,0:T(8,128)(2,1)S(1)}, u32[]{:S(2)}, u32[]{:S(2)}) collective-permute-start(bf16[4,128,128]{2,1,0:T(8,128)(2,1)S(1)} %get-tuple-element.50), channel_id=1, source_target_pairs={{0,64},{16,80},{32,96},{48,112},{64,0},{80,16},{96,32},{112,48},{1... | collective-permute-start | bytes 393224 | tf_op jit(solution)/shard_map/ppermute | solution.py:43
  45.0 3.8 %collective-permute-start.15 = (bf16[16,128,128]{2,1,0:T(8,128)(2,1)S(1)}, bf16[16,128,128]{2,1,0:T(8,128)(2,1)S(1)}, u32[]{:S(2)}, u32[]{:S(2)}) collective-permute-start(bf16[16,128,128]{2,1,0:T(8,128)(2,1)S(1)} %collective-permute-done.8.after.refs_4_), channel_id=1, source_target_pairs={{0,2},{2,4},{4,6},{6,8},{8,10},{10,12},{12,14},{3,1},{5,3},{7,5},{... | collective-permute-start | bytes 1572872 | tf_op jit(solution)/shard_map/ppermute | solution.py:62
  48.8 2.0 %collective-permute-done.12.refs_4_ = bf16[16,128,128]{2,1,0:T(8,128)(2,1)S(1)} collective-permute-done((bf16[16,128,128]{2,1,0:T(8,128)(2,1)S(1)}, bf16[16,128,128]{2,1,0:T(8,128)(2,1)S(1)}, u32[]{:S(2)}, u32[]{:S(2)}) %collective-permute-start.12) | collective-permute-done | bytes 524320 | tf_op jit(solution)/shard_map/ppermute | solution.py:38
  50.8 0.4 turned.4
  51.2 4.4 %collective-permute-start.14 = (bf16[16,128,128]{2,1,0:T(8,128)(2,1)S(1)}, bf16[16,128,128]{2,1,0:T(8,128)(2,1)S(1)}, u32[]{:S(2)}, u32[]{:S(2)}) collective-permute-start(bf16[16,128,128]{2,1,0:T(8,128)(2,1)S(1)} %get-tuple-element.54.after.refs_2_), channel_id=1, source_target_pairs={{48,16},{80,48},{112,80},{0,32},{32,64},{64,96},{49,17},{81,49},{1... | collective-permute-start | bytes 1572872 | tf_op jit(solution)/shard_map/ppermute | solution.py:49
  55.6 0.1 collective-permute-start.13
  55.7 3.5 %others_1.1 = (f32[24,128,128]{2,1,0:T(8,128)S(1)}, bf16[24,128,128]{2,1,0:T(8,128)(2,1)S(1)}) custom-call(s32[40]{0:T(128)S(1)} %get-tuple-element.41.order, s32[12,40]{1,0:T(8,128)S(1)} %get-tuple-element.42.index, bf16[40,1536,128]{2,1,0:T(8,128)(2,1)S(1)} %bitcast.16, f32[40,128,128]{2,1,0:T(8,128)S(1)} %base_1.1.base, ...), custom_call_target="tpu_custom_call" | custom-call | tf_op jit(solution)/shard_map/others_1/pallas_call | solution.py:426
  59.2 4.9 %collective-permute-done.13.refs_9_ = bf16[8,128,128]{2,1,0:T(8,128)(2,1)S(1)} collective-permute-done((bf16[8,128,128]{2,1,0:T(8,128)(2,1)S(1)}, bf16[8,128,128]{2,1,0:T(8,128)(2,1)S(1)}, u32[]{:S(2)}, u32[]{:S(2)}) %collective-permute-start.13) | collective-permute-done | bytes 262176 | tf_op jit(solution)/shard_map/ppermute | solution.py:38
  64.1 1.6 %base_2.1.base = f32[40,128,128]{2,1,0:T(8,128)S(1)} custom-call(s32[2,8]{1,0:T(2,128)S(1)} %get-tuple-element.43.wall_at, s32[40]{0:T(128)S(1)} %get-tuple-element.41.order, f32[40,128,128]{2,1,0:T(8,128)S(1)} %copy-done.1, bf16[4,144,128]{2,1,0:T(8,128)(2,1)S(1)} %get-tuple-element.36.refs_0_, bf16[4,144,128]{2,1,0:T(8,128)(2,1)S(1)} %collective-permute-done.1.refs_1_, ...), custom_call_target="tpu_custom_call" | custom-call | tf_op jit(solution)/shard_map/base_2/pallas_call | solution.py:316
  65.7 0.5 collective-permute-done.14.refs_3_
  66.2 2.8 %exports_2.1 = (f32[16,128,128]{2,1,0:T(8,128)S(1)}, bf16[16,128,128]{2,1,0:T(8,128)(2,1)S(1)}, bf16[104,128,128]{2,1,0:T(8,128)(2,1)S(1)}) custom-call(s32[40]{0:T(128)S(1)} %get-tuple-element.41.order, s32[12,40]{1,0:T(8,128)S(1)} %get-tuple-element.42.index, bf16[40,1536,128]{2,1,0:T(8,128)(2,1)S(1)} %bitcast.17, f32[40,128,128]{2,1,0:T(8,128)S(1)} %base_2.1.base, ...), custom_call_target="tpu_custom_call" | custom-call | flops 3100000000 | tf_op jit(solution)/shard_map/exports_2/pallas_call | solution.py:396
  69.0 0.3 collective-permute-start.20
  69.3 2.2 %collective-permute-start.16 = (bf16[16,128,128]{2,1,0:T(8,128)(2,1)S(1)}, bf16[16,128,128]{2,1,0:T(8,128)(2,1)S(1)}, u32[]{:S(2)}, u32[]{:S(2)}) collective-permute-start(bf16[16,128,128]{2,1,0:T(8,128)(2,1)S(1)} %get-tuple-element.59.after.refs_14_.refs_0_.refs_5_), channel_id=1, source_target_pairs={{0,16},{16,0},{32,48},{48,32},{64,80},{80,64},{96,112},{112,96},{1... | collective-permute-start | bytes 1572872 | tf_op jit(solution)/shard_map/ppermute | solution.py:38
  71.5 1.3 %collective-permute-start.18 = (bf16[6,128,128]{2,1,0:T(8,128)(2,1)S(1)}, bf16[6,128,128]{2,1,0:T(8,128)(2,1)S(1)}, u32[]{:S(2)}, u32[]{:S(2)}) collective-permute-start(bf16[6,128,128]{2,1,0:T(8,128)(2,1)S(1)} %slice.7), channel_id=1, source_target_pairs={{32,0},{64,32},{96,64},{16,48},{48,80},{80,112},{33,1},{65,33},{97... | collective-permute-start | bytes 589832 | tf_op jit(solution)/shard_map/ppermute | solution.py:55
  72.8 3.5 %others_2.1 = (f32[24,128,128]{2,1,0:T(8,128)S(1)}, bf16[24,128,128]{2,1,0:T(8,128)(2,1)S(1)}) custom-call(s32[40]{0:T(128)S(1)} %get-tuple-element.41.order, s32[12,40]{1,0:T(8,128)S(1)} %get-tuple-element.42.index, bf16[40,1536,128]{2,1,0:T(8,128)(2,1)S(1)} %bitcast.18, f32[40,128,128]{2,1,0:T(8,128)S(1)} %base_2.1.base, ...), custom_call_target="tpu_custom_call" | custom-call | tf_op jit(solution)/shard_map/others_2/pallas_call | solution.py:426
  76.2 4.1 %collective-permute-done.18.refs_12_ = bf16[6,128,128]{2,1,0:T(8,128)(2,1)S(1)} collective-permute-done((bf16[6,128,128]{2,1,0:T(8,128)(2,1)S(1)}, bf16[6,128,128]{2,1,0:T(8,128)(2,1)S(1)}, u32[]{:S(2)}, u32[]{:S(2)}) %collective-permute-start.18) | collective-permute-done | bytes 196640 | tf_op jit(solution)/shard_map/ppermute | solution.py:55
  80.3 1.3 %walls.1 = (bf16[4,256,128]{2,1,0:T(8,128)(2,1)S(1)}, bf16[4,256,128]{2,1,0:T(8,128)(2,1)S(1)}, bf16[4,256,128]{2,1,0:T(8,128)(2,1)S(1)}, bf16[4,256,128]{2,1,0:T(8,128)(2,1)S(1)}) custom-call(s32[2,8]{1,0:T(2,128)S(1)} %get-tuple-element.43.wall_at, bf16[4,144,128]{2,1,0:T(8,128)(2,1)S(1)} %get-tuple-element.36.refs_0_, ...), custom_call_target="tpu_custom_call" | custom-call | tf_op jit(solution)/shard_map/walls/pallas_call | solution.py:353
  81.7 1.6 %collective-permute-start.22 = (bf16[4,256,128]{2,1,0:T(8,128)(2,1)S(1)}, bf16[4,256,128]{2,1,0:T(8,128)(2,1)S(1)}, u32[]{:S(2)}, u32[]{:S(2)}) collective-permute-start(bf16[4,256,128]{2,1,0:T(8,128)(2,1)S(1)} %get-tuple-element.64), channel_id=1, source_target_pairs={{0,32},{16,48},{32,64},{48,80},{64,96},{80,112},{96,0},{112,16},{1... | collective-permute-start | bytes 786440 | tf_op jit(solution)/shard_map/ppermute | solution.py:43
  83.3 1.7 %collective-permute-start.23 = (bf16[4,256,128]{2,1,0:T(8,128)(2,1)S(1)}, bf16[4,256,128]{2,1,0:T(8,128)(2,1)S(1)}, u32[]{:S(2)}, u32[]{:S(2)}) collective-permute-start(bf16[4,256,128]{2,1,0:T(8,128)(2,1)S(1)} %get-tuple-element.65), channel_id=1, source_target_pairs={{0,96},{16,112},{32,0},{48,16},{64,32},{80,48},{96,64},{112,80},{1... | collective-permute-start | bytes 786440 | tf_op jit(solution)/shard_map/ppermute | solution.py:43
  85.0 2.0 %collective-permute-start.24 = (bf16[4,256,128]{2,1,0:T(8,128)(2,1)S(1)}, bf16[4,256,128]{2,1,0:T(8,128)(2,1)S(1)}, u32[]{:S(2)}, u32[]{:S(2)}) collective-permute-start(bf16[4,256,128]{2,1,0:T(8,128)(2,1)S(1)} %get-tuple-element.66), channel_id=1, source_target_pairs={{0,64},{16,80},{32,96},{48,112},{64,0},{80,16},{96,32},{112,48},{1... | collective-permute-start | bytes 786440 | tf_op jit(solution)/shard_map/ppermute | solution.py:43
  87.0 0.8 collective-permute-start.19
  87.8 4.8 %collective-permute-done.19.refs_4_.refs_5_ = bf16[6,128,128]{2,1,0:T(8,128)(2,1)S(1)} collective-permute-done((bf16[6,128,128]{2,1,0:T(8,128)(2,1)S(1)}, bf16[6,128,128]{2,1,0:T(8,128)(2,1)S(1)}, u32[]{:S(2)}, u32[]{:S(2)}) %collective-permute-start.19) | collective-permute-done | bytes 196640 | tf_op jit(solution)/shard_map/ppermute | solution.py:38
  92.7 3.8 %collective-permute-start.21 = (bf16[16,128,128]{2,1,0:T(8,128)(2,1)S(1)}, bf16[16,128,128]{2,1,0:T(8,128)(2,1)S(1)}, u32[]{:S(2)}, u32[]{:S(2)}) collective-permute-start(bf16[16,128,128]{2,1,0:T(8,128)(2,1)S(1)} %collective-permute-done.20.refs_5_.refs_11_), channel_id=1, source_target_pairs={{0,2},{2,4},{4,6},{6,8},{8,10},{10,12},{12,14},{3,1},{5,3},{7,5},{... | collective-permute-start | bytes 1572872 | tf_op jit(solution)/shard_map/ppermute | solution.py:62
  96.5 0.7 turned.5
  97.2 1.5 %collective-permute-start.25 = (bf16[8,256,128]{2,1,0:T(8,128)(2,1)S(1)}, bf16[8,256,128]{2,1,0:T(8,128)(2,1)S(1)}, u32[]{:S(2)}, u32[]{:S(2)}) collective-permute-start(bf16[8,256,128]{2,1,0:T(8,128)(2,1)S(1)} %turned.5), channel_id=1, source_target_pairs={{0,16},{16,0},{32,48},{48,32},{64,80},{80,64},{96,112},{112,96},{1... | collective-permute-start | bytes 1572872 | tf_op jit(solution)/shard_map/ppermute | solution.py:38
  98.7 3.1 %collective-permute-start.17 = (bf16[10,128,128]{2,1,0:T(8,128)(2,1)S(1)}, bf16[10,128,128]{2,1,0:T(8,128)(2,1)S(1)}, u32[]{:S(2)}, u32[]{:S(2)}) collective-permute-start(bf16[10,128,128]{2,1,0:T(8,128)(2,1)S(1)} %slice.8), channel_id=1, source_target_pairs={{48,16},{80,48},{112,80},{0,32},{32,64},{64,96},{49,17},{81,49},{1... | collective-permute-start | bytes 983048 | tf_op jit(solution)/shard_map/ppermute | solution.py:49
  101.8 1.8 %base_3.1.base = f32[40,128,128]{2,1,0:T(8,128)S(1)} custom-call(s32[2,8]{1,0:T(2,128)S(1)} %get-tuple-element.43.wall_at, s32[40]{0:T(128)S(1)} %get-tuple-element.41.order, f32[40,128,128]{2,1,0:T(8,128)S(1)} %copy-done.1, bf16[4,144,128]{2,1,0:T(8,128)(2,1)S(1)} %get-tuple-element.36.refs_0_, bf16[4,144,128]{2,1,0:T(8,128)(2,1)S(1)} %collective-permute-done.1.refs_1_, ...), custom_call_target="tpu_custom_call" | custom-call | tf_op jit(solution)/shard_map/base_3/pallas_call | solution.py:316
  103.7 3.6 %collective-permute-done.17.refs_3_ = bf16[10,128,128]{2,1,0:T(8,128)(2,1)S(1)} collective-permute-done((bf16[10,128,128]{2,1,0:T(8,128)(2,1)S(1)}, bf16[10,128,128]{2,1,0:T(8,128)(2,1)S(1)}, u32[]{:S(2)}, u32[]{:S(2)}) %collective-permute-start.17) | collective-permute-done | bytes 327712 | tf_op jit(solution)/shard_map/ppermute | solution.py:49
  107.3 5.5 %collective-permute-done.21.refs_6_ = bf16[16,128,128]{2,1,0:T(8,128)(2,1)S(1)} collective-permute-done((bf16[16,128,128]{2,1,0:T(8,128)(2,1)S(1)}, bf16[16,128,128]{2,1,0:T(8,128)(2,1)S(1)}, u32[]{:S(2)}, u32[]{:S(2)}) %collective-permute-start.21) | collective-permute-done | bytes 524320 | tf_op jit(solution)/shard_map/ppermute | solution.py:62
  112.8 5.1 %last.1 = (f32[40,128,128]{2,1,0:T(8,128)}, bf16[104,128,128]{2,1,0:T(8,128)(2,1)S(1)}) custom-call(s32[40]{0:T(128)S(1)} %get-tuple-element.41.order, s32[12,40]{1,0:T(8,128)S(1)} %get-tuple-element.42.index, bf16[40,1536,128]{2,1,0:T(8,128)(2,1)S(1)} %bitcast.19, f32[40,128,128]{2,1,0:T(8,128)S(1)} %base_3.1.base, ...), custom_call_target="tpu_custom_call" | custom-call | tf_op jit(solution)/shard_map/last/pallas_call | solution.py:459
  117.9 4.4 %end.1 = (f32[40,128,128]{2,1,0:T(8,128)}, f32[16,2,128,128]{3,2,1,0:T(8,128)}) custom-call(s32[40]{0:T(128)S(1)} %get-tuple-element.41.order, s32[12,40]{1,0:T(8,128)S(1)} %get-tuple-element.42.index, s32[2,8]{1,0:T(2,128)S(1)} %bitcast.24, f32[2,16]{1,0:T(2,128)S(1)} %bitcast.28, f32[2,16]{1,0:T(2,128)S(1)} %bitcast.26, ...), custom_call_target="tpu_custom_call", output_to_operand_aliasing={{0}: (14, {})} | custom-call | tf_op jit(solution)/shard_map/end/pallas_call | solution.py:508
  (39 shorter events, 0.2 us)
Async XLA Ops:
  0.6 4.4 %copy-start.4 = (s32[1,1,8,2]{2,3,1,0:T(2,128)S(1)}, s32[1,1,8,2]{2,3,1,0:T(2,128)}, u32[]{:S(2)}) copy-start(s32[1,1,8,2]{2,3,1,0:T(2,128)} %param.19) | copy-start | bytes 196
  0.6 4.5 %copy-start.5 = (f32[16,2]{0,1:T(2,128)S(1)}, f32[16,2]{0,1:T(2,128)}, u32[]{:S(2)}) copy-start(f32[16,2]{0,1:T(2,128)} %param.22) | copy-start | bytes 388
  0.7 4.6 %copy-start.6 = (f32[16,2]{0,1:T(2,128)S(1)}, f32[16,2]{0,1:T(2,128)}, u32[]{:S(2)}) copy-start(f32[16,2]{0,1:T(2,128)} %param.21) | copy-start | bytes 388
  0.7 4.6 %copy-start.12 = (f32[16]{0:T(128)S(1)}, f32[16]{0:T(128)}, u32[]{:S(2)}) copy-start(f32[16]{0:T(128)} %param.23) | copy-start | bytes 196
  0.7 5.2 %copy-start.3 = (f32[1,1,8,2,2,128,128]{6,5,4,3,2,1,0:T(8,128)S(1)}, f32[1,1,8,2,2,128,128]{6,5,4,3,2,1,0:T(8,128)}, u32[]{:S(2)}) copy-start(f32[1,1,8,2,2,128,128]{6,5,4,3,2,1,0:T(8,128)} %param.20) | copy-start | bytes 6291460
  0.7 5.2 %copy-start.9 = (f32[1,1,8,2,128]{4,3,2,1,0:T(2,128)S(1)}, f32[1,1,8,2,128]{4,3,2,1,0:T(2,128)}, u32[]{:S(2)}) copy-start(f32[1,1,8,2,128]{4,3,2,1,0:T(2,128)} %param.18) | copy-start | bytes 24580
  3.7 2.2 %collective-permute-start = (bf16[16,128,128]{2,1,0:T(8,128)(2,1)}, bf16[16,128,128]{2,1,0:T(8,128)(2,1)S(1)}, u32[]{:S(2)}, u32[]{:S(2)}) collective-permute-start(bf16[16,128,128]{2,1,0:T(8,128)(2,1)} %exports.1.refs_5_.refs_0_.refs_14_.refs_18_.refs_9_), channel_id=1, source_target_pairs={{0,1},{1,0},{2,3},{3,2},{4,5},{5,4},{6,7},{7,6},{8,9},{9,8},{10,11... | collective-permute-start | bytes 1572872 | tf_op jit(solution)/shard_map/ppermute | solution.py:60
  3.8 14.6 %collective-permute-start.4 = (bf16[16,128,128]{2,1,0:T(8,128)(2,1)}, bf16[16,128,128]{2,1,0:T(8,128)(2,1)S(1)}, u32[]{:S(2)}, u32[]{:S(2)}) collective-permute-start(bf16[16,128,128]{2,1,0:T(8,128)(2,1)} %exports.1.refs_5_.refs_0_.refs_14_.refs_18_.refs_9_), channel_id=1, source_target_pairs={{0,16},{16,0},{32,48},{48,32},{64,80},{80,64},{96,112},{112,96},{1... | collective-permute-start | bytes 1572872 | tf_op jit(solution)/shard_map/ppermute | solution.py:38
  6.7 15.8 %copy-start.1 = (f32[40,128,128]{2,1,0:T(8,128)S(1)}, f32[40,128,128]{2,1,0:T(8,128)}, u32[]{:S(2)}) copy-start(f32[40,128,128]{2,1,0:T(8,128)} %pressure.9) | copy-start | bytes 7864324
  6.7 15.7 %copy-start.7 = (s32[40,12]{0,1:T(8,128)S(1)}, s32[40,12]{0,1:T(8,128)}, u32[]{:S(2)}) copy-start(s32[40,12]{0,1:T(8,128)} %param.14) | copy-start | bytes 5764
  6.7 15.7 %copy-start.8 = (s32[40,12]{0,1:T(8,128)S(1)}, s32[40,12]{0,1:T(8,128)}, u32[]{:S(2)}) copy-start(s32[40,12]{0,1:T(8,128)} %param.15) | copy-start | bytes 5764
  6.7 15.7 %copy-start.10 = (s32[1,1,8,2]{2,3,1,0:T(2,128)S(1)}, s32[1,1,8,2]{2,3,1,0:T(2,128)}, u32[]{:S(2)}) copy-start(s32[1,1,8,2]{2,3,1,0:T(2,128)} %param.17) | copy-start | bytes 196
  6.8 15.7 %copy-start.11 = (s32[16]{0:T(128)S(1)}, s32[16]{0:T(128)}, u32[]{:S(2)}) copy-start(s32[16]{0:T(128)} %ids.3) | copy-start | bytes 196
  6.8 11.6 %collective-permute-start.1 = (bf16[4,144,128]{2,1,0:T(8,128)(2,1)S(1)}, bf16[4,144,128]{2,1,0:T(8,128)(2,1)S(1)}, u32[]{:S(2)}, u32[]{:S(2)}) collective-permute-start(bf16[4,144,128]{2,1,0:T(8,128)(2,1)S(1)} %get-tuple-element.37), channel_id=1, source_target_pairs={{0,32},{16,48},{32,64},{48,80},{64,96},{80,112},{96,0},{112,16},{1... | collective-permute-start | bytes 442376 | tf_op jit(solution)/shard_map/ppermute | solution.py:43
  8.4 9.9 %collective-permute-start.2 = (bf16[4,144,128]{2,1,0:T(8,128)(2,1)S(1)}, bf16[4,144,128]{2,1,0:T(8,128)(2,1)S(1)}, u32[]{:S(2)}, u32[]{:S(2)}) collective-permute-start(bf16[4,144,128]{2,1,0:T(8,128)(2,1)S(1)} %get-tuple-element.38), channel_id=1, source_target_pairs={{0,96},{16,112},{32,0},{48,16},{64,32},{80,48},{96,64},{112,80},{1... | collective-permute-start | bytes 442376 | tf_op jit(solution)/shard_map/ppermute | solution.py:43
  10.1 8.3 %collective-permute-start.3 = (bf16[4,144,128]{2,1,0:T(8,128)(2,1)S(1)}, bf16[4,144,128]{2,1,0:T(8,128)(2,1)S(1)}, u32[]{:S(2)}, u32[]{:S(2)}) collective-permute-start(bf16[4,144,128]{2,1,0:T(8,128)(2,1)S(1)} %get-tuple-element.39), channel_id=1, source_target_pairs={{0,64},{16,80},{32,96},{48,112},{64,0},{80,16},{96,32},{112,48},{1... | collective-permute-start | bytes 442376 | tf_op jit(solution)/shard_map/ppermute | solution.py:43
  12.1 21.2 %collective-permute-start.7 = (bf16[16,128,128]{2,1,0:T(8,128)(2,1)S(1)}, bf16[16,128,128]{2,1,0:T(8,128)(2,1)S(1)}, u32[]{:S(2)}, u32[]{:S(2)}) collective-permute-start(bf16[16,128,128]{2,1,0:T(8,128)(2,1)S(1)} %collective-permute-done.after.value), channel_id=1, source_target_pairs={{0,2},{2,4},{4,6},{6,8},{8,10},{10,12},{12,14},{3,1},{5,3},{7,5},{... | collective-permute-start | bytes 1572872 | tf_op jit(solution)/shard_map/ppermute | solution.py:62
  18.3 13.5 %copy-start.2 = (bf16[16,128,128]{2,1,0:T(8,128)(2,1)S(1)}, bf16[16,128,128]{2,1,0:T(8,128)(2,1)}, u32[]{:S(2)}) copy-start(bf16[16,128,128]{2,1,0:T(8,128)(2,1)} %exports.1.refs_5_.refs_0_.refs_14_.refs_18_.refs_9_) | copy-start | bytes 1572868
  18.8 14.5 %collective-permute-start.6 = (bf16[16,128,128]{2,1,0:T(8,128)(2,1)S(1)}, bf16[16,128,128]{2,1,0:T(8,128)(2,1)S(1)}, u32[]{:S(2)}, u32[]{:S(2)}) collective-permute-start(bf16[16,128,128]{2,1,0:T(8,128)(2,1)S(1)} %get-tuple-element.40.after.refs_2_), channel_id=1, source_target_pairs={{48,16},{80,48},{112,80},{0,32},{32,64},{64,96},{49,17},{81,49},{1... | collective-permute-start | bytes 1572872 | tf_op jit(solution)/shard_map/ppermute | solution.py:49
  22.3 9.5 %collective-permute-start.5 = (bf16[8,144,128]{2,1,0:T(8,128)(2,1)S(1)}, bf16[8,144,128]{2,1,0:T(8,128)(2,1)S(1)}, u32[]{:S(2)}, u32[]{:S(2)}) collective-permute-start(bf16[8,144,128]{2,1,0:T(8,128)(2,1)S(1)} %get-tuple-element.44), channel_id=1, source_target_pairs={{0,16},{16,0},{32,48},{48,32},{64,80},{80,64},{96,112},{112,96},{1... | collective-permute-start | bytes 884744 | tf_op jit(solution)/shard_map/ppermute | solution.py:38
  22.4 10.9 %copy-start = (bf16[40,12,128,128]{3,2,1,0:T(8,128)(2,1)S(1)}, bf16[40,12,128,128]{3,2,1,0:T(8,128)(2,1)}, u32[]{:S(2)}) copy-start(bf16[40,12,128,128]{3,2,1,0:T(8,128)(2,1)} %param.13) | copy-start | bytes 47185924
  36.1 2.2 %collective-permute-start.8 = (bf16[16,128,128]{2,1,0:T(8,128)(2,1)S(1)}, bf16[16,128,128]{2,1,0:T(8,128)(2,1)S(1)}, u32[]{:S(2)}, u32[]{:S(2)}) collective-permute-start(bf16[16,128,128]{2,1,0:T(8,128)(2,1)S(1)} %get-tuple-element.46.refs_12_.refs_0_.refs_16_.refs_7_), channel_id=1, source_target_pairs={{0,1},{1,0},{2,3},{3,2},{4,5},{5,4},{6,7},{7,6},{8,9},{9,8},{10,11... | collective-permute-start | bytes 1572872 | tf_op jit(solution)/shard_map/ppermute | solution.py:60
  36.2 14.7 %collective-permute-start.12 = (bf16[16,128,128]{2,1,0:T(8,128)(2,1)S(1)}, bf16[16,128,128]{2,1,0:T(8,128)(2,1)S(1)}, u32[]{:S(2)}, u32[]{:S(2)}) collective-permute-start(bf16[16,128,128]{2,1,0:T(8,128)(2,1)S(1)} %get-tuple-element.46.refs_12_.refs_0_.refs_16_.refs_7_), channel_id=1, source_target_pairs={{0,16},{16,0},{32,48},{48,32},{64,80},{80,64},{96,112},{112,96},{1... | collective-permute-start | bytes 1572872 | tf_op jit(solution)/shard_map/ppermute | solution.py:38
  39.1 11.7 %collective-permute-start.9 = (bf16[4,128,128]{2,1,0:T(8,128)(2,1)S(1)}, bf16[4,128,128]{2,1,0:T(8,128)(2,1)S(1)}, u32[]{:S(2)}, u32[]{:S(2)}) collective-permute-start(bf16[4,128,128]{2,1,0:T(8,128)(2,1)S(1)} %get-tuple-element.48), channel_id=1, source_target_pairs={{0,32},{16,48},{32,64},{48,80},{64,96},{80,112},{96,0},{112,16},{1... | collective-permute-start | bytes 393224 | tf_op jit(solution)/shard_map/ppermute | solution.py:43
  41.4 9.4 %collective-permute-start.10 = (bf16[4,128,128]{2,1,0:T(8,128)(2,1)S(1)}, bf16[4,128,128]{2,1,0:T(8,128)(2,1)S(1)}, u32[]{:S(2)}, u32[]{:S(2)}) collective-permute-start(bf16[4,128,128]{2,1,0:T(8,128)(2,1)S(1)} %get-tuple-element.49), channel_id=1, source_target_pairs={{0,96},{16,112},{32,0},{48,16},{64,32},{80,48},{96,64},{112,80},{1... | collective-permute-start | bytes 393224 | tf_op jit(solution)/shard_map/ppermute | solution.py:43
  42.9 7.9 %collective-permute-start.11 = (bf16[4,128,128]{2,1,0:T(8,128)(2,1)S(1)}, bf16[4,128,128]{2,1,0:T(8,128)(2,1)S(1)}, u32[]{:S(2)}, u32[]{:S(2)}) collective-permute-start(bf16[4,128,128]{2,1,0:T(8,128)(2,1)S(1)} %get-tuple-element.50), channel_id=1, source_target_pairs={{0,64},{16,80},{32,96},{48,112},{64,0},{80,16},{96,32},{112,48},{1... | collective-permute-start | bytes 393224 | tf_op jit(solution)/shard_map/ppermute | solution.py:43
  45.0 20.7 %collective-permute-start.15 = (bf16[16,128,128]{2,1,0:T(8,128)(2,1)S(1)}, bf16[16,128,128]{2,1,0:T(8,128)(2,1)S(1)}, u32[]{:S(2)}, u32[]{:S(2)}) collective-permute-start(bf16[16,128,128]{2,1,0:T(8,128)(2,1)S(1)} %collective-permute-done.8.after.refs_4_), channel_id=1, source_target_pairs={{0,2},{2,4},{4,6},{6,8},{8,10},{10,12},{12,14},{3,1},{5,3},{7,5},{... | collective-permute-start | bytes 1572872 | tf_op jit(solution)/shard_map/ppermute | solution.py:62
  51.2 15.0 %collective-permute-start.14 = (bf16[16,128,128]{2,1,0:T(8,128)(2,1)S(1)}, bf16[16,128,128]{2,1,0:T(8,128)(2,1)S(1)}, u32[]{:S(2)}, u32[]{:S(2)}) collective-permute-start(bf16[16,128,128]{2,1,0:T(8,128)(2,1)S(1)} %get-tuple-element.54.after.refs_2_), channel_id=1, source_target_pairs={{48,16},{80,48},{112,80},{0,32},{32,64},{64,96},{49,17},{81,49},{1... | collective-permute-start | bytes 1572872 | tf_op jit(solution)/shard_map/ppermute | solution.py:49
  55.6 8.5 %collective-permute-start.13 = (bf16[8,128,128]{2,1,0:T(8,128)(2,1)S(1)}, bf16[8,128,128]{2,1,0:T(8,128)(2,1)S(1)}, u32[]{:S(2)}, u32[]{:S(2)}) collective-permute-start(bf16[8,128,128]{2,1,0:T(8,128)(2,1)S(1)} %get-tuple-element.51), channel_id=1, source_target_pairs={{0,16},{16,0},{32,48},{48,32},{64,80},{80,64},{96,112},{112,96},{1... | collective-permute-start | bytes 786440 | tf_op jit(solution)/shard_map/ppermute | solution.py:38
  69.0 11.3 %collective-permute-start.20 = (bf16[16,128,128]{2,1,0:T(8,128)(2,1)S(1)}, bf16[16,128,128]{2,1,0:T(8,128)(2,1)S(1)}, u32[]{:S(2)}, u32[]{:S(2)}) collective-permute-start(bf16[16,128,128]{2,1,0:T(8,128)(2,1)S(1)} %get-tuple-element.59.after.refs_14_.refs_0_.refs_5_), channel_id=1, source_target_pairs={{0,1},{1,0},{2,3},{3,2},{4,5},{5,4},{6,7},{7,6},{8,9},{9,8},{10,11... | collective-permute-start | bytes 1572872 | tf_op jit(solution)/shard_map/ppermute | solution.py:60
  69.3 27.2 %collective-permute-start.16 = (bf16[16,128,128]{2,1,0:T(8,128)(2,1)S(1)}, bf16[16,128,128]{2,1,0:T(8,128)(2,1)S(1)}, u32[]{:S(2)}, u32[]{:S(2)}) collective-permute-start(bf16[16,128,128]{2,1,0:T(8,128)(2,1)S(1)} %get-tuple-element.59.after.refs_14_.refs_0_.refs_5_), channel_id=1, source_target_pairs={{0,16},{16,0},{32,48},{48,32},{64,80},{80,64},{96,112},{112,96},{1... | collective-permute-start | bytes 1572872 | tf_op jit(solution)/shard_map/ppermute | solution.py:38
  71.5 8.9 %collective-permute-start.18 = (bf16[6,128,128]{2,1,0:T(8,128)(2,1)S(1)}, bf16[6,128,128]{2,1,0:T(8,128)(2,1)S(1)}, u32[]{:S(2)}, u32[]{:S(2)}) collective-permute-start(bf16[6,128,128]{2,1,0:T(8,128)(2,1)S(1)} %slice.7), channel_id=1, source_target_pairs={{32,0},{64,32},{96,64},{16,48},{48,80},{80,112},{33,1},{65,33},{97... | collective-permute-start | bytes 589832 | tf_op jit(solution)/shard_map/ppermute | solution.py:55
  81.7 14.8 %collective-permute-start.22 = (bf16[4,256,128]{2,1,0:T(8,128)(2,1)S(1)}, bf16[4,256,128]{2,1,0:T(8,128)(2,1)S(1)}, u32[]{:S(2)}, u32[]{:S(2)}) collective-permute-start(bf16[4,256,128]{2,1,0:T(8,128)(2,1)S(1)} %get-tuple-element.64), channel_id=1, source_target_pairs={{0,32},{16,48},{32,64},{48,80},{64,96},{80,112},{96,0},{112,16},{1... | collective-permute-start | bytes 786440 | tf_op jit(solution)/shard_map/ppermute | solution.py:43
  83.3 13.2 %collective-permute-start.23 = (bf16[4,256,128]{2,1,0:T(8,128)(2,1)S(1)}, bf16[4,256,128]{2,1,0:T(8,128)(2,1)S(1)}, u32[]{:S(2)}, u32[]{:S(2)}) collective-permute-start(bf16[4,256,128]{2,1,0:T(8,128)(2,1)S(1)} %get-tuple-element.65), channel_id=1, source_target_pairs={{0,96},{16,112},{32,0},{48,16},{64,32},{80,48},{96,64},{112,80},{1... | collective-permute-start | bytes 786440 | tf_op jit(solution)/shard_map/ppermute | solution.py:43
  85.0 11.5 %collective-permute-start.24 = (bf16[4,256,128]{2,1,0:T(8,128)(2,1)S(1)}, bf16[4,256,128]{2,1,0:T(8,128)(2,1)S(1)}, u32[]{:S(2)}, u32[]{:S(2)}) collective-permute-start(bf16[4,256,128]{2,1,0:T(8,128)(2,1)S(1)} %get-tuple-element.66), channel_id=1, source_target_pairs={{0,64},{16,80},{32,96},{48,112},{64,0},{80,16},{96,32},{112,48},{1... | collective-permute-start | bytes 786440 | tf_op jit(solution)/shard_map/ppermute | solution.py:43
  87.0 5.7 %collective-permute-start.19 = (bf16[6,128,128]{2,1,0:T(8,128)(2,1)S(1)}, bf16[6,128,128]{2,1,0:T(8,128)(2,1)S(1)}, u32[]{:S(2)}, u32[]{:S(2)}) collective-permute-start(bf16[6,128,128]{2,1,0:T(8,128)(2,1)S(1)} %collective-permute-done.18.refs_12_), channel_id=1, source_target_pairs={{0,16},{16,0},{32,48},{48,32},{64,80},{80,64},{96,112},{112,96},{1... | collective-permute-start | bytes 589832 | tf_op jit(solution)/shard_map/ppermute | solution.py:38
  92.7 20.2 %collective-permute-start.21 = (bf16[16,128,128]{2,1,0:T(8,128)(2,1)S(1)}, bf16[16,128,128]{2,1,0:T(8,128)(2,1)S(1)}, u32[]{:S(2)}, u32[]{:S(2)}) collective-permute-start(bf16[16,128,128]{2,1,0:T(8,128)(2,1)S(1)} %collective-permute-done.20.refs_5_.refs_11_), channel_id=1, source_target_pairs={{0,2},{2,4},{4,6},{6,8},{8,10},{10,12},{12,14},{3,1},{5,3},{7,5},{... | collective-permute-start | bytes 1572872 | tf_op jit(solution)/shard_map/ppermute | solution.py:62
  97.2 20.7 %collective-permute-start.25 = (bf16[8,256,128]{2,1,0:T(8,128)(2,1)S(1)}, bf16[8,256,128]{2,1,0:T(8,128)(2,1)S(1)}, u32[]{:S(2)}, u32[]{:S(2)}) collective-permute-start(bf16[8,256,128]{2,1,0:T(8,128)(2,1)S(1)} %turned.5), channel_id=1, source_target_pairs={{0,16},{16,0},{32,48},{48,32},{64,80},{80,64},{96,112},{112,96},{1... | collective-permute-start | bytes 1572872 | tf_op jit(solution)/shard_map/ppermute | solution.py:38
  98.7 8.6 %collective-permute-start.17 = (bf16[10,128,128]{2,1,0:T(8,128)(2,1)S(1)}, bf16[10,128,128]{2,1,0:T(8,128)(2,1)S(1)}, u32[]{:S(2)}, u32[]{:S(2)}) collective-permute-start(bf16[10,128,128]{2,1,0:T(8,128)(2,1)S(1)} %slice.8), channel_id=1, source_target_pairs={{48,16},{80,48},{112,80},{0,32},{32,64},{64,96},{49,17},{81,49},{1... | collective-permute-start | bytes 983048 | tf_op jit(solution)/shard_map/ppermute | solution.py:49
